TPU v7x, 256 devices: a whole 4x4x8 slice. The times are simulated.
256 devices in a mesh: band: 16 (over x_hi, y, core), dom: 16 (over z, x_lo).
Axes of the slice: x: 4 (x_hi: 2, x_lo: 2; x = x_hi * 2 + x_lo), y: 4, z: 8, core: 2. Of those that a mesh axis runs over, the one named last changes fastest.
Arguments:
- orbitals: float32 [128, 64, 32, 128], P('band', 'dom'), may hold values from -6 to 6
- owner_order: int32 [32], replicated, may hold values from 0 to 31, each once
Outputs:
- exchange_applied: float32 [128, 64, 32, 128], P('band', 'dom')
Inputs may be any that keep to these rules, and one draw needn't show every extreme that they name: `owner_order`: a permutation of the block numbers; a block number k names orbitals of the group of index k // 2.
All inputs are finite; a program needn't handle non-finite values.
Results may differ from a plain program's by a relative error of at most 0.0003.
Values sent between devices are 32-bit elements; how exact they have to be, the bound alone decides.
No kernel may reach another device: no remote copies, remote signals or barrier semaphores. Data moves between devices by JAX's collectives and lax.ppermute only.
A program may use at most 192 MiB of HBM per device.

v0:
```python
import jax
import jax.numpy as jnp
from jax import lax
from jax.sharding import PartitionSpec as P

LOCAL = 8
BLOCK = 4
STEPS = 2
SWEEPS = 3


screen = 0.5
exchange_scale = 0.25


def spread(block, axis, holder):
    block = jnp.where(lax.axis_index(axis) == holder, block, jnp.zeros_like(block))
    return lax.psum(block, axis)


def extended_2(cells, sides, width):
    for axis, dim in sides:
        count = lax.axis_size(axis)
        head = lax.slice_in_dim(cells, 0, width, axis=dim)
        tail = lax.slice_in_dim(cells, cells.shape[dim] - width, cells.shape[dim], axis=dim)
        cells = jnp.concatenate(
            [
                lax.ppermute(tail, axis, [(i, (i + 1) % count) for i in range(count)]),
                cells,
                lax.ppermute(head, axis, [((i + 1) % count, i) for i in range(count)]),
            ],
            axis=dim,
        )
    return cells


def neighbour_sum(x_plus, x_minus, potential):
    neighbours = x_plus + x_minus
    neighbours = neighbours + jnp.roll(potential, -1, 3) + jnp.roll(potential, 1, 3)
    neighbours = neighbours + jnp.roll(potential, -1, 4) + jnp.roll(potential, 1, 4)
    return neighbours


def local(orbitals, owner_order):
    halves = LOCAL // BLOCK
    applied = jnp.zeros_like(orbitals)
    for step_index in range(STEPS):
        block_id = owner_order[step_index]
        owner_index = block_id // halves
        half_index = block_id % halves * BLOCK
        own_block = lax.dynamic_slice_in_dim(orbitals, half_index, BLOCK, 0)
        block = spread(own_block, "band", owner_index)
        density = block[:, None] * orbitals[None]
        potential = density / screen
        for sweep_index in range(SWEEPS):
            padded = extended_2(potential, (("dom", 2),), 1)
            neighbours = neighbour_sum(padded[:, :, 2:], padded[:, :, :-2], potential)
            potential = (neighbours + density) / (6.0 + screen)
        applied = applied + jnp.sum(potential * block[:, None], axis=0)
    return -exchange_scale * applied


def solution(mesh):
    in_specs = (P("band", "dom", None, None), P())
    out_specs = P("band", "dom", None, None)
    return jax.shard_map(local, mesh=mesh, in_specs=in_specs, out_specs=out_specs, check_vma=False)
```

profile of v0, /device:TPU:1, one launch (start us, length us, event | category | flops | bytes accessed | tf_op | source)
XLA Modules:
  0.0 351.7 jit_solution(16343014644058733463)
XLA Ops:
  6.5 1.3 fusion.68
  13.0 1.9 dynamic-slice_select_fusion
  14.9 147.8 %all-reduce.3.cloned.1.call-done = (f32[4,4,32,128]{3,2,1,0:T(8,128)}, f32[4,4,32,128]{3,2,1,0:T(8,128)}) async-done(((f32[4,4,32,128]{3,2,1,0:T(8,128)}, f32[4,4,32,128]{3,2,1,0:T(8,128)}), (f32[4,4,32,128]{3,2,1,0:T(8,128)}, f32[4,4,32,128]{3,2,1,0:T(8,128)})) %all-reduce.3.cloned.1.call-update) | async-done | bytes 524304 | tf_op jit(solution)/shard_map/psum | solution.py:18
  162.7 1.4 multiply_multiply_fusion
  164.1 0.8 fusion.48
  164.9 0.7 fusion.49
  165.8 0.7 copy-done.2
  166.6 3.1 collective-permute-start.6
  169.8 0.5 fusion.51
  170.3 20.3 %collective-permute-done.6 = f32[4,8,1,32,128]{4,3,2,1,0:T(8,128)S(1)} collective-permute-done((f32[4,8,1,32,128]{4,3,2,1,0:T(8,128)S(1)}, f32[4,8,1,32,128]{4,3,2,1,0:T(8,128)S(1)}, u32[]{:S(2)}, u32[]{:S(2)}) %collective-permute-start.6) | collective-permute-done | bytes 524320 | tf_op jit(solution)/shard_map/ppermute | solution.py:30
  190.6 0.1 collective-permute-done.7
  190.8 2.4 fusion.4
  193.2 0.7 fusion.43
  193.9 0.7 fusion.44
  194.7 4.3 %collective-permute-start.8 = (f32[4,8,1,32,128]{4,3,2,1,0:T(8,128)S(1)}, f32[4,8,1,32,128]{4,3,2,1,0:T(8,128)S(1)}, u32[]{:S(2)}, u32[]{:S(2)}) collective-permute-start(f32[4,8,1,32,128]{4,3,2,1,0:T(8,128)S(1)} %get-tuple-element.25), channel_id=1, source_target_pairs={{1,0},{2,1},{3,2},{4,3},{5,4},{6,5},{7,6},{8,7},{9,8},{10,9},{11,1... | collective-permute-start | bytes 1572872 | tf_op jit(solution)/shard_map/ppermute | solution.py:30
  199.1 0.5 fusion.46
  199.7 19.8 %collective-permute-done.8 = f32[4,8,1,32,128]{4,3,2,1,0:T(8,128)S(1)} collective-permute-done((f32[4,8,1,32,128]{4,3,2,1,0:T(8,128)S(1)}, f32[4,8,1,32,128]{4,3,2,1,0:T(8,128)S(1)}, u32[]{:S(2)}, u32[]{:S(2)}) %collective-permute-start.8) | collective-permute-done | bytes 524320 | tf_op jit(solution)/shard_map/ppermute | solution.py:30
  219.4 1.3 collective-permute-done.9
  220.8 2.5 fusion.5
  223.3 0.8 fusion.39
  224.1 0.8 fusion.41
  225.0 4.6 %collective-permute-start.10 = (f32[4,8,1,32,128]{4,3,2,1,0:T(8,128)S(1)}, f32[4,8,1,32,128]{4,3,2,1,0:T(8,128)S(1)}, u32[]{:S(2)}, u32[]{:S(2)}) collective-permute-start(f32[4,8,1,32,128]{4,3,2,1,0:T(8,128)S(1)} %get-tuple-element.15), channel_id=1, source_target_pairs={{1,0},{2,1},{3,2},{4,3},{5,4},{6,5},{7,6},{8,7},{9,8},{10,9},{11,1... | collective-permute-start | bytes 1572872 | tf_op jit(solution)/shard_map/ppermute | solution.py:30
  229.7 0.8 fusion.38
  230.5 20.1 %collective-permute-done.10 = f32[4,8,1,32,128]{4,3,2,1,0:T(8,128)S(1)} collective-permute-done((f32[4,8,1,32,128]{4,3,2,1,0:T(8,128)S(1)}, f32[4,8,1,32,128]{4,3,2,1,0:T(8,128)S(1)}, u32[]{:S(2)}, u32[]{:S(2)}) %collective-permute-start.10) | collective-permute-done | bytes 524320 | tf_op jit(solution)/shard_map/ppermute | solution.py:30
  250.6 0.7 collective-permute-done.11
  251.2 2.7 fusion.7
  254.0 0.8 fusion.63
  254.8 0.8 fusion.64
  255.7 3.9 %collective-permute-start = (f32[4,8,1,32,128]{4,3,2,1,0:T(8,128)S(1)}, f32[4,8,1,32,128]{4,3,2,1,0:T(8,128)S(1)}, u32[]{:S(2)}, u32[]{:S(2)}) collective-permute-start(f32[4,8,1,32,128]{4,3,2,1,0:T(8,128)S(1)} %get-tuple-element.65), channel_id=1, source_target_pairs={{1,0},{2,1},{3,2},{4,3},{5,4},{6,5},{7,6},{8,7},{9,8},{10,9},{11,1... | collective-permute-start | bytes 1572872 | tf_op jit(solution)/shard_map/ppermute | solution.py:30
  259.7 0.8 fusion.66
  260.5 20.5 %collective-permute-done = f32[4,8,1,32,128]{4,3,2,1,0:T(8,128)S(1)} collective-permute-done((f32[4,8,1,32,128]{4,3,2,1,0:T(8,128)S(1)}, f32[4,8,1,32,128]{4,3,2,1,0:T(8,128)S(1)}, u32[]{:S(2)}, u32[]{:S(2)}) %collective-permute-start) | collective-permute-done | bytes 524320 | tf_op jit(solution)/shard_map/ppermute | solution.py:30
  281.0 0.7 collective-permute-done.1
  281.7 2.4 fusion
  284.1 0.8 fusion.58
  284.9 0.8 fusion.59
  285.8 4.0 %collective-permute-start.2 = (f32[4,8,1,32,128]{4,3,2,1,0:T(8,128)S(1)}, f32[4,8,1,32,128]{4,3,2,1,0:T(8,128)S(1)}, u32[]{:S(2)}, u32[]{:S(2)}) collective-permute-start(f32[4,8,1,32,128]{4,3,2,1,0:T(8,128)S(1)} %get-tuple-element.55), channel_id=1, source_target_pairs={{1,0},{2,1},{3,2},{4,3},{5,4},{6,5},{7,6},{8,7},{9,8},{10,9},{11,1... | collective-permute-start | bytes 1572872 | tf_op jit(solution)/shard_map/ppermute | solution.py:30
  290.0 0.8 fusion.61
  290.8 20.4 %collective-permute-done.2 = f32[4,8,1,32,128]{4,3,2,1,0:T(8,128)S(1)} collective-permute-done((f32[4,8,1,32,128]{4,3,2,1,0:T(8,128)S(1)}, f32[4,8,1,32,128]{4,3,2,1,0:T(8,128)S(1)}, u32[]{:S(2)}, u32[]{:S(2)}) %collective-permute-start.2) | collective-permute-done | bytes 524320 | tf_op jit(solution)/shard_map/ppermute | solution.py:30
  311.2 0.7 collective-permute-done.3
  311.9 2.4 fusion.1
  314.3 0.8 fusion.53
  315.2 0.8 fusion.54
  316.0 2.0 collective-permute-start.4
  318.0 0.4 collective-permute-start.5
  318.5 0.6 fusion.56
  319.1 22.3 %collective-permute-done.4 = f32[4,8,1,32,128]{4,3,2,1,0:T(8,128)S(1)} collective-permute-done((f32[4,8,1,32,128]{4,3,2,1,0:T(8,128)S(1)}, f32[4,8,1,32,128]{4,3,2,1,0:T(8,128)S(1)}, u32[]{:S(2)}, u32[]{:S(2)}) %collective-permute-start.4) | collective-permute-done | bytes 524320 | tf_op jit(solution)/shard_map/ppermute | solution.py:30
  341.4 2.6 fusion.3
  344.0 0.9 add_multiply_fusion
  (27 shorter events, 1.2 us)
Async XLA Ops:
  6.5 156.2 %all-reduce.3.cloned.1.call-start = ((), (), s32[]{:S(2)}) async-start(), calls=%async_computation | async-start | bytes 1048576 | tf_op jit(solution)/shard_map/psum | solution.py:18
  165.6 1.0 copy-start.2
  165.6 4.1 %copy-start.1 = (f32[4,4,32,128]{3,2,1,0:T(8,128)S(1)}, f32[4,4,32,128]{3,2,1,0:T(8,128)}, u32[]{:S(2)}) copy-start(f32[4,4,32,128]{3,2,1,0:T(8,128)} %get-tuple-element.5) | copy-start | bytes 786436
  166.6 24.0 %collective-permute-start.6 = (f32[4,8,1,32,128]{4,3,2,1,0:T(8,128)S(1)}, f32[4,8,1,32,128]{4,3,2,1,0:T(8,128)S(1)}, u32[]{:S(2)}, u32[]{:S(2)}) collective-permute-start(f32[4,8,1,32,128]{4,3,2,1,0:T(8,128)S(1)} %get-tuple-element.35), channel_id=1, source_target_pairs={{1,0},{2,1},{3,2},{4,3},{5,4},{6,5},{7,6},{8,7},{9,8},{10,9},{11,1... | collective-permute-start | bytes 1572872 | tf_op jit(solution)/shard_map/ppermute | solution.py:30
  169.7 21.0 %collective-permute-start.7 = (f32[4,8,1,32,128]{4,3,2,1,0:T(8,128)S(1)}, f32[4,8,1,32,128]{4,3,2,1,0:T(8,128)S(1)}, u32[]{:S(2)}, u32[]{:S(2)}) collective-permute-start(f32[4,8,1,32,128]{4,3,2,1,0:T(8,128)S(1)} %get-tuple-element.36), channel_id=1, source_target_pairs={{0,1},{1,2},{2,3},{3,4},{4,5},{5,6},{6,7},{7,8},{8,9},{9,10},{10,1... | collective-permute-start | bytes 1572872 | tf_op jit(solution)/shard_map/ppermute | solution.py:28
  169.8 21.0 %copy-start = (f32[8,4,32,128]{3,2,1,0:T(8,128)S(1)}, f32[8,4,32,128]{3,2,1,0:T(8,128)}, u32[]{:S(2)}) copy-start(f32[8,4,32,128]{3,2,1,0:T(8,128)} %param.2) | copy-start | bytes 1572868
  194.7 24.7 %collective-permute-start.8 = (f32[4,8,1,32,128]{4,3,2,1,0:T(8,128)S(1)}, f32[4,8,1,32,128]{4,3,2,1,0:T(8,128)S(1)}, u32[]{:S(2)}, u32[]{:S(2)}) collective-permute-start(f32[4,8,1,32,128]{4,3,2,1,0:T(8,128)S(1)} %get-tuple-element.25), channel_id=1, source_target_pairs={{1,0},{2,1},{3,2},{4,3},{5,4},{6,5},{7,6},{8,7},{9,8},{10,9},{11,1... | collective-permute-start | bytes 1572872 | tf_op jit(solution)/shard_map/ppermute | solution.py:30
  199.0 21.8 %collective-permute-start.9 = (f32[4,8,1,32,128]{4,3,2,1,0:T(8,128)S(1)}, f32[4,8,1,32,128]{4,3,2,1,0:T(8,128)S(1)}, u32[]{:S(2)}, u32[]{:S(2)}) collective-permute-start(f32[4,8,1,32,128]{4,3,2,1,0:T(8,128)S(1)} %get-tuple-element.26), channel_id=1, source_target_pairs={{0,1},{1,2},{2,3},{3,4},{4,5},{5,6},{6,7},{7,8},{8,9},{9,10},{10,1... | collective-permute-start | bytes 1572872 | tf_op jit(solution)/shard_map/ppermute | solution.py:28
  225.0 25.6 %collective-permute-start.10 = (f32[4,8,1,32,128]{4,3,2,1,0:T(8,128)S(1)}, f32[4,8,1,32,128]{4,3,2,1,0:T(8,128)S(1)}, u32[]{:S(2)}, u32[]{:S(2)}) collective-permute-start(f32[4,8,1,32,128]{4,3,2,1,0:T(8,128)S(1)} %get-tuple-element.15), channel_id=1, source_target_pairs={{1,0},{2,1},{3,2},{4,3},{5,4},{6,5},{7,6},{8,7},{9,8},{10,9},{11,1... | collective-permute-start | bytes 1572872 | tf_op jit(solution)/shard_map/ppermute | solution.py:30
  229.6 21.7 %collective-permute-start.11 = (f32[4,8,1,32,128]{4,3,2,1,0:T(8,128)S(1)}, f32[4,8,1,32,128]{4,3,2,1,0:T(8,128)S(1)}, u32[]{:S(2)}, u32[]{:S(2)}) collective-permute-start(f32[4,8,1,32,128]{4,3,2,1,0:T(8,128)S(1)} %get-tuple-element.16), channel_id=1, source_target_pairs={{0,1},{1,2},{2,3},{3,4},{4,5},{5,6},{6,7},{7,8},{8,9},{9,10},{10,1... | collective-permute-start | bytes 1572872 | tf_op jit(solution)/shard_map/ppermute | solution.py:28
  255.7 25.4 %collective-permute-start = (f32[4,8,1,32,128]{4,3,2,1,0:T(8,128)S(1)}, f32[4,8,1,32,128]{4,3,2,1,0:T(8,128)S(1)}, u32[]{:S(2)}, u32[]{:S(2)}) collective-permute-start(f32[4,8,1,32,128]{4,3,2,1,0:T(8,128)S(1)} %get-tuple-element.65), channel_id=1, source_target_pairs={{1,0},{2,1},{3,2},{4,3},{5,4},{6,5},{7,6},{8,7},{9,8},{10,9},{11,1... | collective-permute-start | bytes 1572872 | tf_op jit(solution)/shard_map/ppermute | solution.py:30
  259.6 22.1 %collective-permute-start.1 = (f32[4,8,1,32,128]{4,3,2,1,0:T(8,128)S(1)}, f32[4,8,1,32,128]{4,3,2,1,0:T(8,128)S(1)}, u32[]{:S(2)}, u32[]{:S(2)}) collective-permute-start(f32[4,8,1,32,128]{4,3,2,1,0:T(8,128)S(1)} %get-tuple-element.66), channel_id=1, source_target_pairs={{0,1},{1,2},{2,3},{3,4},{4,5},{5,6},{6,7},{7,8},{8,9},{9,10},{10,1... | collective-permute-start | bytes 1572872 | tf_op jit(solution)/shard_map/ppermute | solution.py:28
  285.8 25.4 %collective-permute-start.2 = (f32[4,8,1,32,128]{4,3,2,1,0:T(8,128)S(1)}, f32[4,8,1,32,128]{4,3,2,1,0:T(8,128)S(1)}, u32[]{:S(2)}, u32[]{:S(2)}) collective-permute-start(f32[4,8,1,32,128]{4,3,2,1,0:T(8,128)S(1)} %get-tuple-element.55), channel_id=1, source_target_pairs={{1,0},{2,1},{3,2},{4,3},{5,4},{6,5},{7,6},{8,7},{9,8},{10,9},{11,1... | collective-permute-start | bytes 1572872 | tf_op jit(solution)/shard_map/ppermute | solution.py:30
  289.9 22.0 %collective-permute-start.3 = (f32[4,8,1,32,128]{4,3,2,1,0:T(8,128)S(1)}, f32[4,8,1,32,128]{4,3,2,1,0:T(8,128)S(1)}, u32[]{:S(2)}, u32[]{:S(2)}) collective-permute-start(f32[4,8,1,32,128]{4,3,2,1,0:T(8,128)S(1)} %get-tuple-element.56), channel_id=1, source_target_pairs={{0,1},{1,2},{2,3},{3,4},{4,5},{5,6},{6,7},{7,8},{8,9},{9,10},{10,1... | collective-permute-start | bytes 1572872 | tf_op jit(solution)/shard_map/ppermute | solution.py:28
  316.0 25.4 %collective-permute-start.4 = (f32[4,8,1,32,128]{4,3,2,1,0:T(8,128)S(1)}, f32[4,8,1,32,128]{4,3,2,1,0:T(8,128)S(1)}, u32[]{:S(2)}, u32[]{:S(2)}) collective-permute-start(f32[4,8,1,32,128]{4,3,2,1,0:T(8,128)S(1)} %get-tuple-element.45), channel_id=1, source_target_pairs={{1,0},{2,1},{3,2},{4,3},{5,4},{6,5},{7,6},{8,7},{9,8},{10,9},{11,1... | collective-permute-start | bytes 1572872 | tf_op jit(solution)/shard_map/ppermute | solution.py:30
  318.0 23.4 %collective-permute-start.5 = (f32[4,8,1,32,128]{4,3,2,1,0:T(8,128)S(1)}, f32[4,8,1,32,128]{4,3,2,1,0:T(8,128)S(1)}, u32[]{:S(2)}, u32[]{:S(2)}) collective-permute-start(f32[4,8,1,32,128]{4,3,2,1,0:T(8,128)S(1)} %get-tuple-element.46), channel_id=1, source_target_pairs={{0,1},{1,2},{2,3},{3,4},{4,5},{5,6},{6,7},{7,8},{8,9},{9,10},{10,1... | collective-permute-start | bytes 1572872 | tf_op jit(solution)/shard_map/ppermute | solution.py:28
Sparse Core Ops, SparseCore 0:
  15.0 147.6 all-reduce.2
where the time goes:
time: 352 us
  waiting for transfers between devices  275 us (78%)
  starting transfers between devices  22.3 us (6%)
  other arithmetic  19.2 us (5%)
  between operations  18.8 us (5%)
  local copies, waits for them, and re-layouts  16.6 us (5%)
    psum x1, waiting for transfers between devices, spread(): return lax.psum(block, axis)  148 us
    ppermute x6, waiting for transfers between devices, extended_2(): lax.ppermute(head, axis, [((i + 1) % count, i) for i in range(count)])  123 us
    ppermute x6, starting transfers between devices, extended_2(): lax.ppermute(head, axis, [((i + 1) % count, i) for i in range(count)])  21.9 us
    div x4, other arithmetic, local(): potential = (neighbours + density) / (6.0 + screen)  9.72 us
    slice x12, local copies, waits for them, and re-layouts, neighbour_sum(): jnp.roll(potential, 1, 4)  9.34 us
  transfers between devices with their start and end apart: 13, of which 12 were waited for; matrix products, arithmetic and copies ran while one was open for 1% of the time, Pallas kernels for 0%

commit v1 on v0

v1 whole, which is shorter than its diff:
```python
import itertools

import jax
import jax.numpy as jnp
import numpy as np
from jax import lax
from jax.experimental import pallas as pl
from jax.experimental.pallas import tpu as pltpu
from jax.sharding import PartitionSpec as P

LOCAL = 8
BLOCK = 4
SWEEPS = 3
ROWS = 8
screen = 0.5
exchange_scale = 0.25


def stencil():
    steps = [tuple(s * (d == k) for d in range(3)) for k in range(3) for s in (1, -1)]
    taps = {(0, 0, 0): 1.0 / screen}
    for _ in range(SWEEPS):
        spread = {(0, 0, 0): 1.0}
        for at, weight in taps.items():
            for step in steps:
                to = tuple(a + s for a, s in zip(at, step))
                spread[to] = spread.get(to, 0.0) + weight
        taps = {at: weight / (6.0 + screen) for at, weight in spread.items()}
    return {at: -exchange_scale * weight for at, weight in taps.items()}


TAPS = stencil()
REACH = SWEEPS


def pad_rows(dst, at, layer, cells):
    ny = cells.shape[0]
    dst[at, layer, ROWS : ROWS + ny] = cells
    dst[at, layer, 0:ROWS] = cells[ny - ROWS :]
    dst[at, layer, ROWS + ny :] = cells[:ROWS]


def turned(cells, shift):
    return pltpu.roll(cells, shift % cells.shape[-1], cells.ndim - 1) if shift else cells


def apply_taps(y0, x, pairs, centre, padded_b, padded_phi, sums):
    count = len(sums)
    for reach in range(REACH + 1):
        shifts = (0,) if reach == 0 else (reach, -reach)
        reached = [
            (dx, dy, layer)
            for dx, layer in pairs
            for dy in range(-REACH, REACH + 1)
            if abs(dx) + abs(dy) + reach <= REACH
        ]
        if not reached:
            continue
        here = {dz: [centre(dz, i, x, y0) for i in range(count)] for dz in shifts}
        totals = {dz: [None] * count for dz in shifts}
        for dx, dy, layer in reached:
            rows = pl.ds(y0 + ROWS + dy, ROWS)
            there = [padded_b[i, layer, rows, :] for i in range(count)]
            weights = {}
            for dz in shifts:
                gram = here[dz][0] * there[0]
                for i in range(1, count):
                    gram = gram + here[dz][i] * there[i]
                weights[dz] = gram * np.float32(TAPS[dx, dy, dz])
            for j in range(count):
                phi = padded_phi[j, layer, rows, :]
                for dz in shifts:
                    part = weights[dz] * phi
                    totals[dz][j] = part if totals[dz][j] is None else totals[dz][j] + part
        for dz in shifts:
            for j in range(count):
                sums[j] = sums[j] + turned(totals[dz][j], -dz)
    return sums


def inner_kernel(phi, b_mine, b_other, out, padded_phi, padded_b, rolled):
    count, nx, ny, _ = phi.shape

    def fill(i, _):
        for x in range(nx):
            pad_rows(padded_phi, i, x, phi[i, x])
            pad_rows(padded_phi, i + BLOCK, x, phi[i + BLOCK, x])
            for source, at in ((b_mine, i), (b_other, i + BLOCK)):
                cells = source[i, x]
                pad_rows(padded_b, at, x, cells)
                for dz in range(1, REACH + 1):
                    rolled[2 * dz - 2, at, x] = turned(cells, dz)
                    rolled[2 * dz - 1, at, x] = turned(cells, -dz)
        return 0

    lax.fori_loop(0, BLOCK, fill, 0)

    def centre(dz, i, x, y0):
        if dz == 0:
            return padded_b[i, x, pl.ds(y0 + ROWS, ROWS), :]
        return rolled[2 * abs(dz) - (2 if dz > 0 else 1), i, x, pl.ds(y0, ROWS), :]

    def tile(t, _):
        y0 = pl.multiple_of(t * ROWS, ROWS)
        for x in range(nx):
            pairs = [(to - x, to) for to in range(nx) if abs(to - x) <= REACH]
            sums = [jnp.zeros((ROWS, phi.shape[3]), jnp.float32)] * count
            sums = apply_taps(y0, x, pairs, centre, padded_b, padded_phi, sums)
            for j in range(count):
                out[j, x, pl.ds(y0, ROWS), :] = sums[j]
        return 0

    lax.fori_loop(0, ny // ROWS, tile, 0)


def outer_kernel(
    part, phi_low, phi_high, b_mine, b_other, low_mine, low_other, high_mine, high_other,
    out, padded_phi, padded_b, rolled,
):
    count, nx, ny, _ = part.shape

    def fill(i, _):
        for layer in range(REACH):
            for k in (0, BLOCK):
                pad_rows(padded_phi, i + k, layer, phi_low[i + k, layer])
                pad_rows(padded_phi, i + k, REACH + layer, phi_high[i + k, layer])
            pad_rows(padded_b, i, layer, low_mine[i, layer])
            pad_rows(padded_b, i + BLOCK, layer, low_other[i, layer])
            pad_rows(padded_b, i, REACH + layer, high_mine[i, layer])
            pad_rows(padded_b, i + BLOCK, REACH + layer, high_other[i, layer])
        for x in range(nx):
            for source, at in ((b_mine, i), (b_other, i + BLOCK)):
                cells = source[i, x]
                for dz in range(1, REACH):
                    if dz == 1 or x in (0, nx - 1):
                        rolled[2 * dz - 2, at, x] = turned(cells, dz)
                        rolled[2 * dz - 1, at, x] = turned(cells, -dz)
        return 0

    lax.fori_loop(0, BLOCK, fill, 0)

    def centre(dz, i, x, y0):
        if dz == 0:
            return (b_mine if i < BLOCK else b_other)[i % BLOCK, x, pl.ds(y0, ROWS), :]
        return rolled[2 * abs(dz) - (2 if dz > 0 else 1), i, x, pl.ds(y0, ROWS), :]

    def tile(t, _):
        y0 = pl.multiple_of(t * ROWS, ROWS)
        for x in range(nx):
            pairs = [(layer - REACH - x, layer) for layer in range(REACH) if x - (layer - REACH) <= REACH]
            pairs += [(nx + layer - x, REACH + layer) for layer in range(REACH) if nx + layer - x <= REACH]
            sums = [part[j, x, pl.ds(y0, ROWS), :] for j in range(count)]
            sums = apply_taps(y0, x, pairs, centre, padded_b, padded_phi, sums)
            for j in range(count):
                out[j, x, pl.ds(y0, ROWS), :] = sums[j]
        return 0

    lax.fori_loop(0, ny // ROWS, tile, 0)


def call(kernel, count, nx, ny, nz, layers, rolls, args):
    f32 = jnp.float32
    whole = pl.BlockSpec(memory_space=pltpu.VMEM)
    return pl.pallas_call(
        kernel,
        out_shape=jax.ShapeDtypeStruct((count, nx, ny, nz), f32),
        in_specs=[whole] * len(args),
        out_specs=whole,
        scratch_shapes=[
            pltpu.VMEM((count, layers, ny + 2 * ROWS, nz), f32),
            pltpu.VMEM((count, layers, ny + 2 * ROWS, nz), f32),
            pltpu.VMEM((rolls, count, nx, ny, nz), f32),
        ],
        compiler_params=pltpu.CompilerParams(vmem_limit_bytes=32 * 1024 * 1024),
    )(*args)


def local(orbitals, owner_order):
    count, nx, ny, nz = orbitals.shape
    halves = LOCAL // BLOCK
    band = lax.axis_index("band")
    bands, doms = lax.axis_size("band"), lax.axis_size("dom")
    chips = bands // 2
    core = band % 2
    same_core = [[2 * chip + c for chip in range(chips)] for c in range(2)]
    partner = [(i, i ^ 1) for i in range(bands)]
    up = [(i, (i + 1) % doms) for i in range(doms)]
    down = [((i + 1) % doms, i) for i in range(doms)]

    phi_low = lax.ppermute(orbitals[:, nx - REACH :], "dom", up)
    phi_high = lax.ppermute(orbitals[:, :REACH], "dom", down)

    mine, theirs = owner_order[core], owner_order[1 - core]
    own = lax.dynamic_slice_in_dim(orbitals, mine % halves * BLOCK, BLOCK, 0)
    give = lax.dynamic_slice_in_dim(orbitals, theirs % halves * BLOCK, BLOCK, 0)
    got = lax.ppermute(give, "band", partner)
    owner = mine // halves
    chosen = jnp.where(owner % 2 == core, own, got)
    chunks = chosen.reshape(chips, BLOCK * nx // chips, ny, nz)
    chunks = lax.all_to_all(chunks, "band", 0, 0, axis_index_groups=same_core)
    chunk = lax.dynamic_index_in_dim(chunks, owner // 2, 0, keepdims=True)
    chunks = jnp.broadcast_to(chunk, chunks.shape)
    b_mine = lax.all_to_all(chunks, "band", 0, 0, axis_index_groups=same_core)
    b_mine = b_mine.reshape(BLOCK, nx, ny, nz)

    low_mine = lax.ppermute(b_mine[:, nx - REACH :], "dom", up)
    high_mine = lax.ppermute(b_mine[:, :REACH], "dom", down)
    b_other = lax.ppermute(b_mine, "band", partner)

    part = call(inner_kernel, count, nx, ny, nz, nx, 2 * REACH, (orbitals, b_mine, b_other))

    low_other = lax.ppermute(low_mine, "band", partner)
    high_other = lax.ppermute(high_mine, "band", partner)
    return call(
        outer_kernel, count, nx, ny, nz, 2 * REACH, 2 * REACH - 2,
        (part, phi_low, phi_high, b_mine, b_other, low_mine, low_other, high_mine, high_other),
    )


def solution(mesh):
    in_specs = (P("band", "dom", None, None), P())
    out_specs = P("band", "dom", None, None)
    return jax.shard_map(local, mesh=mesh, in_specs=in_specs, out_specs=out_specs, check_vma=False)
```

time: 352 us -> 70.2 us (0.20)
  waiting for transfers between devices: 275 us -> 10.6 us
  starting transfers between devices: 22.3 us -> 42.1 us
  other arithmetic: 19.2 us -> 0.74 us
  between operations: 18.8 us -> 4.61 us
  local copies, waits for them, and re-layouts: 16.6 us -> 3.2 us
  Pallas kernels: 0 us -> 8.47 us
    psum x1 -> x0, waiting for transfers between devices: 148 us -> none  [spread(): return lax.psum(block, axis)]
    ppermute x12 -> x8, waiting for transfers between devices: 127 us -> 1.2 us  [the longest x1 1.18 us: local(): high_mine = lax.ppermute(b_mine[:, :REACH], 'dom', down)]
    slice x31 -> x2, local copies, waits for them, and re-layouts: 15.9 us -> 0.11 us  [the longest x1 0.08 us: local(): phi_high = lax.ppermute(orbitals[:, :REACH], 'dom', down)]
    div x5 -> x0, other arithmetic: 11.1 us -> none  [the longest x4 9.72 us: local(): potential = (neighbours + density) / (6.0 + screen)]
    ppermute x12 -> x8, starting transfers between devices: 22.3 us -> 33.1 us  [the longest x1 11.8 us: local(): b_other = lax.ppermute(b_mine, 'band', partner)]
    all_to_all x0 -> x2, waiting for transfers between devices: none -> 9.43 us  [the longest x1 7.63 us: local(): chunks = lax.all_to_all(chunks, 'band', 0, 0, axis_index_groups=same_core)]
    all_to_all x0 -> x2, starting transfers between devices: none -> 9.01 us  [the longest x1 4.91 us: local(): chunks = lax.all_to_all(chunks, 'band', 0, 0, axis_index_groups=same_core)]
    pallas_call x0 -> x2, Pallas kernels: none -> 8.47 us  [call(): pl.pallas_call(kernel, out_shape=jax.ShapeDtypeStruct((count, nx, ny, nz)...]
  transfers between devices with their start and end apart: 13 -> 10, of which waited for: 12 -> 3; matrix products, arithmetic and copies ran while one was open for 1% -> 0% of each run, Pallas kernels for 0% -> 8%
where the time goes in v1:
time: 70.2 us; the launch traced here: 69.8 us
  starting transfers between devices  42.1 us (60%)
  waiting for transfers between devices  10.6 us (15%)
  Pallas kernels  8.47 us (12%)
  between operations  4.61 us (7%)
  local copies, waits for them, and re-layouts  3.2 us (5%)
  other arithmetic  0.74 us (1%)
    ppermute x1, starting transfers between devices, local(): b_other = lax.ppermute(b_mine, 'band', partner)  11.8 us
    pallas_call x2, Pallas kernels, call(): pl.pallas_call(kernel, out_shape=jax.ShapeDtypeStruct((count, nx, ny, nz)...  8.47 us
    all_to_all x1, waiting for transfers between devices, local(): chunks = lax.all_to_all(chunks, 'band', 0, 0, axis_index_groups=same_core)  7.63 us
    ppermute x1, starting transfers between devices, local(): phi_high = lax.ppermute(orbitals[:, :REACH], 'dom', down)  5.68 us
    ppermute x1, starting transfers between devices, local(): high_mine = lax.ppermute(b_mine[:, :REACH], 'dom', down)  5.68 us
    all_to_all x1, starting transfers between devices, local(): chunks = lax.all_to_all(chunks, 'band', 0, 0, axis_index_groups=same_core)  4.91 us
    ppermute x1, starting transfers between devices, local(): low_other = lax.ppermute(low_mine, 'band', partner)  4.59 us
    all_to_all x1, starting transfers between devices, local(): b_mine = lax.all_to_all(chunks, 'band', 0, 0, axis_index_groups=same_core)  4.09 us
  transfers between devices with their start and end apart: 10, of which 3 were waited for; matrix products, arithmetic and copies ran while one was open for 0% of the time, Pallas kernels for 8%

profile of v1, /device:TPU:1, one launch (start us, length us, event | category | flops | bytes accessed | tf_op | source)
XLA Modules:
  0.0 69.8 jit_solution(18077643647964790175)
XLA Ops:
  0.0 0.0 copy-start
  0.0 1.4 %fusion.2 = (s32[1]{0:T(128)}, s32[1]{0:T(128)}) fusion(s32[32]{0:T(128)} %param.3, s32[]{:T(128)S(6)} %select_n.51, s32[]{:T(128)S(6)} %select_n.57), kind=kLoop, calls=%fused_computation.5 | loop fusion | bytes 24 | tf_op jit(solution)/shard_map/dynamic_slice | solution.py:193
  3.3 1.0 %constant_dynamic-slice_fusion = f32[4,4,32,128]{3,2,1,0:T(8,128)S(1)} fusion(f32[8,4,32,128]{3,2,1,0:T(8,128)} %phi.1, s32[]{:T(128)S(6)} %select_n.59), kind=kLoop, calls=%fused_computation.2 | loop fusion | bytes 524292 | tf_op jit(solution)/shard_map/dynamic_slice | solution.py:195
  4.2 3.3 %collective-permute-start = (f32[4,4,32,128]{3,2,1,0:T(8,128)S(1)}, f32[4,4,32,128]{3,2,1,0:T(8,128)S(1)}, u32[]{:S(2)}, u32[]{:S(2)}) collective-permute-start(f32[4,4,32,128]{3,2,1,0:T(8,128)S(1)} %constant_dynamic-slice_fusion), channel_id=1, source_target_pairs={{0,16},{16,0},{32,48},{48,32},{64,80},{80,64},{96,112},{112,96},{1... | collective-permute-start | bytes 786440 | tf_op jit(solution)/shard_map/ppermute | solution.py:196
  10.2 0.0 collective-permute-done
  10.2 0.0 copy-done
  10.2 0.7 %dynamic-slice_select_fusion = f32[4,4,32,128]{3,2,1,0:T(8,128)} fusion(f32[4,4,32,128]{3,2,1,0:T(8,128)S(1)} %collective-permute-done, f32[8,4,32,128]{3,2,1,0:T(8,128)S(1)} %copy-done, s32[]{:T(128)S(6)} %select_n.56, pred[]{:T(512)S(6)} %eq.8), kind=kLoop, calls=%fused_computation | loop fusion | flops 65536 | bytes 786437 | tf_op jit(solution)/shard_map/jit(_where)/select_n | solution.py:198
  11.0 4.9 %all-to-all-start = ((f32[8,2,32,128]{3,2,1,0:T(8,128)}), f32[8,2,32,128]{3,2,1,0:T(8,128)S(1)}, u32[]{:S(2)}, u32[]{:S(2)}) async-start(f32[8,2,32,128]{3,2,1,0:T(8,128)} %bitcast.2), calls=%async_computation | async-start | bytes 524288 | tf_op jit(solution)/shard_map/all_to_all | solution.py:200
  15.9 7.6 %all-to-all-done = f32[8,2,32,128]{3,2,1,0:T(8,128)S(1)} async-done(((f32[8,2,32,128]{3,2,1,0:T(8,128)}), f32[8,2,32,128]{3,2,1,0:T(8,128)S(1)}, u32[]{:S(2)}, u32[]{:S(2)}) %all-to-all-start) | async-done | bytes 262176 | tf_op jit(solution)/shard_map/all_to_all | solution.py:200
  23.5 0.7 %broadcast_in_dim.8 = f32[8,2,32,128]{3,2,1,0:T(8,128)} broadcast(f32[2,32,128]{2,1,0:T(8,128)S(1)} %dynamic-slice_bitcast_fusion), dimensions={1,2,3} | broadcast | bytes 294912 | tf_op jit(solution)/shard_map/broadcast_in_dim | solution.py:202
  24.2 4.1 %all-to-all-start.1 = ((f32[8,2,32,128]{3,2,1,0:T(8,128)}), f32[8,2,32,128]{3,2,1,0:T(8,128)S(1)}, u32[]{:S(2)}, u32[]{:S(2)}) async-start(f32[8,2,32,128]{3,2,1,0:T(8,128)} %broadcast_in_dim.8), calls=%async_computation.1 | async-start | bytes 524288 | tf_op jit(solution)/shard_map/all_to_all | solution.py:203
  28.3 0.1 fusion
  28.4 5.7 %collective-permute-start.3 = (f32[8,3,32,128]{3,2,1,0:T(8,128)S(1)}, f32[8,3,32,128]{3,2,1,0:T(8,128)S(1)}, u32[]{:S(2)}, u32[]{:S(2)}) collective-permute-start(f32[8,3,32,128]{3,2,1,0:T(8,128)S(1)} %get-tuple-element.5), channel_id=1, source_target_pairs={{1,0},{2,1},{3,2},{4,3},{5,4},{6,5},{7,6},{8,7},{9,8},{10,9},{11,1... | collective-permute-start | bytes 1179656 | tf_op jit(solution)/shard_map/ppermute | solution.py:191
  34.1 0.0 collective-permute-start.2
  34.1 1.8 %all-to-all-done.1 = f32[8,2,32,128]{3,2,1,0:T(8,128)S(1)} async-done(((f32[8,2,32,128]{3,2,1,0:T(8,128)}), f32[8,2,32,128]{3,2,1,0:T(8,128)S(1)}, u32[]{:S(2)}, u32[]{:S(2)}) %all-to-all-start.1) | async-done | bytes 262176 | tf_op jit(solution)/shard_map/all_to_all | solution.py:203
  36.0 5.7 %collective-permute-start.6 = (f32[4,3,32,128]{3,2,1,0:T(8,128)S(1)}, f32[4,3,32,128]{3,2,1,0:T(8,128)S(1)}, u32[]{:S(2)}, u32[]{:S(2)}) collective-permute-start(f32[4,3,32,128]{3,2,1,0:T(8,128)S(1)} %get-tuple-element.7), channel_id=1, source_target_pairs={{1,0},{2,1},{3,2},{4,3},{5,4},{6,5},{7,6},{8,7},{9,8},{10,9},{11,1... | collective-permute-start | bytes 589832 | tf_op jit(solution)/shard_map/ppermute | solution.py:207
  41.6 0.0 collective-permute-start.4
  41.6 11.8 %collective-permute-start.1 = (f32[4,4,32,128]{3,2,1,0:T(8,128)S(1)}, f32[4,4,32,128]{3,2,1,0:T(8,128)S(1)}, u32[]{:S(2)}, u32[]{:S(2)}) collective-permute-start(f32[4,4,32,128]{3,2,1,0:T(8,128)S(1)} %bitcast.7), channel_id=1, source_target_pairs={{0,16},{16,0},{32,48},{48,32},{64,80},{80,64},{96,112},{112,96},{1... | collective-permute-start | bytes 786440 | tf_op jit(solution)/shard_map/ppermute | solution.py:208
  53.5 1.2 %collective-permute-done.6.high_mine = f32[4,3,32,128]{3,2,1,0:T(8,128)S(1)} collective-permute-done((f32[4,3,32,128]{3,2,1,0:T(8,128)S(1)}, f32[4,3,32,128]{3,2,1,0:T(8,128)S(1)}, u32[]{:S(2)}, u32[]{:S(2)}) %collective-permute-start.6) | collective-permute-done | bytes 196640 | tf_op jit(solution)/shard_map/ppermute | solution.py:207
  54.7 2.0 %collective-permute-start.7 = (f32[4,3,32,128]{3,2,1,0:T(8,128)S(1)}, f32[4,3,32,128]{3,2,1,0:T(8,128)S(1)}, u32[]{:S(2)}, u32[]{:S(2)}) collective-permute-start(f32[4,3,32,128]{3,2,1,0:T(8,128)S(1)} %collective-permute-done.6.high_mine), channel_id=1, source_target_pairs={{0,16},{16,0},{32,48},{48,32},{64,80},{80,64},{96,112},{112,96},{1... | collective-permute-start | bytes 589832 | tf_op jit(solution)/shard_map/ppermute | solution.py:213
  56.7 0.0 collective-permute-done.4.low_mine
  56.7 4.6 %collective-permute-start.5 = (f32[4,3,32,128]{3,2,1,0:T(8,128)S(1)}, f32[4,3,32,128]{3,2,1,0:T(8,128)S(1)}, u32[]{:S(2)}, u32[]{:S(2)}) collective-permute-start(f32[4,3,32,128]{3,2,1,0:T(8,128)S(1)} %collective-permute-done.4.low_mine), channel_id=1, source_target_pairs={{0,16},{16,0},{32,48},{48,32},{64,80},{80,64},{96,112},{112,96},{1... | collective-permute-start | bytes 589832 | tf_op jit(solution)/shard_map/ppermute | solution.py:212
  61.3 0.0 collective-permute-done.1.b_other
  61.3 5.7 %shard_map.28.part = f32[8,4,32,128]{3,2,1,0:T(8,128)S(1)} custom-call(f32[8,4,32,128]{3,2,1,0:T(8,128)S(1)} %copy-done, f32[4,4,32,128]{3,2,1,0:T(8,128)S(1)} %bitcast.8, f32[4,4,32,128]{3,2,1,0:T(8,128)S(1)} %collective-permute-done.1.b_other), custom_call_target="tpu_custom_call" | custom-call | tf_op jit(solution)/shard_map/pallas_call | solution.py:164
  67.0 0.0 collective-permute-done.3.phi_high
  67.0 0.0 collective-permute-done.2.phi_low
  67.0 0.0 collective-permute-done.7.high_other
  67.1 0.0 collective-permute-done.5.low_other
  67.1 2.7 %shard_map.29 = f32[8,4,32,128]{3,2,1,0:T(8,128)} custom-call(f32[8,4,32,128]{3,2,1,0:T(8,128)S(1)} %shard_map.28.part, f32[8,3,32,128]{3,2,1,0:T(8,128)S(1)} %collective-permute-done.2.phi_low, f32[8,3,32,128]{3,2,1,0:T(8,128)S(1)} %collective-permute-done.3.phi_high, f32[4,4,32,128]{3,2,1,0:T(8,128)S(1)} %bitcast.9, ...), custom_call_target="tpu_custom_call" | custom-call | tf_op jit(solution)/shard_map/pallas_call | solution.py:164
  (2 shorter events, 0.0 us)
Async XLA Ops:
  0.0 10.2 %copy-start = (f32[8,4,32,128]{3,2,1,0:T(8,128)S(1)}, f32[8,4,32,128]{3,2,1,0:T(8,128)}, u32[]{:S(2)}) copy-start(f32[8,4,32,128]{3,2,1,0:T(8,128)} %phi.1) | copy-start | bytes 1572868
  4.2 6.0 %collective-permute-start = (f32[4,4,32,128]{3,2,1,0:T(8,128)S(1)}, f32[4,4,32,128]{3,2,1,0:T(8,128)S(1)}, u32[]{:S(2)}, u32[]{:S(2)}) collective-permute-start(f32[4,4,32,128]{3,2,1,0:T(8,128)S(1)} %constant_dynamic-slice_fusion), channel_id=1, source_target_pairs={{0,16},{16,0},{32,48},{48,32},{64,80},{80,64},{96,112},{112,96},{1... | collective-permute-start | bytes 786440 | tf_op jit(solution)/shard_map/ppermute | solution.py:196
  11.0 12.5 %all-to-all-start = ((f32[8,2,32,128]{3,2,1,0:T(8,128)}), f32[8,2,32,128]{3,2,1,0:T(8,128)S(1)}, u32[]{:S(2)}, u32[]{:S(2)}) async-start(f32[8,2,32,128]{3,2,1,0:T(8,128)} %bitcast.2), calls=%async_computation | async-start | bytes 524288 | tf_op jit(solution)/shard_map/all_to_all | solution.py:200
  24.2 11.7 %all-to-all-start.1 = ((f32[8,2,32,128]{3,2,1,0:T(8,128)}), f32[8,2,32,128]{3,2,1,0:T(8,128)S(1)}, u32[]{:S(2)}, u32[]{:S(2)}) async-start(f32[8,2,32,128]{3,2,1,0:T(8,128)} %broadcast_in_dim.8), calls=%async_computation.1 | async-start | bytes 524288 | tf_op jit(solution)/shard_map/all_to_all | solution.py:203
  28.4 38.6 %collective-permute-start.3 = (f32[8,3,32,128]{3,2,1,0:T(8,128)S(1)}, f32[8,3,32,128]{3,2,1,0:T(8,128)S(1)}, u32[]{:S(2)}, u32[]{:S(2)}) collective-permute-start(f32[8,3,32,128]{3,2,1,0:T(8,128)S(1)} %get-tuple-element.5), channel_id=1, source_target_pairs={{1,0},{2,1},{3,2},{4,3},{5,4},{6,5},{7,6},{8,7},{9,8},{10,9},{11,1... | collective-permute-start | bytes 1179656 | tf_op jit(solution)/shard_map/ppermute | solution.py:191
  34.1 32.9 %collective-permute-start.2 = (f32[8,3,32,128]{3,2,1,0:T(8,128)S(1)}, f32[8,3,32,128]{3,2,1,0:T(8,128)S(1)}, u32[]{:S(2)}, u32[]{:S(2)}) collective-permute-start(f32[8,3,32,128]{3,2,1,0:T(8,128)S(1)} %get-tuple-element.6), channel_id=1, source_target_pairs={{0,1},{1,2},{2,3},{3,4},{4,5},{5,6},{6,7},{7,8},{8,9},{9,10},{10,1... | collective-permute-start | bytes 1179656 | tf_op jit(solution)/shard_map/ppermute | solution.py:190
  36.0 18.7 %collective-permute-start.6 = (f32[4,3,32,128]{3,2,1,0:T(8,128)S(1)}, f32[4,3,32,128]{3,2,1,0:T(8,128)S(1)}, u32[]{:S(2)}, u32[]{:S(2)}) collective-permute-start(f32[4,3,32,128]{3,2,1,0:T(8,128)S(1)} %get-tuple-element.7), channel_id=1, source_target_pairs={{1,0},{2,1},{3,2},{4,3},{5,4},{6,5},{7,6},{8,7},{9,8},{10,9},{11,1... | collective-permute-start | bytes 589832 | tf_op jit(solution)/shard_map/ppermute | solution.py:207
  41.6 15.0 %collective-permute-start.4 = (f32[4,3,32,128]{3,2,1,0:T(8,128)S(1)}, f32[4,3,32,128]{3,2,1,0:T(8,128)S(1)}, u32[]{:S(2)}, u32[]{:S(2)}) collective-permute-start(f32[4,3,32,128]{3,2,1,0:T(8,128)S(1)} %get-tuple-element.8), channel_id=1, source_target_pairs={{0,1},{1,2},{2,3},{3,4},{4,5},{5,6},{6,7},{7,8},{8,9},{9,10},{10,1... | collective-permute-start | bytes 589832 | tf_op jit(solution)/shard_map/ppermute | solution.py:206
  41.6 19.6 %collective-permute-start.1 = (f32[4,4,32,128]{3,2,1,0:T(8,128)S(1)}, f32[4,4,32,128]{3,2,1,0:T(8,128)S(1)}, u32[]{:S(2)}, u32[]{:S(2)}) collective-permute-start(f32[4,4,32,128]{3,2,1,0:T(8,128)S(1)} %bitcast.7), channel_id=1, source_target_pairs={{0,16},{16,0},{32,48},{48,32},{64,80},{80,64},{96,112},{112,96},{1... | collective-permute-start | bytes 786440 | tf_op jit(solution)/shard_map/ppermute | solution.py:208
  54.7 12.4 %collective-permute-start.7 = (f32[4,3,32,128]{3,2,1,0:T(8,128)S(1)}, f32[4,3,32,128]{3,2,1,0:T(8,128)S(1)}, u32[]{:S(2)}, u32[]{:S(2)}) collective-permute-start(f32[4,3,32,128]{3,2,1,0:T(8,128)S(1)} %collective-permute-done.6.high_mine), channel_id=1, source_target_pairs={{0,16},{16,0},{32,48},{48,32},{64,80},{80,64},{96,112},{112,96},{1... | collective-permute-start | bytes 589832 | tf_op jit(solution)/shard_map/ppermute | solution.py:213
  56.7 10.4 %collective-permute-start.5 = (f32[4,3,32,128]{3,2,1,0:T(8,128)S(1)}, f32[4,3,32,128]{3,2,1,0:T(8,128)S(1)}, u32[]{:S(2)}, u32[]{:S(2)}) collective-permute-start(f32[4,3,32,128]{3,2,1,0:T(8,128)S(1)} %collective-permute-done.4.low_mine), channel_id=1, source_target_pairs={{0,16},{16,0},{32,48},{48,32},{64,80},{80,64},{96,112},{112,96},{1... | collective-permute-start | bytes 589832 | tf_op jit(solution)/shard_map/ppermute | solution.py:212

commit v2 on v1

--- a/solution.py
+++ b/solution.py
@@ -190,24 +190,25 @@
     phi_low = lax.ppermute(orbitals[:, nx - REACH :], "dom", up)
     phi_high = lax.ppermute(orbitals[:, :REACH], "dom", down)
 
-    mine, theirs = owner_order[core], owner_order[1 - core]
-    own = lax.dynamic_slice_in_dim(orbitals, mine % halves * BLOCK, BLOCK, 0)
-    give = lax.dynamic_slice_in_dim(orbitals, theirs % halves * BLOCK, BLOCK, 0)
-    got = lax.ppermute(give, "band", partner)
+    got = lax.ppermute(orbitals, "band", partner)
+    mine = owner_order[core]
     owner = mine // halves
-    chosen = jnp.where(owner % 2 == core, own, got)
+    chosen = jnp.where(owner % 2 == core, orbitals, got)
+    chosen = lax.dynamic_slice_in_dim(chosen, mine % halves * BLOCK, BLOCK, 0)
     chunks = chosen.reshape(chips, BLOCK * nx // chips, ny, nz)
     chunks = lax.all_to_all(chunks, "band", 0, 0, axis_index_groups=same_core)
     chunk = lax.dynamic_index_in_dim(chunks, owner // 2, 0, keepdims=True)
+    chunk, phi_low = lax.optimization_barrier((chunk, phi_low))
     chunks = jnp.broadcast_to(chunk, chunks.shape)
     b_mine = lax.all_to_all(chunks, "band", 0, 0, axis_index_groups=same_core)
+    b_mine, phi_high = lax.optimization_barrier((b_mine, phi_high))
     b_mine = b_mine.reshape(BLOCK, nx, ny, nz)
 
     low_mine = lax.ppermute(b_mine[:, nx - REACH :], "dom", up)
     high_mine = lax.ppermute(b_mine[:, :REACH], "dom", down)
     b_other = lax.ppermute(b_mine, "band", partner)
-
     part = call(inner_kernel, count, nx, ny, nz, nx, 2 * REACH, (orbitals, b_mine, b_other))
+    low_mine, high_mine, part = lax.optimization_barrier((low_mine, high_mine, part))
 
     low_other = lax.ppermute(low_mine, "band", partner)
     high_other = lax.ppermute(high_mine, "band", partner)

time: 70.2 us -> 66.8 us (0.952)
  starting transfers between devices: 42.1 us -> 30 us
  waiting for transfers between devices: 10.6 us -> 21.3 us
  between operations: 4.61 us -> 2.74 us
    ppermute x1, waiting for transfers between devices: 0.01 us -> 9.45 us  [local(): low_mine = lax.ppermute(b_mine[:, nx - REACH:], 'dom', up)]
    ppermute x1, starting transfers between devices: 5.68 us -> 0.08 us  [local(): high_mine = lax.ppermute(b_mine[:, :REACH], 'dom', down)]
    all_to_all x1, waiting for transfers between devices: 7.63 us -> 2.86 us  [local(): chunks = lax.all_to_all(chunks, 'band', 0, 0, axis_index_groups=same_core)]
    ppermute x1, starting transfers between devices: 4.59 us -> 0.78 us  [local(): low_other = lax.ppermute(low_mine, 'band', partner)]
    all_to_all x1, waiting for transfers between devices: 1.81 us -> 5.17 us  [local(): b_mine = lax.all_to_all(chunks, 'band', 0, 0, axis_index_groups=same_core)]
    ppermute x1, waiting for transfers between devices: 0.01 us -> 2.41 us  [local(): phi_high = lax.ppermute(orbitals[:, :REACH], 'dom', down)]
    ppermute x1, starting transfers between devices: 11.8 us -> 9.47 us  [local(): b_other = lax.ppermute(b_mine, 'band', partner)]
    ppermute x1, starting transfers between devices: 2 us -> 0.01 us  [local(): high_other = lax.ppermute(high_mine, 'band', partner)]
  transfers between devices with their start and end apart: 10 -> 10, of which waited for: 3 -> 6; matrix products, arithmetic and copies ran while one was open for 0% -> 5% of each run, Pallas kernels for 8% -> 9%
where the time goes in v2:
time: 66.8 us; the launch traced here: 66.5 us
  starting transfers between devices  30 us (45%)
  waiting for transfers between devices  21.3 us (32%)
  Pallas kernels  8.47 us (13%)
  local copies, waits for them, and re-layouts  3.17 us (5%)
  between operations  2.74 us (4%)
  other arithmetic  0.74 us (1%)
    ppermute x1, starting transfers between devices, local(): b_other = lax.ppermute(b_mine, 'band', partner)  9.47 us
    ppermute x1, waiting for transfers between devices, local(): low_mine = lax.ppermute(b_mine[:, nx - REACH:], 'dom', up)  9.45 us
    pallas_call x2, Pallas kernels, call(): pl.pallas_call(kernel, out_shape=jax.ShapeDtypeStruct((count, nx, ny, nz)...  8.47 us
    all_to_all x1, starting transfers between devices, local(): chunks = lax.all_to_all(chunks, 'band', 0, 0, axis_index_groups=same_core)  5.8 us
    all_to_all x1, waiting for transfers between devices, local(): b_mine = lax.all_to_all(chunks, 'band', 0, 0, axis_index_groups=same_core)  5.17 us
    ppermute x1, starting transfers between devices, local(): phi_high = lax.ppermute(orbitals[:, :REACH], 'dom', down)  4.72 us
    all_to_all x1, starting transfers between devices, local(): b_mine = lax.all_to_all(chunks, 'band', 0, 0, axis_index_groups=same_core)  4.39 us
    ppermute x1, starting transfers between devices, local(): got = lax.ppermute(orbitals, 'band', partner)  3.24 us
  transfers between devices with their start and end apart: 10, of which 6 were waited for; matrix products, arithmetic and copies ran while one was open for 5% of the time, Pallas kernels for 9%

profile of v2, /device:TPU:1, one launch (start us, length us, event | category | flops | bytes accessed | tf_op | source)
XLA Modules:
  0.0 66.5 jit_solution(17940705509092718644)
XLA Ops:
  0.0 0.0 copy-start
  0.0 3.2 %collective-permute-start = (f32[8,4,32,128]{3,2,1,0:T(8,128)}, f32[8,4,32,128]{3,2,1,0:T(8,128)S(1)}, u32[]{:S(2)}, u32[]{:S(2)}) collective-permute-start(f32[8,4,32,128]{3,2,1,0:T(8,128)} %phi.1), channel_id=1, source_target_pairs={{0,16},{16,0},{32,48},{48,32},{64,80},{80,64},{96,112},{112,96},{1... | collective-permute-start | bytes 1572872 | tf_op jit(solution)/shard_map/ppermute | solution.py:193
  3.2 1.2 %fusion = (f32[8,3,32,128]{3,2,1,0:T(8,128)S(1)}, f32[8,3,32,128]{3,2,1,0:T(8,128)S(1)}) fusion(f32[8,4,32,128]{3,2,1,0:T(8,128)} %phi.1), kind=kLoop, calls=%fused_computation.2 | loop fusion | bytes 1572864 | tf_op jit(solution)/shard_map/slice | solution.py:191
  4.4 0.1 collective-permute-start.1
  4.5 0.0 copy-start.1
  4.5 0.6 copy-done.1
  5.2 0.6 dynamic_slice.10
  8.4 0.0 collective-permute-done
  8.4 0.0 copy-done
  8.4 0.7 %dynamic-slice_select_fusion = f32[4,4,32,128]{3,2,1,0:T(8,128)} fusion(f32[8,4,32,128]{3,2,1,0:T(8,128)S(1)} %collective-permute-done, s32[]{:T(128)S(6)} %select_n.47, f32[8,4,32,128]{3,2,1,0:T(8,128)S(1)} %copy-done, pred[]{:T(512)S(6)} %eq.7), kind=kLoop, calls=%fused_computation | loop fusion | flops 65536 | bytes 786437 | tf_op jit(solution)/shard_map/jit(_where)/select_n | solution.py:196
  9.2 5.8 %all-to-all-start = ((f32[8,2,32,128]{3,2,1,0:T(8,128)}), f32[8,2,32,128]{3,2,1,0:T(8,128)S(1)}, u32[]{:S(2)}, u32[]{:S(2)}) async-start(f32[8,2,32,128]{3,2,1,0:T(8,128)} %bitcast.1), calls=%async_computation | async-start | bytes 524288 | tf_op jit(solution)/shard_map/all_to_all | solution.py:199
  15.0 4.7 %collective-permute-start.2 = (f32[8,3,32,128]{3,2,1,0:T(8,128)S(1)}, f32[8,3,32,128]{3,2,1,0:T(8,128)S(1)}, u32[]{:S(2)}, u32[]{:S(2)}) collective-permute-start(f32[8,3,32,128]{3,2,1,0:T(8,128)S(1)} %get-tuple-element.19), channel_id=1, source_target_pairs={{1,0},{2,1},{3,2},{4,3},{5,4},{6,5},{7,6},{8,7},{9,8},{10,9},{11,1... | collective-permute-start | bytes 1179656 | tf_op jit(solution)/shard_map/ppermute | solution.py:191
  19.7 2.9 %all-to-all-done = f32[8,2,32,128]{3,2,1,0:T(8,128)S(1)} async-done(((f32[8,2,32,128]{3,2,1,0:T(8,128)}), f32[8,2,32,128]{3,2,1,0:T(8,128)S(1)}, u32[]{:S(2)}, u32[]{:S(2)}) %all-to-all-start) | async-done | bytes 262176 | tf_op jit(solution)/shard_map/all_to_all | solution.py:199
  22.6 0.0 collective-permute-done.1.phi_low
  22.6 0.7 %broadcast_in_dim.8 = f32[8,2,32,128]{3,2,1,0:T(8,128)} broadcast(f32[2,32,128]{2,1,0:T(8,128)S(1)} %bitcast.8), dimensions={1,2,3} | broadcast | bytes 294912 | tf_op jit(solution)/shard_map/broadcast_in_dim | solution.py:202
  23.3 4.4 %all-to-all-start.1 = ((f32[8,2,32,128]{3,2,1,0:T(8,128)}), f32[8,2,32,128]{3,2,1,0:T(8,128)S(1)}, u32[]{:S(2)}, u32[]{:S(2)}) async-start(f32[8,2,32,128]{3,2,1,0:T(8,128)} %broadcast_in_dim.8), calls=%async_computation.1 | async-start | bytes 524288 | tf_op jit(solution)/shard_map/all_to_all | solution.py:203
  27.7 2.4 %collective-permute-done.2.phi_high = f32[8,3,32,128]{3,2,1,0:T(8,128)S(1)} collective-permute-done((f32[8,3,32,128]{3,2,1,0:T(8,128)S(1)}, f32[8,3,32,128]{3,2,1,0:T(8,128)S(1)}, u32[]{:S(2)}, u32[]{:S(2)}) %collective-permute-start.2) | collective-permute-done | bytes 393248 | tf_op jit(solution)/shard_map/ppermute | solution.py:191
  30.1 5.2 %all-to-all-done.1 = f32[8,2,32,128]{3,2,1,0:T(8,128)S(1)} async-done(((f32[8,2,32,128]{3,2,1,0:T(8,128)}), f32[8,2,32,128]{3,2,1,0:T(8,128)S(1)}, u32[]{:S(2)}, u32[]{:S(2)}) %all-to-all-start.1) | async-done | bytes 262176 | tf_op jit(solution)/shard_map/all_to_all | solution.py:203
  35.3 9.5 %collective-permute-start.5 = (f32[4,4,32,128]{3,2,1,0:T(8,128)S(1)}, f32[4,4,32,128]{3,2,1,0:T(8,128)S(1)}, u32[]{:S(2)}, u32[]{:S(2)}) collective-permute-start(f32[4,4,32,128]{3,2,1,0:T(8,128)S(1)} %bitcast.4), channel_id=1, source_target_pairs={{0,16},{16,0},{32,48},{48,32},{64,80},{80,64},{96,112},{112,96},{1... | collective-permute-start | bytes 786440 | tf_op jit(solution)/shard_map/ppermute | solution.py:209
  44.8 0.1 collective-permute-start.4
  44.9 1.5 %collective-permute-start.3 = (f32[4,3,32,128]{3,2,1,0:T(8,128)S(1)}, f32[4,3,32,128]{3,2,1,0:T(8,128)S(1)}, u32[]{:S(2)}, u32[]{:S(2)}) collective-permute-start(f32[4,3,32,128]{3,2,1,0:T(8,128)S(1)} %get-tuple-element.22), channel_id=1, source_target_pairs={{0,1},{1,2},{2,3},{3,4},{4,5},{5,6},{6,7},{7,8},{8,9},{9,10},{10,1... | collective-permute-start | bytes 589832 | tf_op jit(solution)/shard_map/ppermute | solution.py:207
  46.3 0.0 collective-permute-done.5.b_other
  46.3 5.8 %shard_map.28.part = f32[8,4,32,128]{3,2,1,0:T(8,128)S(1)} custom-call(f32[8,4,32,128]{3,2,1,0:T(8,128)S(1)} %copy-done, f32[4,4,32,128]{3,2,1,0:T(8,128)S(1)} %bitcast.6, f32[4,4,32,128]{3,2,1,0:T(8,128)S(1)} %collective-permute-done.5.b_other), custom_call_target="tpu_custom_call" | custom-call | tf_op jit(solution)/shard_map/pallas_call | solution.py:164
  52.1 0.0 collective-permute-done.4.high_mine
  52.1 9.4 %collective-permute-done.3.low_mine = f32[4,3,32,128]{3,2,1,0:T(8,128)S(1)} collective-permute-done((f32[4,3,32,128]{3,2,1,0:T(8,128)S(1)}, f32[4,3,32,128]{3,2,1,0:T(8,128)S(1)}, u32[]{:S(2)}, u32[]{:S(2)}) %collective-permute-start.3) | collective-permute-done | bytes 196640 | tf_op jit(solution)/shard_map/ppermute | solution.py:207
  61.5 0.8 %collective-permute-start.6 = (f32[4,3,32,128]{3,2,1,0:T(8,128)S(1)}, f32[4,3,32,128]{3,2,1,0:T(8,128)S(1)}, u32[]{:S(2)}, u32[]{:S(2)}) collective-permute-start(f32[4,3,32,128]{3,2,1,0:T(8,128)S(1)} %collective-permute-done.3.low_mine), channel_id=1, source_target_pairs={{0,16},{16,0},{32,48},{48,32},{64,80},{80,64},{96,112},{112,96},{1... | collective-permute-start | bytes 589832 | tf_op jit(solution)/shard_map/ppermute | solution.py:213
  62.3 0.0 collective-permute-start.7
  62.3 1.1 %collective-permute-done.6.low_other = f32[4,3,32,128]{3,2,1,0:T(8,128)S(1)} collective-permute-done((f32[4,3,32,128]{3,2,1,0:T(8,128)S(1)}, f32[4,3,32,128]{3,2,1,0:T(8,128)S(1)}, u32[]{:S(2)}, u32[]{:S(2)}) %collective-permute-start.6) | collective-permute-done | bytes 196640 | tf_op jit(solution)/shard_map/ppermute | solution.py:213
  63.4 0.4 collective-permute-done.7.high_other
  63.8 2.7 %shard_map.29 = f32[8,4,32,128]{3,2,1,0:T(8,128)} custom-call(f32[8,4,32,128]{3,2,1,0:T(8,128)S(1)} %shard_map.28.part, f32[8,3,32,128]{3,2,1,0:T(8,128)S(1)} %collective-permute-done.1.phi_low, f32[8,3,32,128]{3,2,1,0:T(8,128)S(1)} %collective-permute-done.2.phi_high, f32[4,4,32,128]{3,2,1,0:T(8,128)S(1)} %bitcast.7, ...), custom_call_target="tpu_custom_call" | custom-call | tf_op jit(solution)/shard_map/pallas_call | solution.py:164
  (2 shorter events, 0.0 us)
Async XLA Ops:
  0.0 8.4 %copy-start = (f32[8,4,32,128]{3,2,1,0:T(8,128)S(1)}, f32[8,4,32,128]{3,2,1,0:T(8,128)}, u32[]{:S(2)}) copy-start(f32[8,4,32,128]{3,2,1,0:T(8,128)} %phi.1) | copy-start | bytes 1572868
  0.0 8.4 %collective-permute-start = (f32[8,4,32,128]{3,2,1,0:T(8,128)}, f32[8,4,32,128]{3,2,1,0:T(8,128)S(1)}, u32[]{:S(2)}, u32[]{:S(2)}) collective-permute-start(f32[8,4,32,128]{3,2,1,0:T(8,128)} %phi.1), channel_id=1, source_target_pairs={{0,16},{16,0},{32,48},{48,32},{64,80},{80,64},{96,112},{112,96},{1... | collective-permute-start | bytes 1572872 | tf_op jit(solution)/shard_map/ppermute | solution.py:193
  4.4 18.1 %collective-permute-start.1 = (f32[8,3,32,128]{3,2,1,0:T(8,128)S(1)}, f32[8,3,32,128]{3,2,1,0:T(8,128)S(1)}, u32[]{:S(2)}, u32[]{:S(2)}) collective-permute-start(f32[8,3,32,128]{3,2,1,0:T(8,128)S(1)} %get-tuple-element.20), channel_id=1, source_target_pairs={{0,1},{1,2},{2,3},{3,4},{4,5},{5,6},{6,7},{7,8},{8,9},{9,10},{10,1... | collective-permute-start | bytes 1179656 | tf_op jit(solution)/shard_map/ppermute | solution.py:190
  4.5 0.7 copy-start.1
  9.2 13.4 %all-to-all-start = ((f32[8,2,32,128]{3,2,1,0:T(8,128)}), f32[8,2,32,128]{3,2,1,0:T(8,128)S(1)}, u32[]{:S(2)}, u32[]{:S(2)}) async-start(f32[8,2,32,128]{3,2,1,0:T(8,128)} %bitcast.1), calls=%async_computation | async-start | bytes 524288 | tf_op jit(solution)/shard_map/all_to_all | solution.py:199
  15.0 15.1 %collective-permute-start.2 = (f32[8,3,32,128]{3,2,1,0:T(8,128)S(1)}, f32[8,3,32,128]{3,2,1,0:T(8,128)S(1)}, u32[]{:S(2)}, u32[]{:S(2)}) collective-permute-start(f32[8,3,32,128]{3,2,1,0:T(8,128)S(1)} %get-tuple-element.19), channel_id=1, source_target_pairs={{1,0},{2,1},{3,2},{4,3},{5,4},{6,5},{7,6},{8,7},{9,8},{10,9},{11,1... | collective-permute-start | bytes 1179656 | tf_op jit(solution)/shard_map/ppermute | solution.py:191
  23.3 12.0 %all-to-all-start.1 = ((f32[8,2,32,128]{3,2,1,0:T(8,128)}), f32[8,2,32,128]{3,2,1,0:T(8,128)S(1)}, u32[]{:S(2)}, u32[]{:S(2)}) async-start(f32[8,2,32,128]{3,2,1,0:T(8,128)} %broadcast_in_dim.8), calls=%async_computation.1 | async-start | bytes 524288 | tf_op jit(solution)/shard_map/all_to_all | solution.py:203
  35.3 11.1 %collective-permute-start.5 = (f32[4,4,32,128]{3,2,1,0:T(8,128)S(1)}, f32[4,4,32,128]{3,2,1,0:T(8,128)S(1)}, u32[]{:S(2)}, u32[]{:S(2)}) collective-permute-start(f32[4,4,32,128]{3,2,1,0:T(8,128)S(1)} %bitcast.4), channel_id=1, source_target_pairs={{0,16},{16,0},{32,48},{48,32},{64,80},{80,64},{96,112},{112,96},{1... | collective-permute-start | bytes 786440 | tf_op jit(solution)/shard_map/ppermute | solution.py:209
  44.8 7.3 %collective-permute-start.4 = (f32[4,3,32,128]{3,2,1,0:T(8,128)S(1)}, f32[4,3,32,128]{3,2,1,0:T(8,128)S(1)}, u32[]{:S(2)}, u32[]{:S(2)}) collective-permute-start(f32[4,3,32,128]{3,2,1,0:T(8,128)S(1)} %get-tuple-element.21), channel_id=1, source_target_pairs={{1,0},{2,1},{3,2},{4,3},{5,4},{6,5},{7,6},{8,7},{9,8},{10,9},{11,1... | collective-permute-start | bytes 589832 | tf_op jit(solution)/shard_map/ppermute | solution.py:208
  44.9 16.7 %collective-permute-start.3 = (f32[4,3,32,128]{3,2,1,0:T(8,128)S(1)}, f32[4,3,32,128]{3,2,1,0:T(8,128)S(1)}, u32[]{:S(2)}, u32[]{:S(2)}) collective-permute-start(f32[4,3,32,128]{3,2,1,0:T(8,128)S(1)} %get-tuple-element.22), channel_id=1, source_target_pairs={{0,1},{1,2},{2,3},{3,4},{4,5},{5,6},{6,7},{7,8},{8,9},{9,10},{10,1... | collective-permute-start | bytes 589832 | tf_op jit(solution)/shard_map/ppermute | solution.py:207
  61.5 1.9 %collective-permute-start.6 = (f32[4,3,32,128]{3,2,1,0:T(8,128)S(1)}, f32[4,3,32,128]{3,2,1,0:T(8,128)S(1)}, u32[]{:S(2)}, u32[]{:S(2)}) collective-permute-start(f32[4,3,32,128]{3,2,1,0:T(8,128)S(1)} %collective-permute-done.3.low_mine), channel_id=1, source_target_pairs={{0,16},{16,0},{32,48},{48,32},{64,80},{80,64},{96,112},{112,96},{1... | collective-permute-start | bytes 589832 | tf_op jit(solution)/shard_map/ppermute | solution.py:213
  62.3 1.4 %collective-permute-start.7 = (f32[4,3,32,128]{3,2,1,0:T(8,128)S(1)}, f32[4,3,32,128]{3,2,1,0:T(8,128)S(1)}, u32[]{:S(2)}, u32[]{:S(2)}) collective-permute-start(f32[4,3,32,128]{3,2,1,0:T(8,128)S(1)} %collective-permute-done.4.high_mine), channel_id=1, source_target_pairs={{0,16},{16,0},{32,48},{48,32},{64,80},{80,64},{96,112},{112,96},{1... | collective-permute-start | bytes 589832 | tf_op jit(solution)/shard_map/ppermute | solution.py:214

commit v3 on v2

--- a/solution.py
+++ b/solution.py
@@ -175,34 +175,60 @@
     )(*args)
 
 
+def choose_kernel(order, own, got, chosen, sem):
+    core = lax.axis_index("band") & 1
+    block = order[core]
+    at = (block & 1) * BLOCK
+
+    def copy(source):
+        move = pltpu.make_async_copy(source.at[pl.ds(at, BLOCK)], chosen, sem)
+        move.start()
+        move.wait()
+
+    pl.when((block >> 1) & 1 == core)(lambda: copy(own))
+    pl.when((block >> 1) & 1 != core)(lambda: copy(got))
+
+
+def choose(order, own, got):
+    return pl.pallas_call(
+        choose_kernel,
+        out_shape=jax.ShapeDtypeStruct((BLOCK,) + own.shape[1:], own.dtype),
+        in_specs=[
+            pl.BlockSpec(memory_space=pltpu.SMEM),
+            pl.BlockSpec(memory_space=pl.ANY),
+            pl.BlockSpec(memory_space=pl.ANY),
+        ],
+        out_specs=pl.BlockSpec(memory_space=pltpu.VMEM),
+        scratch_shapes=[pltpu.SemaphoreType.DMA],
+    )(order, own, got)
+
+
 def local(orbitals, owner_order):
     count, nx, ny, nz = orbitals.shape
-    halves = LOCAL // BLOCK
-    band = lax.axis_index("band")
     bands, doms = lax.axis_size("band"), lax.axis_size("dom")
-    chips = bands // 2
-    core = band % 2
-    same_core = [[2 * chip + c for chip in range(chips)] for c in range(2)]
+    rows = [[first + 2 * y for y in range(4)] for first in (0, 1, 8, 9)]
     partner = [(i, i ^ 1) for i in range(bands)]
+    across = [(i, i ^ 8) for i in range(bands)]
     up = [(i, (i + 1) % doms) for i in range(doms)]
     down = [((i + 1) % doms, i) for i in range(doms)]
 
+    got = lax.ppermute(orbitals, "band", partner)
+    chosen = choose(owner_order, orbitals, got)
+    chosen, orbitals, owner_order = lax.optimization_barrier((chosen, orbitals, owner_order))
+
     phi_low = lax.ppermute(orbitals[:, nx - REACH :], "dom", up)
     phi_high = lax.ppermute(orbitals[:, :REACH], "dom", down)
 
-    got = lax.ppermute(orbitals, "band", partner)
-    mine = owner_order[core]
-    owner = mine // halves
-    chosen = jnp.where(owner % 2 == core, orbitals, got)
-    chosen = lax.dynamic_slice_in_dim(chosen, mine % halves * BLOCK, BLOCK, 0)
-    chunks = chosen.reshape(chips, BLOCK * nx // chips, ny, nz)
-    chunks = lax.all_to_all(chunks, "band", 0, 0, axis_index_groups=same_core)
-    chunk = lax.dynamic_index_in_dim(chunks, owner // 2, 0, keepdims=True)
+    band = lax.axis_index("band")
+    block_id = lax.dynamic_slice_in_dim(owner_order, band & 1, 1)[0]
+    chunks = lax.all_to_all(chosen, "band", 0, 0, axis_index_groups=rows, tiled=True)
+    chunk = lax.dynamic_slice_in_dim(chunks, (block_id >> 2) & 3, 1, 0)
     chunk, phi_low = lax.optimization_barrier((chunk, phi_low))
+    crossed = lax.ppermute(chunk, "band", across)
+    chunk = jnp.where(block_id >> 4 == band >> 3, chunk, crossed)
     chunks = jnp.broadcast_to(chunk, chunks.shape)
-    b_mine = lax.all_to_all(chunks, "band", 0, 0, axis_index_groups=same_core)
+    b_mine = lax.all_to_all(chunks, "band", 0, 0, axis_index_groups=rows, tiled=True)
     b_mine, phi_high = lax.optimization_barrier((b_mine, phi_high))
-    b_mine = b_mine.reshape(BLOCK, nx, ny, nz)
 
     low_mine = lax.ppermute(b_mine[:, nx - REACH :], "dom", up)
     high_mine = lax.ppermute(b_mine[:, :REACH], "dom", down)

time: 66.8 us -> 63.3 us (0.948)
  starting transfers between devices: 30 us -> 17.4 us
  waiting for transfers between devices: 21.3 us -> 30.5 us
  Pallas kernels: 8.47 us -> 10.8 us
  between operations: 2.74 us -> 1.39 us
  other arithmetic: 0.74 us -> 0.01 us
    ppermute x1, waiting for transfers between devices: 9.45 us -> 0.01 us  [local(): low_mine = lax.ppermute(b_mine[:, nx - REACH:], 'dom', up)]
    ppermute x0 -> x1, waiting for transfers between devices: none -> 9.43 us  [local(): crossed = lax.ppermute(chunk, 'band', across)]
    ppermute x1, starting transfers between devices: 9.47 us -> 1.63 us  [local(): b_other = lax.ppermute(b_mine, 'band', partner)]
    ppermute x1, waiting for transfers between devices: 0.01 us -> 4.46 us  [local(): phi_low = lax.ppermute(orbitals[:, nx - REACH:], 'dom', up)]
    ppermute x1, starting transfers between devices: 4.72 us -> 0.61 us  [local(): phi_high = lax.ppermute(orbitals[:, :REACH], 'dom', down)]
    ppermute x1, waiting for transfers between devices: 0.01 us -> 3.52 us  [local(): high_mine = lax.ppermute(b_mine[:, :REACH], 'dom', down)]
    all_to_all x2, starting transfers between devices: 10.2 us -> 7.05 us  [the longest x1 3.65 us: local(): lax.all_to_all(chosen, 'band', 0, 0, axis_index_groups=rows, tiled=True)]
    ppermute x0 -> x1, starting transfers between devices: none -> 2.45 us  [local(): crossed = lax.ppermute(chunk, 'band', across)]
  transfers between devices with their start and end apart: 10 -> 11, of which waited for: 6 -> 8; matrix products, arithmetic and copies ran while one was open for 5% -> 2% of each run, Pallas kernels for 9% -> 9%
where the time goes in v3:
time: 63.3 us; the launch traced here: 63 us
  waiting for transfers between devices  30.5 us (48%)
  starting transfers between devices  17.4 us (27%)
  Pallas kernels  10.8 us (17%)
  local copies, waits for them, and re-layouts  2.88 us (5%)
  between operations  1.39 us (2%)
    ppermute x1, waiting for transfers between devices, local(): crossed = lax.ppermute(chunk, 'band', across)  9.43 us
    pallas_call x2, Pallas kernels, call(): pl.pallas_call(kernel, out_shape=jax.ShapeDtypeStruct((count, nx, ny, nz)...  8.47 us
    all_to_all x1, waiting for transfers between devices, local(): lax.all_to_all(chunks, 'band', 0, 0, axis_index_groups=rows, tiled=True)  5.95 us
    ppermute x1, waiting for transfers between devices, local(): phi_low = lax.ppermute(orbitals[:, nx - REACH:], 'dom', up)  4.46 us
    all_to_all x1, waiting for transfers between devices, local(): lax.all_to_all(chosen, 'band', 0, 0, axis_index_groups=rows, tiled=True)  3.93 us
    all_to_all x1, starting transfers between devices, local(): lax.all_to_all(chosen, 'band', 0, 0, axis_index_groups=rows, tiled=True)  3.65 us
    ppermute x1, waiting for transfers between devices, local(): high_mine = lax.ppermute(b_mine[:, :REACH], 'dom', down)  3.52 us
    all_to_all x1, starting transfers between devices, local(): lax.all_to_all(chunks, 'band', 0, 0, axis_index_groups=rows, tiled=True)  3.41 us
  transfers between devices with their start and end apart: 11, of which 8 were waited for; matrix products, arithmetic and copies ran while one was open for 2% of the time, Pallas kernels for 9%

profile of v3, /device:TPU:1, one launch (start us, length us, event | category | flops | bytes accessed | tf_op | source)
XLA Modules:
  0.0 63.0 jit_solution(3123645868562244853)
XLA Ops:
  0.0 0.0 copy-start
  0.0 3.2 %collective-permute-start = (f32[8,4,32,128]{3,2,1,0:T(8,128)}, f32[8,4,32,128]{3,2,1,0:T(8,128)S(1)}, u32[]{:S(2)}, u32[]{:S(2)}) collective-permute-start(f32[8,4,32,128]{3,2,1,0:T(8,128)} %phi), channel_id=1, source_target_pairs={{0,16},{16,0},{32,48},{48,32},{64,80},{80,64},{96,112},{112,96},{1... | collective-permute-start | bytes 1572872 | tf_op jit(solution)/shard_map/ppermute | solution.py:215
  3.2 1.7 %collective-permute-done.got = f32[8,4,32,128]{3,2,1,0:T(8,128)S(1)} collective-permute-done((f32[8,4,32,128]{3,2,1,0:T(8,128)}, f32[8,4,32,128]{3,2,1,0:T(8,128)S(1)}, u32[]{:S(2)}, u32[]{:S(2)}) %collective-permute-start) | collective-permute-done | bytes 524320 | tf_op jit(solution)/shard_map/ppermute | solution.py:215
  5.0 0.0 copy-start.1
  5.0 0.8 %copy-done.1 = f32[8,4,32,128]{3,2,1,0:T(8,128)} copy-done((f32[8,4,32,128]{3,2,1,0:T(8,128)}, f32[8,4,32,128]{3,2,1,0:T(8,128)S(1)}, u32[]{:S(2)}) %copy-start.1) | copy-done | bytes 524312
  5.8 2.3 %shard_map.28 = f32[4,4,32,128]{3,2,1,0:T(8,128)} custom-call(s32[32]{0:T(128)} %order.1, f32[8,4,32,128]{3,2,1,0:T(8,128)} %phi, f32[8,4,32,128]{3,2,1,0:T(8,128)} %copy-done.1), custom_call_target="tpu_custom_call" | custom-call | tf_op jit(solution)/shard_map/pallas_call | solution.py:193
  8.1 0.0 copy-done
  8.1 0.1 fusion
  8.2 0.1 collective-permute-start.1
  8.3 3.6 %all-to-all-start = ((f32[4,4,32,128]{3,2,1,0:T(8,128)}), f32[4,4,32,128]{3,2,1,0:T(8,128)S(1)}, u32[]{:S(2)}, u32[]{:S(2)}) async-start(f32[4,4,32,128]{3,2,1,0:T(8,128)} %shard_map.28), calls=%async_computation | async-start | bytes 524288 | tf_op jit(solution)/shard_map/all_to_all | solution.py:224
  12.0 0.0 copy-start.2
  12.0 0.7 %copy-done.2 = s32[32]{0:T(128)S(1)} copy-done((s32[32]{0:T(128)S(1)}, s32[32]{0:T(128)}, u32[]{:S(2)}) %copy-start.2) | copy-done | bytes 152
  12.6 0.6 dynamic_slice.6
  13.8 3.9 %all-to-all-done = f32[4,4,32,128]{3,2,1,0:T(8,128)S(1)} async-done(((f32[4,4,32,128]{3,2,1,0:T(8,128)}), f32[4,4,32,128]{3,2,1,0:T(8,128)S(1)}, u32[]{:S(2)}, u32[]{:S(2)}) %all-to-all-start) | async-done | bytes 262176 | tf_op jit(solution)/shard_map/all_to_all | solution.py:224
  17.8 4.5 %collective-permute-done.1.phi_low = f32[8,3,32,128]{3,2,1,0:T(8,128)S(1)} collective-permute-done((f32[8,3,32,128]{3,2,1,0:T(8,128)S(1)}, f32[8,3,32,128]{3,2,1,0:T(8,128)S(1)}, u32[]{:S(2)}, u32[]{:S(2)}) %collective-permute-start.1) | collective-permute-done | bytes 393248 | tf_op jit(solution)/shard_map/ppermute | solution.py:219
  22.2 2.5 %collective-permute-start.2 = (f32[1,4,32,128]{3,2,1,0:T(8,128)S(1)}, f32[1,4,32,128]{3,2,1,0:T(8,128)S(1)}, u32[]{:S(2)}, u32[]{:S(2)}) collective-permute-start(f32[1,4,32,128]{3,2,1,0:T(8,128)S(1)} %constant_dynamic-slice_fusion), channel_id=1, source_target_pairs={{0,128},{16,144},{32,160},{48,176},{64,192},{80,208},{96,224},{112... | collective-permute-start | bytes 196616 | tf_op jit(solution)/shard_map/ppermute | solution.py:227
  25.4 0.6 collective-permute-start.3
  26.0 9.4 %collective-permute-done.2 = f32[1,4,32,128]{3,2,1,0:T(8,128)S(1)} collective-permute-done((f32[1,4,32,128]{3,2,1,0:T(8,128)S(1)}, f32[1,4,32,128]{3,2,1,0:T(8,128)S(1)}, u32[]{:S(2)}, u32[]{:S(2)}) %collective-permute-start.2) | collective-permute-done | bytes 65568 | tf_op jit(solution)/shard_map/ppermute | solution.py:227
  35.4 0.7 %broadcast_in_dim.8 = f32[4,4,32,128]{3,2,1,0:T(8,128)} broadcast(f32[4,32,128]{2,1,0:T(8,128)S(1)} %select_bitcast_fusion), dimensions={1,2,3} | broadcast | bytes 327680 | tf_op jit(solution)/shard_map/broadcast_in_dim | solution.py:229
  36.1 3.4 %all-to-all-start.1 = ((f32[4,4,32,128]{3,2,1,0:T(8,128)}), f32[4,4,32,128]{3,2,1,0:T(8,128)S(1)}, u32[]{:S(2)}, u32[]{:S(2)}) async-start(f32[4,4,32,128]{3,2,1,0:T(8,128)} %broadcast_in_dim.8), calls=%async_computation.1 | async-start | bytes 524288 | tf_op jit(solution)/shard_map/all_to_all | solution.py:230
  39.6 0.0 collective-permute-done.3.phi_high
  39.6 5.9 %all-to-all-done.1.b_mine = f32[4,4,32,128]{3,2,1,0:T(8,128)S(1)} async-done(((f32[4,4,32,128]{3,2,1,0:T(8,128)}), f32[4,4,32,128]{3,2,1,0:T(8,128)S(1)}, u32[]{:S(2)}, u32[]{:S(2)}) %all-to-all-start.1) | async-done | bytes 262176 | tf_op jit(solution)/shard_map/all_to_all | solution.py:230
  45.5 1.6 %collective-permute-start.6 = (f32[4,4,32,128]{3,2,1,0:T(8,128)S(1)}, f32[4,4,32,128]{3,2,1,0:T(8,128)S(1)}, u32[]{:S(2)}, u32[]{:S(2)}) collective-permute-start(f32[4,4,32,128]{3,2,1,0:T(8,128)S(1)} %all-to-all-done.1.b_mine), channel_id=1, source_target_pairs={{0,16},{16,0},{32,48},{48,32},{64,80},{80,64},{96,112},{112,96},{1... | collective-permute-start | bytes 786440 | tf_op jit(solution)/shard_map/ppermute | solution.py:235
  47.2 0.1 collective-permute-start.5
  47.3 1.5 %collective-permute-start.4 = (f32[4,3,32,128]{3,2,1,0:T(8,128)S(1)}, f32[4,3,32,128]{3,2,1,0:T(8,128)S(1)}, u32[]{:S(2)}, u32[]{:S(2)}) collective-permute-start(f32[4,3,32,128]{3,2,1,0:T(8,128)S(1)} %get-tuple-element.28), channel_id=1, source_target_pairs={{0,1},{1,2},{2,3},{3,4},{4,5},{5,6},{6,7},{7,8},{8,9},{9,10},{10,1... | collective-permute-start | bytes 589832 | tf_op jit(solution)/shard_map/ppermute | solution.py:233
  48.7 0.0 collective-permute-done.6.b_other
  48.7 5.8 %shard_map.29.part = f32[8,4,32,128]{3,2,1,0:T(8,128)S(1)} custom-call(f32[8,4,32,128]{3,2,1,0:T(8,128)S(1)} %copy-done, f32[4,4,32,128]{3,2,1,0:T(8,128)S(1)} %all-to-all-done.1.b_mine, f32[4,4,32,128]{3,2,1,0:T(8,128)S(1)} %collective-permute-done.6.b_other), custom_call_target="tpu_custom_call" | custom-call | tf_op jit(solution)/shard_map/pallas_call | solution.py:164
  54.5 3.5 %collective-permute-done.5.high_mine = f32[4,3,32,128]{3,2,1,0:T(8,128)S(1)} collective-permute-done((f32[4,3,32,128]{3,2,1,0:T(8,128)S(1)}, f32[4,3,32,128]{3,2,1,0:T(8,128)S(1)}, u32[]{:S(2)}, u32[]{:S(2)}) %collective-permute-start.5) | collective-permute-done | bytes 196640 | tf_op jit(solution)/shard_map/ppermute | solution.py:234
  58.0 0.0 collective-permute-done.4.low_mine
  58.0 0.8 %collective-permute-start.7 = (f32[4,3,32,128]{3,2,1,0:T(8,128)S(1)}, f32[4,3,32,128]{3,2,1,0:T(8,128)S(1)}, u32[]{:S(2)}, u32[]{:S(2)}) collective-permute-start(f32[4,3,32,128]{3,2,1,0:T(8,128)S(1)} %collective-permute-done.4.low_mine), channel_id=1, source_target_pairs={{0,16},{16,0},{32,48},{48,32},{64,80},{80,64},{96,112},{112,96},{1... | collective-permute-start | bytes 589832 | tf_op jit(solution)/shard_map/ppermute | solution.py:239
  58.8 0.0 collective-permute-start.8
  58.8 1.1 %collective-permute-done.7.low_other = f32[4,3,32,128]{3,2,1,0:T(8,128)S(1)} collective-permute-done((f32[4,3,32,128]{3,2,1,0:T(8,128)S(1)}, f32[4,3,32,128]{3,2,1,0:T(8,128)S(1)}, u32[]{:S(2)}, u32[]{:S(2)}) %collective-permute-start.7) | collective-permute-done | bytes 196640 | tf_op jit(solution)/shard_map/ppermute | solution.py:239
  59.9 0.4 collective-permute-done.8.high_other
  60.2 2.7 %shard_map.30 = f32[8,4,32,128]{3,2,1,0:T(8,128)} custom-call(f32[8,4,32,128]{3,2,1,0:T(8,128)S(1)} %shard_map.29.part, f32[8,3,32,128]{3,2,1,0:T(8,128)S(1)} %collective-permute-done.1.phi_low, f32[8,3,32,128]{3,2,1,0:T(8,128)S(1)} %collective-permute-done.3.phi_high, f32[4,4,32,128]{3,2,1,0:T(8,128)S(1)} %all-to-all-done.1.b_mine, ...), custom_call_target="tpu_custom_call" | custom-call | tf_op jit(solution)/shard_map/pallas_call | solution.py:164
  (3 shorter events, 0.0 us)
Async XLA Ops:
  0.0 8.1 %copy-start = (f32[8,4,32,128]{3,2,1,0:T(8,128)S(1)}, f32[8,4,32,128]{3,2,1,0:T(8,128)}, u32[]{:S(2)}) copy-start(f32[8,4,32,128]{3,2,1,0:T(8,128)} %phi) | copy-start | bytes 1572868
  0.0 5.0 %collective-permute-start = (f32[8,4,32,128]{3,2,1,0:T(8,128)}, f32[8,4,32,128]{3,2,1,0:T(8,128)S(1)}, u32[]{:S(2)}, u32[]{:S(2)}) collective-permute-start(f32[8,4,32,128]{3,2,1,0:T(8,128)} %phi), channel_id=1, source_target_pairs={{0,16},{16,0},{32,48},{48,32},{64,80},{80,64},{96,112},{112,96},{1... | collective-permute-start | bytes 1572872 | tf_op jit(solution)/shard_map/ppermute | solution.py:215
  5.0 0.8 %copy-start.1 = (f32[8,4,32,128]{3,2,1,0:T(8,128)}, f32[8,4,32,128]{3,2,1,0:T(8,128)S(1)}, u32[]{:S(2)}) copy-start(f32[8,4,32,128]{3,2,1,0:T(8,128)S(1)} %collective-permute-done.got) | copy-start | bytes 1572868
  8.2 14.0 %collective-permute-start.1 = (f32[8,3,32,128]{3,2,1,0:T(8,128)S(1)}, f32[8,3,32,128]{3,2,1,0:T(8,128)S(1)}, u32[]{:S(2)}, u32[]{:S(2)}) collective-permute-start(f32[8,3,32,128]{3,2,1,0:T(8,128)S(1)} %get-tuple-element.26), channel_id=1, source_target_pairs={{0,1},{1,2},{2,3},{3,4},{4,5},{5,6},{6,7},{7,8},{8,9},{9,10},{10,1... | collective-permute-start | bytes 1179656 | tf_op jit(solution)/shard_map/ppermute | solution.py:219
  8.3 9.5 %all-to-all-start = ((f32[4,4,32,128]{3,2,1,0:T(8,128)}), f32[4,4,32,128]{3,2,1,0:T(8,128)S(1)}, u32[]{:S(2)}, u32[]{:S(2)}) async-start(f32[4,4,32,128]{3,2,1,0:T(8,128)} %shard_map.28), calls=%async_computation | async-start | bytes 524288 | tf_op jit(solution)/shard_map/all_to_all | solution.py:224
  12.0 0.7 %copy-start.2 = (s32[32]{0:T(128)S(1)}, s32[32]{0:T(128)}, u32[]{:S(2)}) copy-start(s32[32]{0:T(128)} %order.1) | copy-start | bytes 388
  22.2 13.1 %collective-permute-start.2 = (f32[1,4,32,128]{3,2,1,0:T(8,128)S(1)}, f32[1,4,32,128]{3,2,1,0:T(8,128)S(1)}, u32[]{:S(2)}, u32[]{:S(2)}) collective-permute-start(f32[1,4,32,128]{3,2,1,0:T(8,128)S(1)} %constant_dynamic-slice_fusion), channel_id=1, source_target_pairs={{0,128},{16,144},{32,160},{48,176},{64,192},{80,208},{96,224},{112... | collective-permute-start | bytes 196616 | tf_op jit(solution)/shard_map/ppermute | solution.py:227
  25.4 14.2 %collective-permute-start.3 = (f32[8,3,32,128]{3,2,1,0:T(8,128)S(1)}, f32[8,3,32,128]{3,2,1,0:T(8,128)S(1)}, u32[]{:S(2)}, u32[]{:S(2)}) collective-permute-start(f32[8,3,32,128]{3,2,1,0:T(8,128)S(1)} %get-tuple-element.25), channel_id=1, source_target_pairs={{1,0},{2,1},{3,2},{4,3},{5,4},{6,5},{7,6},{8,7},{9,8},{10,9},{11,1... | collective-permute-start | bytes 1179656 | tf_op jit(solution)/shard_map/ppermute | solution.py:220
  36.1 9.4 %all-to-all-start.1 = ((f32[4,4,32,128]{3,2,1,0:T(8,128)}), f32[4,4,32,128]{3,2,1,0:T(8,128)S(1)}, u32[]{:S(2)}, u32[]{:S(2)}) async-start(f32[4,4,32,128]{3,2,1,0:T(8,128)} %broadcast_in_dim.8), calls=%async_computation.1 | async-start | bytes 524288 | tf_op jit(solution)/shard_map/all_to_all | solution.py:230
  45.5 3.2 %collective-permute-start.6 = (f32[4,4,32,128]{3,2,1,0:T(8,128)S(1)}, f32[4,4,32,128]{3,2,1,0:T(8,128)S(1)}, u32[]{:S(2)}, u32[]{:S(2)}) collective-permute-start(f32[4,4,32,128]{3,2,1,0:T(8,128)S(1)} %all-to-all-done.1.b_mine), channel_id=1, source_target_pairs={{0,16},{16,0},{32,48},{48,32},{64,80},{80,64},{96,112},{112,96},{1... | collective-permute-start | bytes 786440 | tf_op jit(solution)/shard_map/ppermute | solution.py:235
  47.2 10.8 %collective-permute-start.5 = (f32[4,3,32,128]{3,2,1,0:T(8,128)S(1)}, f32[4,3,32,128]{3,2,1,0:T(8,128)S(1)}, u32[]{:S(2)}, u32[]{:S(2)}) collective-permute-start(f32[4,3,32,128]{3,2,1,0:T(8,128)S(1)} %get-tuple-element.27), channel_id=1, source_target_pairs={{1,0},{2,1},{3,2},{4,3},{5,4},{6,5},{7,6},{8,7},{9,8},{10,9},{11,1... | collective-permute-start | bytes 589832 | tf_op jit(solution)/shard_map/ppermute | solution.py:234
  47.3 10.7 %collective-permute-start.4 = (f32[4,3,32,128]{3,2,1,0:T(8,128)S(1)}, f32[4,3,32,128]{3,2,1,0:T(8,128)S(1)}, u32[]{:S(2)}, u32[]{:S(2)}) collective-permute-start(f32[4,3,32,128]{3,2,1,0:T(8,128)S(1)} %get-tuple-element.28), channel_id=1, source_target_pairs={{0,1},{1,2},{2,3},{3,4},{4,5},{5,6},{6,7},{7,8},{8,9},{9,10},{10,1... | collective-permute-start | bytes 589832 | tf_op jit(solution)/shard_map/ppermute | solution.py:233
  58.0 1.9 %collective-permute-start.7 = (f32[4,3,32,128]{3,2,1,0:T(8,128)S(1)}, f32[4,3,32,128]{3,2,1,0:T(8,128)S(1)}, u32[]{:S(2)}, u32[]{:S(2)}) collective-permute-start(f32[4,3,32,128]{3,2,1,0:T(8,128)S(1)} %collective-permute-done.4.low_mine), channel_id=1, source_target_pairs={{0,16},{16,0},{32,48},{48,32},{64,80},{80,64},{96,112},{112,96},{1... | collective-permute-start | bytes 589832 | tf_op jit(solution)/shard_map/ppermute | solution.py:239
  58.8 1.4 %collective-permute-start.8 = (f32[4,3,32,128]{3,2,1,0:T(8,128)S(1)}, f32[4,3,32,128]{3,2,1,0:T(8,128)S(1)}, u32[]{:S(2)}, u32[]{:S(2)}) collective-permute-start(f32[4,3,32,128]{3,2,1,0:T(8,128)S(1)} %collective-permute-done.5.high_mine), channel_id=1, source_target_pairs={{0,16},{16,0},{32,48},{48,32},{64,80},{80,64},{96,112},{112,96},{1... | collective-permute-start | bytes 589832 | tf_op jit(solution)/shard_map/ppermute | solution.py:240

commit v4 on v2

--- a/solution.py
+++ b/solution.py
@@ -177,38 +177,56 @@
 
 def local(orbitals, owner_order):
     count, nx, ny, nz = orbitals.shape
-    halves = LOCAL // BLOCK
-    band = lax.axis_index("band")
     bands, doms = lax.axis_size("band"), lax.axis_size("dom")
-    chips = bands // 2
-    core = band % 2
-    same_core = [[2 * chip + c for chip in range(chips)] for c in range(2)]
     partner = [(i, i ^ 1) for i in range(bands)]
+    across = [(i, i ^ 8) for i in range(bands)]
     up = [(i, (i + 1) % doms) for i in range(doms)]
     down = [((i + 1) % doms, i) for i in range(doms)]
 
-    phi_low = lax.ppermute(orbitals[:, nx - REACH :], "dom", up)
-    phi_high = lax.ppermute(orbitals[:, :REACH], "dom", down)
+    def along_y(step):
+        return [(i, i // 8 * 8 + (i + 2 * step) % 8) for i in range(bands)]
+
+    pair = lax.ppermute(orbitals, "dom", [(i, i ^ 1) for i in range(doms)])
+    onward = [(i, (i + 2 - 4 * (i % 2)) % doms) for i in range(doms)]
+    even = lax.axis_index("dom") & 1 == 0
 
     got = lax.ppermute(orbitals, "band", partner)
-    mine = owner_order[core]
-    owner = mine // halves
-    chosen = jnp.where(owner % 2 == core, orbitals, got)
-    chosen = lax.dynamic_slice_in_dim(chosen, mine % halves * BLOCK, BLOCK, 0)
-    chunks = chosen.reshape(chips, BLOCK * nx // chips, ny, nz)
-    chunks = lax.all_to_all(chunks, "band", 0, 0, axis_index_groups=same_core)
-    chunk = lax.dynamic_index_in_dim(chunks, owner // 2, 0, keepdims=True)
-    chunk, phi_low = lax.optimization_barrier((chunk, phi_low))
-    chunks = jnp.broadcast_to(chunk, chunks.shape)
-    b_mine = lax.all_to_all(chunks, "band", 0, 0, axis_index_groups=same_core)
-    b_mine, phi_high = lax.optimization_barrier((b_mine, phi_high))
-    b_mine = b_mine.reshape(BLOCK, nx, ny, nz)
-
+    band = lax.axis_index("band")
+    core = band & 1
+    block_id = jnp.where(core == 0, owner_order[0], owner_order[1])
+    here = (block_id >> 1) & 1 == core
+    chosen = jnp.where(
+        block_id & 1 == 0,
+        jnp.where(here, orbitals[:BLOCK], got[:BLOCK]),
+        jnp.where(here, orbitals[BLOCK:], got[BLOCK:]),
+    )
+
+    below = lax.ppermute(chosen, "band", along_y(1))
+    above = lax.ppermute(chosen, "band", along_y(-1))
+    opposite = lax.ppermute(chosen, "band", along_y(2))
+    ahead = ((block_id >> 2) - (band >> 1)) & 3
+    chosen, pair = lax.optimization_barrier((chosen, pair))
+    chosen = lax.optimization_barrier(jnp.where(ahead == 0, chosen, 0.0))
+    picked = jnp.where(
+        ahead < 2, jnp.where(ahead == 0, chosen, above), jnp.where(ahead == 2, opposite, below)
+    )
+    after, before = pair[:, nx - REACH :], pair[:, :REACH]
+    far = lax.ppermute(jnp.where(even, after, before), "dom", onward)
+    crossed = lax.ppermute(picked, "band", across)
+    picked, far = lax.optimization_barrier((picked, far))
+    valid = block_id >> 4 == band >> 3
+    picked = lax.optimization_barrier(jnp.where(valid, picked, 0.0))
+    b_mine = jnp.where(valid, picked, crossed)
+
+    phi_low = jnp.where(even, far, after)
+    phi_high = jnp.where(even, before, far)
     low_mine = lax.ppermute(b_mine[:, nx - REACH :], "dom", up)
     high_mine = lax.ppermute(b_mine[:, :REACH], "dom", down)
     b_other = lax.ppermute(b_mine, "band", partner)
     part = call(inner_kernel, count, nx, ny, nz, nx, 2 * REACH, (orbitals, b_mine, b_other))
-    low_mine, high_mine, part = lax.optimization_barrier((low_mine, high_mine, part))
+    low_mine, high_mine, part, phi_low, phi_high = lax.optimization_barrier(
+        (low_mine, high_mine, part, phi_low, phi_high)
+    )
 
     low_other = lax.ppermute(low_mine, "band", partner)
     high_other = lax.ppermute(high_mine, "band", partner)

time: 66.8 us -> 52.1 us (0.78)
  starting transfers between devices: 30 us -> 19.3 us
  waiting for transfers between devices: 21.3 us -> 19.2 us
  between operations: 2.74 us -> 1.42 us
  local copies, waits for them, and re-layouts: 3.17 us -> 2.2 us
  other arithmetic: 0.74 us -> 1.41 us
    ppermute x2 -> x6, waiting for transfers between devices: 2.42 us -> 16.3 us  [the longest x1 5.54 us: local(): pair = lax.ppermute(orbitals, 'dom', [(i, i ^ 1) for i in range(doms)])]
    all_to_all x2 -> x0, starting transfers between devices: 10.2 us -> none  [the longest x1 5.8 us: local(): chunks = lax.all_to_all(chunks, 'band', 0, 0, axis_index_groups=same_core)]
    all_to_all x2 -> x0, waiting for transfers between devices: 8.03 us -> none  [the longest x1 5.17 us: local(): b_mine = lax.all_to_all(chunks, 'band', 0, 0, axis_index_groups=same_core)]
    ppermute x1, waiting for transfers between devices: 9.45 us -> 1.51 us  [local(): low_mine = lax.ppermute(b_mine[:, nx - REACH:], 'dom', up)]
    ppermute x1, starting transfers between devices: 9.47 us -> 2.11 us  [local(): b_other = lax.ppermute(b_mine, 'band', partner)]
    ppermute x1, starting transfers between devices: 0.08 us -> 5.62 us  [local(): high_mine = lax.ppermute(b_mine[:, :REACH], 'dom', down)]
    ppermute x2 -> x6, starting transfers between devices: 4.8 us -> 7.16 us  [the longest x1 2.62 us: local(): opposite = lax.ppermute(chosen, 'band', along_y(2))]
    ppermute x1, starting transfers between devices: 1.45 us -> 0.01 us  [local(): low_mine = lax.ppermute(b_mine[:, nx - REACH:], 'dom', up)]
  transfers between devices with their start and end apart: 10 -> 12, of which waited for: 6 -> 7; matrix products, arithmetic and copies ran while one was open for 5% -> 4% of each run, Pallas kernels for 9% -> 11%
where the time goes in v4:
time: 52.1 us; the launch traced here: 52 us
  starting transfers between devices  19.3 us (37%)
  waiting for transfers between devices  19.2 us (37%)
  Pallas kernels  8.46 us (16%)
  local copies, waits for them, and re-layouts  2.2 us (4%)
  between operations  1.42 us (3%)
  other arithmetic  1.41 us (3%)
    pallas_call x2, Pallas kernels, call(): pl.pallas_call(kernel, out_shape=jax.ShapeDtypeStruct((count, nx, ny, nz)...  8.46 us
    ppermute x1, starting transfers between devices, local(): high_mine = lax.ppermute(b_mine[:, :REACH], 'dom', down)  5.62 us
    ppermute x1, waiting for transfers between devices, local(): pair = lax.ppermute(orbitals, 'dom', [(i, i ^ 1) for i in range(doms)])  5.54 us
    ppermute x1, waiting for transfers between devices, local(): opposite = lax.ppermute(chosen, 'band', along_y(2))  4.98 us
    ppermute x1, waiting for transfers between devices, local(): far = lax.ppermute(jnp.where(even, after, before), 'dom', onward)  4.89 us
    ppermute x1, starting transfers between devices, local(): got = lax.ppermute(orbitals, 'band', partner)  3.24 us
    ppermute x1, starting transfers between devices, local(): opposite = lax.ppermute(chosen, 'band', along_y(2))  2.62 us
    ppermute x1, starting transfers between devices, local(): crossed = lax.ppermute(picked, 'band', across)  2.54 us
  transfers between devices with their start and end apart: 12, of which 7 were waited for; matrix products, arithmetic and copies ran while one was open for 4% of the time, Pallas kernels for 11%

profile of v4, /device:TPU:1, one launch (start us, length us, event | category | flops | bytes accessed | tf_op | source)
XLA Modules:
  0.0 52.0 jit_solution(13988533990789344952)
XLA Ops:
  0.0 3.2 %collective-permute-start = (f32[8,4,32,128]{3,2,1,0:T(8,128)}, f32[8,4,32,128]{3,2,1,0:T(8,128)S(1)}, u32[]{:S(2)}, u32[]{:S(2)}) collective-permute-start(f32[8,4,32,128]{3,2,1,0:T(8,128)} %phi.1), channel_id=1, source_target_pairs={{0,16},{16,0},{32,48},{48,32},{64,80},{80,64},{96,112},{112,96},{1... | collective-permute-start | bytes 1572872 | tf_op jit(solution)/shard_map/ppermute | solution.py:193
  3.2 0.0 collective-permute-start.1
  3.2 0.0 copy-start.1
  3.2 0.7 %copy-done.1 = s32[32]{0:T(128)S(1)} copy-done((s32[32]{0:T(128)S(1)}, s32[32]{0:T(128)}, u32[]{:S(2)}) %copy-start.1) | copy-done | bytes 152
  3.9 0.6 %fusion.2 = (s32[1]{0:T(128)}, s32[1]{0:T(128)}) fusion(s32[32]{0:T(128)S(1)} %copy-done.1), kind=kLoop, calls=%fused_computation.11 | loop fusion | bytes 16 | tf_op jit(solution)/shard_map/slice | solution.py:196
  5.8 0.0 collective-permute-done
  5.8 1.1 %fusion = f32[4,4,32,128]{3,2,1,0:T(8,128)S(1)} fusion(f32[8,4,32,128]{3,2,1,0:T(8,128)S(1)} %collective-permute-done, f32[8,4,32,128]{3,2,1,0:T(8,128)} %phi.1, pred[]{:T(512)S(6)} %eq.26, pred[]{:T(512)S(6)} %eq.25), kind=kLoop, calls=%fused_computation.4 | loop fusion | flops 196608 | bytes 1310722 | tf_op jit(solution)/shard_map/jit(_where)/select_n | solution.py:198
  6.9 0.8 %collective-permute-start.4 = (f32[4,4,32,128]{3,2,1,0:T(8,128)S(1)}, f32[4,4,32,128]{3,2,1,0:T(8,128)S(1)}, u32[]{:S(2)}, u32[]{:S(2)}) collective-permute-start(f32[4,4,32,128]{3,2,1,0:T(8,128)S(1)} %fusion), channel_id=1, source_target_pairs={{0,32},{16,48},{32,64},{48,80},{64,96},{80,112},{96,0},{112,16},{1... | collective-permute-start | bytes 786440 | tf_op jit(solution)/shard_map/ppermute | solution.py:204
  7.8 2.6 %collective-permute-start.3 = (f32[4,4,32,128]{3,2,1,0:T(8,128)S(1)}, f32[4,4,32,128]{3,2,1,0:T(8,128)S(1)}, u32[]{:S(2)}, u32[]{:S(2)}) collective-permute-start(f32[4,4,32,128]{3,2,1,0:T(8,128)S(1)} %fusion), channel_id=1, source_target_pairs={{0,64},{16,80},{32,96},{48,112},{64,0},{80,16},{96,32},{112,48},{1... | collective-permute-start | bytes 786440 | tf_op jit(solution)/shard_map/ppermute | solution.py:206
  10.4 1.1 %collective-permute-start.2 = (f32[4,4,32,128]{3,2,1,0:T(8,128)S(1)}, f32[4,4,32,128]{3,2,1,0:T(8,128)S(1)}, u32[]{:S(2)}, u32[]{:S(2)}) collective-permute-start(f32[4,4,32,128]{3,2,1,0:T(8,128)S(1)} %fusion), channel_id=1, source_target_pairs={{0,96},{16,112},{32,0},{48,16},{64,32},{80,48},{96,64},{112,80},{1... | collective-permute-start | bytes 786440 | tf_op jit(solution)/shard_map/ppermute | solution.py:205
  11.5 5.5 %collective-permute-done.1 = f32[8,4,32,128]{3,2,1,0:T(8,128)S(1)} collective-permute-done((f32[8,4,32,128]{3,2,1,0:T(8,128)}, f32[8,4,32,128]{3,2,1,0:T(8,128)S(1)}, u32[]{:S(2)}, u32[]{:S(2)}) %collective-permute-start.1) | collective-permute-done | bytes 524320 | tf_op jit(solution)/shard_map/ppermute | solution.py:189
  17.1 0.1 collective-permute-start.5
  17.2 0.0 collective-permute-done.4
  17.2 5.0 %collective-permute-done.3 = f32[4,4,32,128]{3,2,1,0:T(8,128)S(1)} collective-permute-done((f32[4,4,32,128]{3,2,1,0:T(8,128)S(1)}, f32[4,4,32,128]{3,2,1,0:T(8,128)S(1)}, u32[]{:S(2)}, u32[]{:S(2)}) %collective-permute-start.3) | collective-permute-done | bytes 262176 | tf_op jit(solution)/shard_map/ppermute | solution.py:206
  22.2 0.0 collective-permute-done.2
  22.2 0.1 select_select_fusion
  22.3 2.5 %collective-permute-start.6 = (f32[4,4,32,128]{3,2,1,0:T(8,128)S(1)}, f32[4,4,32,128]{3,2,1,0:T(8,128)S(1)}, u32[]{:S(2)}, u32[]{:S(2)}) collective-permute-start(f32[4,4,32,128]{3,2,1,0:T(8,128)S(1)} %select_select_fusion), channel_id=1, source_target_pairs={{0,128},{16,144},{32,160},{48,176},{64,192},{80,208},{96,224},{112... | collective-permute-start | bytes 786440 | tf_op jit(solution)/shard_map/ppermute | solution.py:215
  24.8 4.9 %collective-permute-done.5 = f32[8,3,32,128]{3,2,1,0:T(8,128)S(1)} collective-permute-done((f32[8,3,32,128]{3,2,1,0:T(8,128)S(1)}, f32[8,3,32,128]{3,2,1,0:T(8,128)S(1)}, u32[]{:S(2)}, u32[]{:S(2)}) %collective-permute-start.5) | collective-permute-done | bytes 393248 | tf_op jit(solution)/shard_map/ppermute | solution.py:214
  29.7 0.8 %collective-permute-done.6 = f32[4,4,32,128]{3,2,1,0:T(8,128)S(1)} collective-permute-done((f32[4,4,32,128]{3,2,1,0:T(8,128)S(1)}, f32[4,4,32,128]{3,2,1,0:T(8,128)S(1)}, u32[]{:S(2)}, u32[]{:S(2)}) %collective-permute-start.6) | collective-permute-done | bytes 262176 | tf_op jit(solution)/shard_map/ppermute | solution.py:215
  30.6 2.1 %collective-permute-start.9 = (f32[4,4,32,128]{3,2,1,0:T(8,128)S(1)}, f32[4,4,32,128]{3,2,1,0:T(8,128)S(1)}, u32[]{:S(2)}, u32[]{:S(2)}) collective-permute-start(f32[4,4,32,128]{3,2,1,0:T(8,128)S(1)} %broadcast_select_fusion.2.b_mine), channel_id=1, source_target_pairs={{0,16},{16,0},{32,48},{48,32},{64,80},{80,64},{96,112},{112,96},{1... | collective-permute-start | bytes 786440 | tf_op jit(solution)/shard_map/ppermute | solution.py:225
  32.7 5.6 %collective-permute-start.8 = (f32[4,3,32,128]{3,2,1,0:T(8,128)S(1)}, f32[4,3,32,128]{3,2,1,0:T(8,128)S(1)}, u32[]{:S(2)}, u32[]{:S(2)}) collective-permute-start(f32[4,3,32,128]{3,2,1,0:T(8,128)S(1)} %get-tuple-element.25), channel_id=1, source_target_pairs={{1,0},{2,1},{3,2},{4,3},{5,4},{6,5},{7,6},{8,7},{9,8},{10,9},{11,1... | collective-permute-start | bytes 589832 | tf_op jit(solution)/shard_map/ppermute | solution.py:224
  38.4 0.0 copy-start
  38.4 0.0 collective-permute-start.7
  38.4 0.1 slice_select_fusion
  38.5 0.0 collective-permute-done.9.b_other
  38.5 0.9 %copy-done = f32[8,4,32,128]{3,2,1,0:T(8,128)S(1)} copy-done((f32[8,4,32,128]{3,2,1,0:T(8,128)S(1)}, f32[8,4,32,128]{3,2,1,0:T(8,128)}, u32[]{:S(2)}) %copy-start) | copy-done | bytes 524312
  39.4 5.7 %shard_map.28.part = f32[8,4,32,128]{3,2,1,0:T(8,128)S(1)} custom-call(f32[8,4,32,128]{3,2,1,0:T(8,128)S(1)} %copy-done, f32[4,4,32,128]{3,2,1,0:T(8,128)S(1)} %broadcast_select_fusion.2.b_mine, f32[4,4,32,128]{3,2,1,0:T(8,128)S(1)} %collective-permute-done.9.b_other), custom_call_target="tpu_custom_call" | custom-call | tf_op jit(solution)/shard_map/pallas_call | solution.py:164
  45.2 0.0 collective-permute-done.8.high_mine
  45.2 1.5 %collective-permute-done.7.low_mine = f32[4,3,32,128]{3,2,1,0:T(8,128)S(1)} collective-permute-done((f32[4,3,32,128]{3,2,1,0:T(8,128)S(1)}, f32[4,3,32,128]{3,2,1,0:T(8,128)S(1)}, u32[]{:S(2)}, u32[]{:S(2)}) %collective-permute-start.7) | collective-permute-done | bytes 196640 | tf_op jit(solution)/shard_map/ppermute | solution.py:223
  46.7 1.1 %collective-permute-start.10 = (f32[4,3,32,128]{3,2,1,0:T(8,128)S(1)}, f32[4,3,32,128]{3,2,1,0:T(8,128)S(1)}, u32[]{:S(2)}, u32[]{:S(2)}) collective-permute-start(f32[4,3,32,128]{3,2,1,0:T(8,128)S(1)} %collective-permute-done.7.low_mine), channel_id=1, source_target_pairs={{0,16},{16,0},{32,48},{48,32},{64,80},{80,64},{96,112},{112,96},{1... | collective-permute-start | bytes 589832 | tf_op jit(solution)/shard_map/ppermute | solution.py:231
  47.8 0.0 collective-permute-start.11
  47.8 1.1 %collective-permute-done.10.low_other = f32[4,3,32,128]{3,2,1,0:T(8,128)S(1)} collective-permute-done((f32[4,3,32,128]{3,2,1,0:T(8,128)S(1)}, f32[4,3,32,128]{3,2,1,0:T(8,128)S(1)}, u32[]{:S(2)}, u32[]{:S(2)}) %collective-permute-start.10) | collective-permute-done | bytes 196640 | tf_op jit(solution)/shard_map/ppermute | solution.py:231
  48.9 0.4 collective-permute-done.11.high_other
  49.2 2.7 %shard_map.29 = f32[8,4,32,128]{3,2,1,0:T(8,128)} custom-call(f32[8,4,32,128]{3,2,1,0:T(8,128)S(1)} %shard_map.28.part, f32[8,3,32,128]{3,2,1,0:T(8,128)S(1)} %get-tuple-element.19.phi_low, f32[8,3,32,128]{3,2,1,0:T(8,128)S(1)} %get-tuple-element.20.phi_high, f32[4,4,32,128]{3,2,1,0:T(8,128)S(1)} %broadcast_select_fusion.2.b_mine, ...), custom_call_target="tpu_custom_call" | custom-call | tf_op jit(solution)/shard_map/pallas_call | solution.py:164
  (5 shorter events, 0.2 us)
Async XLA Ops:
  0.0 5.8 %collective-permute-start = (f32[8,4,32,128]{3,2,1,0:T(8,128)}, f32[8,4,32,128]{3,2,1,0:T(8,128)S(1)}, u32[]{:S(2)}, u32[]{:S(2)}) collective-permute-start(f32[8,4,32,128]{3,2,1,0:T(8,128)} %phi.1), channel_id=1, source_target_pairs={{0,16},{16,0},{32,48},{48,32},{64,80},{80,64},{96,112},{112,96},{1... | collective-permute-start | bytes 1572872 | tf_op jit(solution)/shard_map/ppermute | solution.py:193
  3.2 13.8 %collective-permute-start.1 = (f32[8,4,32,128]{3,2,1,0:T(8,128)}, f32[8,4,32,128]{3,2,1,0:T(8,128)S(1)}, u32[]{:S(2)}, u32[]{:S(2)}) collective-permute-start(f32[8,4,32,128]{3,2,1,0:T(8,128)} %phi.1), channel_id=1, source_target_pairs={{0,1},{1,0},{2,3},{3,2},{4,5},{5,4},{6,7},{7,6},{8,9},{9,8},{10,11... | collective-permute-start | bytes 1572872 | tf_op jit(solution)/shard_map/ppermute | solution.py:189
  3.2 0.7 %copy-start.1 = (s32[32]{0:T(128)S(1)}, s32[32]{0:T(128)}, u32[]{:S(2)}) copy-start(s32[32]{0:T(128)} %param.3) | copy-start | bytes 388
  6.9 10.2 %collective-permute-start.4 = (f32[4,4,32,128]{3,2,1,0:T(8,128)S(1)}, f32[4,4,32,128]{3,2,1,0:T(8,128)S(1)}, u32[]{:S(2)}, u32[]{:S(2)}) collective-permute-start(f32[4,4,32,128]{3,2,1,0:T(8,128)S(1)} %fusion), channel_id=1, source_target_pairs={{0,32},{16,48},{32,64},{48,80},{64,96},{80,112},{96,0},{112,16},{1... | collective-permute-start | bytes 786440 | tf_op jit(solution)/shard_map/ppermute | solution.py:204
  7.8 14.4 %collective-permute-start.3 = (f32[4,4,32,128]{3,2,1,0:T(8,128)S(1)}, f32[4,4,32,128]{3,2,1,0:T(8,128)S(1)}, u32[]{:S(2)}, u32[]{:S(2)}) collective-permute-start(f32[4,4,32,128]{3,2,1,0:T(8,128)S(1)} %fusion), channel_id=1, source_target_pairs={{0,64},{16,80},{32,96},{48,112},{64,0},{80,16},{96,32},{112,48},{1... | collective-permute-start | bytes 786440 | tf_op jit(solution)/shard_map/ppermute | solution.py:206
  10.4 11.8 %collective-permute-start.2 = (f32[4,4,32,128]{3,2,1,0:T(8,128)S(1)}, f32[4,4,32,128]{3,2,1,0:T(8,128)S(1)}, u32[]{:S(2)}, u32[]{:S(2)}) collective-permute-start(f32[4,4,32,128]{3,2,1,0:T(8,128)S(1)} %fusion), channel_id=1, source_target_pairs={{0,96},{16,112},{32,0},{48,16},{64,32},{80,48},{96,64},{112,80},{1... | collective-permute-start | bytes 786440 | tf_op jit(solution)/shard_map/ppermute | solution.py:205
  17.1 12.6 %collective-permute-start.5 = (f32[8,3,32,128]{3,2,1,0:T(8,128)S(1)}, f32[8,3,32,128]{3,2,1,0:T(8,128)S(1)}, u32[]{:S(2)}, u32[]{:S(2)}) collective-permute-start(f32[8,3,32,128]{3,2,1,0:T(8,128)S(1)} %slice_select_fusion.1), channel_id=1, source_target_pairs={{0,2},{1,15},{2,4},{3,1},{4,6},{5,3},{6,8},{7,5},{8,10},{9,7},{10,... | collective-permute-start | bytes 1179656 | tf_op jit(solution)/shard_map/ppermute | solution.py:214
  22.3 8.3 %collective-permute-start.6 = (f32[4,4,32,128]{3,2,1,0:T(8,128)S(1)}, f32[4,4,32,128]{3,2,1,0:T(8,128)S(1)}, u32[]{:S(2)}, u32[]{:S(2)}) collective-permute-start(f32[4,4,32,128]{3,2,1,0:T(8,128)S(1)} %select_select_fusion), channel_id=1, source_target_pairs={{0,128},{16,144},{32,160},{48,176},{64,192},{80,208},{96,224},{112... | collective-permute-start | bytes 786440 | tf_op jit(solution)/shard_map/ppermute | solution.py:215
  30.6 7.9 %collective-permute-start.9 = (f32[4,4,32,128]{3,2,1,0:T(8,128)S(1)}, f32[4,4,32,128]{3,2,1,0:T(8,128)S(1)}, u32[]{:S(2)}, u32[]{:S(2)}) collective-permute-start(f32[4,4,32,128]{3,2,1,0:T(8,128)S(1)} %broadcast_select_fusion.2.b_mine), channel_id=1, source_target_pairs={{0,16},{16,0},{32,48},{48,32},{64,80},{80,64},{96,112},{112,96},{1... | collective-permute-start | bytes 786440 | tf_op jit(solution)/shard_map/ppermute | solution.py:225
  32.7 12.4 %collective-permute-start.8 = (f32[4,3,32,128]{3,2,1,0:T(8,128)S(1)}, f32[4,3,32,128]{3,2,1,0:T(8,128)S(1)}, u32[]{:S(2)}, u32[]{:S(2)}) collective-permute-start(f32[4,3,32,128]{3,2,1,0:T(8,128)S(1)} %get-tuple-element.25), channel_id=1, source_target_pairs={{1,0},{2,1},{3,2},{4,3},{5,4},{6,5},{7,6},{8,7},{9,8},{10,9},{11,1... | collective-permute-start | bytes 589832 | tf_op jit(solution)/shard_map/ppermute | solution.py:224
  38.4 1.0 %copy-start = (f32[8,4,32,128]{3,2,1,0:T(8,128)S(1)}, f32[8,4,32,128]{3,2,1,0:T(8,128)}, u32[]{:S(2)}) copy-start(f32[8,4,32,128]{3,2,1,0:T(8,128)} %phi.1) | copy-start | bytes 1572868
  38.4 8.3 %collective-permute-start.7 = (f32[4,3,32,128]{3,2,1,0:T(8,128)S(1)}, f32[4,3,32,128]{3,2,1,0:T(8,128)S(1)}, u32[]{:S(2)}, u32[]{:S(2)}) collective-permute-start(f32[4,3,32,128]{3,2,1,0:T(8,128)S(1)} %get-tuple-element.26), channel_id=1, source_target_pairs={{0,1},{1,2},{2,3},{3,4},{4,5},{5,6},{6,7},{7,8},{8,9},{9,10},{10,1... | collective-permute-start | bytes 589832 | tf_op jit(solution)/shard_map/ppermute | solution.py:223
  46.7 2.2 %collective-permute-start.10 = (f32[4,3,32,128]{3,2,1,0:T(8,128)S(1)}, f32[4,3,32,128]{3,2,1,0:T(8,128)S(1)}, u32[]{:S(2)}, u32[]{:S(2)}) collective-permute-start(f32[4,3,32,128]{3,2,1,0:T(8,128)S(1)} %collective-permute-done.7.low_mine), channel_id=1, source_target_pairs={{0,16},{16,0},{32,48},{48,32},{64,80},{80,64},{96,112},{112,96},{1... | collective-permute-start | bytes 589832 | tf_op jit(solution)/shard_map/ppermute | solution.py:231
  47.8 1.4 %collective-permute-start.11 = (f32[4,3,32,128]{3,2,1,0:T(8,128)S(1)}, f32[4,3,32,128]{3,2,1,0:T(8,128)S(1)}, u32[]{:S(2)}, u32[]{:S(2)}) collective-permute-start(f32[4,3,32,128]{3,2,1,0:T(8,128)S(1)} %collective-permute-done.8.high_mine), channel_id=1, source_target_pairs={{0,16},{16,0},{32,48},{48,32},{64,80},{80,64},{96,112},{112,96},{1... | collective-permute-start | bytes 589832 | tf_op jit(solution)/shard_map/ppermute | solution.py:232

commit v5 on v2

v5 whole, which is shorter than its diff:
```python
import itertools

import jax
import jax.numpy as jnp
import numpy as np
from jax import lax
from jax.experimental import pallas as pl
from jax.experimental.pallas import tpu as pltpu
from jax.sharding import PartitionSpec as P

LOCAL = 8
BLOCK = 4
SWEEPS = 3
ROWS = 8
screen = 0.5
exchange_scale = 0.25


def stencil():
    steps = [tuple(s * (d == k) for d in range(3)) for k in range(3) for s in (1, -1)]
    taps = {(0, 0, 0): 1.0 / screen}
    for _ in range(SWEEPS):
        spread = {(0, 0, 0): 1.0}
        for at, weight in taps.items():
            for step in steps:
                to = tuple(a + s for a, s in zip(at, step))
                spread[to] = spread.get(to, 0.0) + weight
        taps = {at: weight / (6.0 + screen) for at, weight in spread.items()}
    return {at: -exchange_scale * weight for at, weight in taps.items()}


TAPS = stencil()
REACH = SWEEPS


def turned(cells, shift):
    return pltpu.roll(cells, shift % cells.shape[-1], cells.ndim - 1) if shift else cells


def apply_taps(x, y0, pairs, sums, centre, b_at, phi_at):
    count = len(sums)
    own = [centre(i, x, y0) for i in range(count)]
    for reach in range(REACH + 1):
        shifts = (0,) if reach == 0 else (reach, -reach)
        reached = [
            (dx, dy, layer)
            for dx, layer in pairs
            for dy in range(-REACH, REACH + 1)
            if abs(dx) + abs(dy) + reach <= REACH
        ]
        if not reached:
            continue
        here = {dz: [turned(cells, dz) for cells in own] for dz in shifts}
        totals = {dz: [None] * count for dz in shifts}
        for dx, dy, layer in reached:
            there = [b_at(i, layer, y0, dy) for i in range(count)]
            weights = {}
            for dz in shifts:
                gram = here[dz][0] * there[0]
                for i in range(1, count):
                    gram = gram + here[dz][i] * there[i]
                weights[dz] = gram * np.float32(TAPS[dx, dy, dz])
            for j in range(count):
                phi = phi_at(j, layer, y0, dy)
                for dz in shifts:
                    part = weights[dz] * phi
                    totals[dz][j] = part if totals[dz][j] is None else totals[dz][j] + part
        for dz in shifts:
            for j in range(count):
                sums[j] = sums[j] + turned(totals[dz][j], -dz)
    return sums


def pad_rows(dst, at, layer, cells):
    ny = cells.shape[0]
    dst[at, layer, ROWS : ROWS + ny] = cells
    dst[at, layer, 0:ROWS] = cells[ny - ROWS :]
    dst[at, layer, ROWS + ny :] = cells[:ROWS]


def inner_kernel(phi, b_mine, b_other, pair, far, out, ends, padded_phi, padded_b):
    count, nx, ny, nz = phi.shape

    def fill(i, _):
        for x in range(nx):
            pad_rows(padded_phi, i, x, phi[i, x])
            pad_rows(padded_phi, i + BLOCK, x, phi[i + BLOCK, x])
            pad_rows(padded_b, i, x, b_mine[i, x])
            pad_rows(padded_b, i + BLOCK, x, b_other[i, x])
        return 0

    lax.fori_loop(0, BLOCK, fill, 0)

    even = lax.axis_index("dom") & 1 == 0

    def fill_ends(low, low_at, high, high_at):
        def fill(i, _):
            for layer in range(REACH):
                pad_rows(ends, i, layer, low[i, low_at + layer])
                pad_rows(ends, i, REACH + layer, high[i, high_at + layer])
            return 0

        lax.fori_loop(0, count, fill, 0)

    pl.when(even)(lambda: fill_ends(far, 0, pair, 0))
    pl.when(jnp.logical_not(even))(lambda: fill_ends(pair, nx - REACH, far, 0))

    def tile(t, _):
        y0 = pl.multiple_of(t * ROWS, ROWS)

        def at(ref):
            return lambda i, layer, y0, dy: ref[i, layer, pl.ds(y0 + ROWS + dy, ROWS), :]

        b_at = at(padded_b)
        for x in range(nx):
            pairs = [(to - x, to) for to in range(nx) if abs(to - x) <= REACH]
            sums = [jnp.zeros((ROWS, nz), jnp.float32)] * count
            sums = apply_taps(
                x, y0, pairs, sums, lambda i, x, y0: b_at(i, x, y0, 0), b_at, at(padded_phi)
            )
            for j in range(count):
                out[j, x, pl.ds(y0, ROWS), :] = sums[j]
        return 0

    lax.fori_loop(0, ny // ROWS, tile, 0)


def outer_kernel(
    part, ends, b_mine, b_other, low_mine, low_other, high_mine, high_other, out, padded_b, done, sems
):
    count, nx, ny, _ = part.shape

    def fill(i, _):
        for layer in range(REACH):
            pad_rows(padded_b, i, layer, low_mine[i, layer])
            pad_rows(padded_b, i + BLOCK, layer, low_other[i, layer])
            pad_rows(padded_b, i, REACH + layer, high_mine[i, layer])
            pad_rows(padded_b, i + BLOCK, REACH + layer, high_other[i, layer])
        return 0

    lax.fori_loop(0, BLOCK, fill, 0)

    def move(y0, t):
        rows = pl.ds(y0, ROWS)
        return pltpu.make_async_copy(done.at[:, :, rows], out.at[:, :, rows], sems.at[t])

    def centre(i, x, y0):
        return (b_mine if i < BLOCK else b_other)[i % BLOCK, x, pl.ds(y0, ROWS), :]

    def tile(t, _):
        y0 = pl.multiple_of(t * ROWS, ROWS)

        def at(ref):
            return lambda i, layer, y0, dy: ref[i, layer, pl.ds(y0 + ROWS + dy, ROWS), :]

        for x in range(nx):
            pairs = [(layer - REACH - x, layer) for layer in range(REACH) if x - (layer - REACH) <= REACH]
            pairs += [(nx + layer - x, REACH + layer) for layer in range(REACH) if nx + layer - x <= REACH]
            sums = [part[j, x, pl.ds(y0, ROWS), :] for j in range(count)]
            sums = apply_taps(x, y0, pairs, sums, centre, at(padded_b), at(ends))
            for j in range(count):
                done[j, x, pl.ds(y0, ROWS), :] = sums[j]
        move(y0, t).start()
        return 0

    lax.fori_loop(0, ny // ROWS, tile, 0)
    for t in range(ny // ROWS):
        move(t * ROWS, t).wait()


def flags_kernel(order, flags):
    band = lax.axis_index("band")
    core = band & 1
    block = order[core]
    rows = (
        block & 1,
        ((block >> 1) & 1) ^ core,
        ((block >> 2) - (band >> 1)) & 3,
        (block >> 4) ^ (band >> 3),
    )
    for row, number in enumerate(rows):
        flags[row : row + 1, :] = jnp.full((1, flags.shape[1]), number, jnp.int32)


def flag_is(flags, row, number, like):
    return jnp.broadcast_to(flags[row : row + 1, :], like.shape) == number


def choose_kernel(flags, own, got, *chosen):
    row = (lax.axis_index("band") >> 1) & 3
    for step, out in enumerate(chosen):
        i = (row + step) & 3
        for x in range(out.shape[0]):
            first, last = own[i, x], own[i + BLOCK, x]
            here = flag_is(flags, 1, 0, first)
            first = jnp.where(here, first, got[i, x])
            last = jnp.where(here, last, got[i + BLOCK, x])
            out[x] = jnp.where(flag_is(flags, 0, 0, first), first, last)


def keep_kernel(cells, kept):
    kept[...] = cells[...]


def pick_kernel(flags, own, above, opposite, below, picked):
    for x in range(picked.shape[0]):
        cells = own[x]
        for number, other in ((1, above), (2, opposite), (3, below)):
            cells = jnp.where(flag_is(flags, 2, number, cells), other[x], cells)
        picked[x] = cells


def settle_kernel(flags, own, crossed, settled):
    for x in range(own.shape[0]):
        cells = own[x]
        settled[x] = jnp.where(flag_is(flags, 3, 0, cells), cells, crossed[x])


def gather_kernel(own, below, opposite, above, block, tail, head):
    nx = own.shape[0]
    for i, source in enumerate((own, below, opposite, above)):
        for x in range(nx):
            cells = source[x]
            block[i, x] = cells
            if x >= nx - REACH:
                tail[i, x - (nx - REACH)] = cells
            if x < REACH:
                head[i, x] = cells


VMEM = pl.BlockSpec(memory_space=pltpu.VMEM)
LIMIT = pltpu.CompilerParams(vmem_limit_bytes=32 * 1024 * 1024)


def call(kernel, shapes, *args, in_specs=None, out_specs=VMEM, scratch=(), kind=jnp.float32):
    shapes = [shapes] if isinstance(shapes[0], int) else list(shapes)
    kinds = kind if isinstance(kind, tuple) else (kind,) * len(shapes)
    outs = [jax.ShapeDtypeStruct(shape, kind) for shape, kind in zip(shapes, kinds)]
    single = len(outs) == 1
    return pl.pallas_call(
        kernel,
        out_shape=outs[0] if single else outs,
        in_specs=in_specs or [VMEM] * len(args),
        out_specs=out_specs if single else [out_specs] * len(outs),
        scratch_shapes=list(scratch),
        compiler_params=LIMIT,
    )(*args)


def local(orbitals, owner_order):
    count, nx, ny, nz = orbitals.shape
    bands, doms = lax.axis_size("band"), lax.axis_size("dom")
    whole, half, side = (count, nx, ny, nz), (BLOCK, nx, ny, nz), (BLOCK, REACH, ny, nz)
    layers = (nx, ny, nz)
    partner = [(i, i ^ 1) for i in range(bands)]
    across = [(i, i ^ 8) for i in range(bands)]
    up = [
        (band * doms + i, (band ^ 8 * (i % 2)) * doms + (i + 1) % doms) for band in range(bands) for i in range(doms)
    ]
    down = [(to, source) for source, to in up]

    def along_y(step):
        return [(i, i // 8 * 8 + (i + 2 * step) % 8) for i in range(bands)]

    pair = lax.ppermute(orbitals, "dom", [(i, i ^ 1) for i in range(doms)])
    onward = [(i, (i + 2 - 4 * (i % 2)) % doms) for i in range(doms)]
    even = lax.axis_index("dom") & 1 == 0

    got = lax.ppermute(orbitals, "band", partner)
    flags = call(
        flags_kernel, (8, nz), owner_order, in_specs=[pl.BlockSpec(memory_space=pltpu.SMEM)], kind=jnp.int32
    )
    chosen = call(choose_kernel, (layers,) * 4, flags, orbitals, got)
    below = lax.ppermute(chosen[1], "band", along_y(1))
    opposite = lax.ppermute(chosen[2], "band", along_y(2))
    above = lax.ppermute(chosen[3], "band", along_y(-1))
    own = chosen[0]
    picked = call(pick_kernel, layers, flags, own, above, opposite, below)
    crossed = lax.ppermute(picked, "band", across)
    picked, pair = lax.optimization_barrier((picked, pair))
    picked = call(keep_kernel, layers, picked)
    settled = call(settle_kernel, layers, flags, picked, crossed)
    far = lax.ppermute(jnp.where(even, pair[:, nx - REACH :], pair[:, :REACH]), "dom", onward)
    below = lax.ppermute(settled, "band", along_y(1))
    opposite = lax.ppermute(settled, "band", along_y(2))
    above = lax.ppermute(settled, "band", along_y(-1))
    b_mine, tail, head = call(gather_kernel, (half, side, side), settled, below, opposite, above)
    low_mine = lax.ppermute(tail, ("band", "dom"), up)
    high_mine = lax.ppermute(head, ("band", "dom"), down)
    b_other = lax.ppermute(b_mine, "band", partner)
    padded = pltpu.VMEM((count, nx, ny + 2 * ROWS, nz), jnp.float32)
    part, ends = call(
        inner_kernel, (whole, (count, 2 * REACH, ny + 2 * ROWS, nz)), orbitals, b_mine, b_other, pair, far,
        scratch=[padded, padded],
    )
    low_mine, high_mine, part = lax.optimization_barrier((low_mine, high_mine, part))

    low_other = lax.ppermute(low_mine, "band", partner)
    high_other = lax.ppermute(high_mine, "band", partner)
    return call(
        outer_kernel, whole, part, ends, b_mine, b_other, low_mine, low_other, high_mine, high_other,
        out_specs=pl.BlockSpec(memory_space=pl.ANY),
        scratch=[
            pltpu.VMEM((count, 2 * REACH, ny + 2 * ROWS, nz), jnp.float32),
            pltpu.VMEM(whole, jnp.float32),
            pltpu.SemaphoreType.DMA((ny // ROWS,)),
        ],
    )


def solution(mesh):
    in_specs = (P("band", "dom", None, None), P())
    out_specs = P("band", "dom", None, None)
    return jax.shard_map(local, mesh=mesh, in_specs=in_specs, out_specs=out_specs, check_vma=False)
```

time: 66.8 us -> 45.9 us (0.69)
  waiting for transfers between devices: 21.3 us -> 12.4 us
  starting transfers between devices: 30 us -> 22.7 us
  between operations: 2.74 us -> 0.08 us
  local copies, waits for them, and re-layouts: 3.17 us -> 1.7 us
  other arithmetic: 0.74 us -> 0.04 us
    ppermute x4 -> x11, starting transfers between devices: 6.34 us -> 16.8 us  [the longest x1 3.75 us: local(): low_mine = lax.ppermute(tail, ('band', 'dom'), up)]
    all_to_all x2 -> x0, starting transfers between devices: 10.2 us -> none  [the longest x1 5.8 us: local(): chunks = lax.all_to_all(chunks, 'band', 0, 0, axis_index_groups=same_core)]
    all_to_all x2 -> x0, waiting for transfers between devices: 8.03 us -> none  [the longest x1 5.17 us: local(): b_mine = lax.all_to_all(chunks, 'band', 0, 0, axis_index_groups=same_core)]
    ppermute x1, starting transfers between devices: 9.47 us -> 2.01 us  [local(): b_other = lax.ppermute(b_mine, 'band', partner)]
    ppermute x4 -> x11, waiting for transfers between devices: 11.9 us -> 10.5 us  [the longest x1 3.35 us: local(): opposite = lax.ppermute(settled, 'band', along_y(2))]
    slice x2 -> x0, local copies, waits for them, and re-layouts: 1.2 us -> none  [the longest x1 1.17 us: local(): phi_high = lax.ppermute(orbitals[:, :REACH], 'dom', down)]
    unnamed x4 -> x6, local copies, waits for them, and re-layouts: 0.65 us -> 1.7 us
    broadcast_in_dim x1 -> x0, local copies, waits for them, and re-layouts: 0.73 us -> none  [local(): chunks = jnp.broadcast_to(chunk, chunks.shape)]
  transfers between devices with their start and end apart: 10 -> 15, of which waited for: 6 -> 11; matrix products, arithmetic and copies ran while one was open for 5% -> 0% of each run, Pallas kernels for 9% -> 14%
where the time goes in v5:
time: 45.9 us; the launch traced here: 45.8 us
  starting transfers between devices  22.7 us (49%)
  waiting for transfers between devices  12.4 us (27%)
  Pallas kernels  8.88 us (19%)
  local copies, waits for them, and re-layouts  1.7 us (4%)
    pallas_call x8, Pallas kernels, call(): pl.pallas_call(kernel, out_shape=outs[0] if single else outs, in_specs=in...  8.88 us
    ppermute x1, starting transfers between devices, local(): low_mine = lax.ppermute(tail, ('band', 'dom'), up)  3.75 us
    ppermute x1, waiting for transfers between devices, local(): opposite = lax.ppermute(settled, 'band', along_y(2))  3.35 us
    ppermute x1, starting transfers between devices, local(): got = lax.ppermute(orbitals, 'band', partner)  3.24 us
    ppermute x1, waiting for transfers between devices, local(): opposite = lax.ppermute(chosen[2], 'band', along_y(2))  2.97 us
    ppermute x1, starting transfers between devices, local(): above = lax.ppermute(settled, 'band', along_y(-1))  2.59 us
    ppermute x1, starting transfers between devices, local(): crossed = lax.ppermute(picked, 'band', across)  2.54 us
    ppermute x1, starting transfers between devices, local(): high_mine = lax.ppermute(head, ('band', 'dom'), down)  2.42 us
  transfers between devices with their start and end apart: 15, of which 11 were waited for; matrix products, arithmetic and copies ran while one was open for 0% of the time, Pallas kernels for 14%

profile of v5, /device:TPU:1, one launch (start us, length us, event | category | flops | bytes accessed | tf_op | source)
XLA Modules:
  0.0 45.8 jit_solution(16689969857606160828)
XLA Ops:
  0.0 3.2 %collective-permute-start = (f32[8,4,32,128]{3,2,1,0:T(8,128)}, f32[8,4,32,128]{3,2,1,0:T(8,128)S(1)}, u32[]{:S(2)}, u32[]{:S(2)}) collective-permute-start(f32[8,4,32,128]{3,2,1,0:T(8,128)} %phi.1), channel_id=1, source_target_pairs={{0,16},{16,0},{32,48},{48,32},{64,80},{80,64},{96,112},{112,96},{1... | collective-permute-start | bytes 1572872 | tf_op jit(solution)/shard_map/ppermute | solution.py:269
  3.2 0.0 collective-permute-start.4
  3.2 0.0 copy-start.2
  3.2 0.7 %copy-done.2 = s32[32]{0:T(128)S(1)} copy-done((s32[32]{0:T(128)S(1)}, s32[32]{0:T(128)}, u32[]{:S(2)}) %copy-start.2) | copy-done | bytes 152
  3.9 0.6 %shard_map.28.flags = s32[8,128]{1,0:T(8,128)S(1)} custom-call(s32[32]{0:T(128)S(1)} %copy-done.2), custom_call_target="tpu_custom_call" | custom-call | tf_op jit(solution)/shard_map/pallas_call | solution.py:240
  4.5 0.5 %collective-permute-done.got = f32[8,4,32,128]{3,2,1,0:T(8,128)S(1)} collective-permute-done((f32[8,4,32,128]{3,2,1,0:T(8,128)}, f32[8,4,32,128]{3,2,1,0:T(8,128)S(1)}, u32[]{:S(2)}, u32[]{:S(2)}) %collective-permute-start) | collective-permute-done | bytes 524320 | tf_op jit(solution)/shard_map/ppermute | solution.py:269
  5.0 0.0 copy-start
  5.0 1.0 %copy-done = f32[8,4,32,128]{3,2,1,0:T(8,128)S(1)} copy-done((f32[8,4,32,128]{3,2,1,0:T(8,128)S(1)}, f32[8,4,32,128]{3,2,1,0:T(8,128)}, u32[]{:S(2)}) %copy-start) | copy-done | bytes 524312
  6.0 0.1 shard_map.29
  6.1 0.0 copy-start.1
  6.1 1.8 %collective-permute-start.1 = (f32[4,32,128]{2,1,0:T(8,128)S(1)}, f32[4,32,128]{2,1,0:T(8,128)S(1)}, u32[]{:S(2)}, u32[]{:S(2)}) collective-permute-start(f32[4,32,128]{2,1,0:T(8,128)S(1)} %get-tuple-element.20), channel_id=1, source_target_pairs={{0,96},{16,112},{32,0},{48,16},{64,32},{80,48},{96,64},{112,80},{1... | collective-permute-start | bytes 196616 | tf_op jit(solution)/shard_map/ppermute | solution.py:276
  7.9 0.3 collective-permute-start.2
  8.2 0.7 %collective-permute-start.3 = (f32[4,32,128]{2,1,0:T(8,128)S(1)}, f32[4,32,128]{2,1,0:T(8,128)S(1)}, u32[]{:S(2)}, u32[]{:S(2)}) collective-permute-start(f32[4,32,128]{2,1,0:T(8,128)S(1)} %get-tuple-element.22), channel_id=1, source_target_pairs={{0,32},{16,48},{32,64},{48,80},{64,96},{80,112},{96,0},{112,16},{1... | collective-permute-start | bytes 196616 | tf_op jit(solution)/shard_map/ppermute | solution.py:274
  8.9 0.7 %collective-permute-done.1.above = f32[4,32,128]{2,1,0:T(8,128)S(1)} collective-permute-done((f32[4,32,128]{2,1,0:T(8,128)S(1)}, f32[4,32,128]{2,1,0:T(8,128)S(1)}, u32[]{:S(2)}, u32[]{:S(2)}) %collective-permute-start.1) | collective-permute-done | bytes 65568 | tf_op jit(solution)/shard_map/ppermute | solution.py:276
  9.6 3.0 %collective-permute-done.2.opposite = f32[4,32,128]{2,1,0:T(8,128)S(1)} collective-permute-done((f32[4,32,128]{2,1,0:T(8,128)S(1)}, f32[4,32,128]{2,1,0:T(8,128)S(1)}, u32[]{:S(2)}, u32[]{:S(2)}) %collective-permute-start.2) | collective-permute-done | bytes 65568 | tf_op jit(solution)/shard_map/ppermute | solution.py:275
  12.6 1.8 %collective-permute-done.3.below = f32[4,32,128]{2,1,0:T(8,128)S(1)} collective-permute-done((f32[4,32,128]{2,1,0:T(8,128)S(1)}, f32[4,32,128]{2,1,0:T(8,128)S(1)}, u32[]{:S(2)}, u32[]{:S(2)}) %collective-permute-start.3) | collective-permute-done | bytes 65568 | tf_op jit(solution)/shard_map/ppermute | solution.py:274
  14.4 2.5 %collective-permute-start.5 = (f32[4,32,128]{2,1,0:T(8,128)S(1)}, f32[4,32,128]{2,1,0:T(8,128)S(1)}, u32[]{:S(2)}, u32[]{:S(2)}) collective-permute-start(f32[4,32,128]{2,1,0:T(8,128)S(1)} %shard_map.30.cells), channel_id=1, source_target_pairs={{0,128},{16,144},{32,160},{48,176},{64,192},{80,208},{96,224},{112... | collective-permute-start | bytes 196616 | tf_op jit(solution)/shard_map/ppermute | solution.py:279
  16.9 0.1 collective-permute-done.4.pair
  17.1 1.6 %collective-permute-start.12 = (f32[8,3,32,128]{3,2,1,0:T(8,128)S(1)}, f32[8,3,32,128]{3,2,1,0:T(8,128)S(1)}, u32[]{:S(2)}, u32[]{:S(2)}) collective-permute-start(f32[8,3,32,128]{3,2,1,0:T(8,128)S(1)} %slice_select_fusion), channel_id=1, source_target_pairs={{0,2},{1,15},{2,4},{3,1},{4,6},{5,3},{6,8},{7,5},{8,10},{9,7},{10,... | collective-permute-start | bytes 1179656 | tf_op jit(solution)/shard_map/ppermute | solution.py:283
  18.7 0.4 collective-permute-done.5.crossed
  19.1 2.6 %collective-permute-start.8 = (f32[4,32,128]{2,1,0:T(8,128)S(1)}, f32[4,32,128]{2,1,0:T(8,128)S(1)}, u32[]{:S(2)}, u32[]{:S(2)}) collective-permute-start(f32[4,32,128]{2,1,0:T(8,128)S(1)} %shard_map.32.own), channel_id=1, source_target_pairs={{0,96},{16,112},{32,0},{48,16},{64,32},{80,48},{96,64},{112,80},{1... | collective-permute-start | bytes 196616 | tf_op jit(solution)/shard_map/ppermute | solution.py:286
  21.7 0.3 collective-permute-start.7
  22.0 0.7 %collective-permute-start.6 = (f32[4,32,128]{2,1,0:T(8,128)S(1)}, f32[4,32,128]{2,1,0:T(8,128)S(1)}, u32[]{:S(2)}, u32[]{:S(2)}) collective-permute-start(f32[4,32,128]{2,1,0:T(8,128)S(1)} %shard_map.32.own), channel_id=1, source_target_pairs={{0,32},{16,48},{32,64},{48,80},{64,96},{80,112},{96,0},{112,16},{1... | collective-permute-start | bytes 196616 | tf_op jit(solution)/shard_map/ppermute | solution.py:284
  22.7 0.3 collective-permute-done.8.above
  23.0 3.4 %collective-permute-done.7.opposite = f32[4,32,128]{2,1,0:T(8,128)S(1)} collective-permute-done((f32[4,32,128]{2,1,0:T(8,128)S(1)}, f32[4,32,128]{2,1,0:T(8,128)S(1)}, u32[]{:S(2)}, u32[]{:S(2)}) %collective-permute-start.7) | collective-permute-done | bytes 65568 | tf_op jit(solution)/shard_map/ppermute | solution.py:285
  26.4 0.9 %collective-permute-done.6.below = f32[4,32,128]{2,1,0:T(8,128)S(1)} collective-permute-done((f32[4,32,128]{2,1,0:T(8,128)S(1)}, f32[4,32,128]{2,1,0:T(8,128)S(1)}, u32[]{:S(2)}, u32[]{:S(2)}) %collective-permute-start.6) | collective-permute-done | bytes 65568 | tf_op jit(solution)/shard_map/ppermute | solution.py:284
  27.4 2.0 %collective-permute-start.11 = (f32[4,4,32,128]{3,2,1,0:T(8,128)S(1)}, f32[4,4,32,128]{3,2,1,0:T(8,128)S(1)}, u32[]{:S(2)}, u32[]{:S(2)}) collective-permute-start(f32[4,4,32,128]{3,2,1,0:T(8,128)S(1)} %get-tuple-element.26.b_mine), channel_id=1, source_target_pairs={{0,16},{16,0},{32,48},{48,32},{64,80},{80,64},{96,112},{112,96},{1... | collective-permute-start | bytes 786440 | tf_op jit(solution)/shard_map/ppermute | solution.py:290
  29.4 3.7 %collective-permute-start.9 = (f32[4,3,32,128]{3,2,1,0:T(8,128)S(1)}, f32[4,3,32,128]{3,2,1,0:T(8,128)S(1)}, u32[]{:S(2)}, u32[]{:S(2)}) collective-permute-start(f32[4,3,32,128]{3,2,1,0:T(8,128)S(1)} %get-tuple-element.24), channel_id=1, source_target_pairs={{0,1},{1,130},{2,3},{3,132},{4,5},{5,134},{6,7},{7,136},{8,9},{9,1... | collective-permute-start | bytes 589832 | tf_op jit(solution)/shard_map/ppermute | solution.py:288
  33.1 2.4 %collective-permute-start.10 = (f32[4,3,32,128]{3,2,1,0:T(8,128)S(1)}, f32[4,3,32,128]{3,2,1,0:T(8,128)S(1)}, u32[]{:S(2)}, u32[]{:S(2)}) collective-permute-start(f32[4,3,32,128]{3,2,1,0:T(8,128)S(1)} %get-tuple-element.25), channel_id=1, source_target_pairs={{1,0},{130,1},{3,2},{132,3},{5,4},{134,5},{7,6},{136,7},{9,8},{138... | collective-permute-start | bytes 589832 | tf_op jit(solution)/shard_map/ppermute | solution.py:289
  35.5 0.0 collective-permute-done.11.b_other
  35.5 0.0 collective-permute-done.12.far
  35.5 0.0 copy-done.1
  35.5 5.8 %shard_map.34 = (f32[8,4,32,128]{3,2,1,0:T(8,128)S(1)}, f32[8,6,48,128]{3,2,1,0:T(8,128)S(1)}) custom-call(f32[8,4,32,128]{3,2,1,0:T(8,128)S(1)} %copy-done.1, f32[4,4,32,128]{3,2,1,0:T(8,128)S(1)} %get-tuple-element.26.b_mine, f32[4,4,32,128]{3,2,1,0:T(8,128)S(1)} %collective-permute-done.11.b_other, f32[8,4,32,128]{3,2,1,0:T(8,128)S(1)} %collective-permute-done.4.pair, ...), custom_call_target="tpu_custom_call" | custom-call | tf_op jit(solution)/shard_map/pallas_call | solution.py:240
  41.4 0.0 collective-permute-done.9.low_mine
  41.4 0.0 collective-permute-done.10.high_mine
  41.4 0.5 %collective-permute-start.13 = (f32[4,3,32,128]{3,2,1,0:T(8,128)S(1)}, f32[4,3,32,128]{3,2,1,0:T(8,128)S(1)}, u32[]{:S(2)}, u32[]{:S(2)}) collective-permute-start(f32[4,3,32,128]{3,2,1,0:T(8,128)S(1)} %collective-permute-done.9.low_mine), channel_id=1, source_target_pairs={{0,16},{16,0},{32,48},{48,32},{64,80},{80,64},{96,112},{112,96},{1... | collective-permute-start | bytes 589832 | tf_op jit(solution)/shard_map/ppermute | solution.py:298
  41.9 0.1 collective-permute-start.14
  42.0 1.0 %collective-permute-done.13.low_other = f32[4,3,32,128]{3,2,1,0:T(8,128)S(1)} collective-permute-done((f32[4,3,32,128]{3,2,1,0:T(8,128)S(1)}, f32[4,3,32,128]{3,2,1,0:T(8,128)S(1)}, u32[]{:S(2)}, u32[]{:S(2)}) %collective-permute-start.13) | collective-permute-done | bytes 196640 | tf_op jit(solution)/shard_map/ppermute | solution.py:298
  43.0 0.4 collective-permute-done.14.high_other
  43.4 2.4 %shard_map.35 = f32[8,4,32,128]{3,2,1,0:T(8,128)} custom-call(f32[8,4,32,128]{3,2,1,0:T(8,128)S(1)} %get-tuple-element.29.part, f32[8,6,48,128]{3,2,1,0:T(8,128)S(1)} %get-tuple-element.30.ends, f32[4,4,32,128]{3,2,1,0:T(8,128)S(1)} %get-tuple-element.26.b_mine, f32[4,4,32,128]{3,2,1,0:T(8,128)S(1)} %collective-permute-done.11.b_other, ...), custom_call_target="tpu_custom_call" | custom-call | tf_op jit(solution)/shard_map/pallas_call | solution.py:240
  (5 shorter events, 0.1 us)
Async XLA Ops:
  0.0 5.0 %collective-permute-start = (f32[8,4,32,128]{3,2,1,0:T(8,128)}, f32[8,4,32,128]{3,2,1,0:T(8,128)S(1)}, u32[]{:S(2)}, u32[]{:S(2)}) collective-permute-start(f32[8,4,32,128]{3,2,1,0:T(8,128)} %phi.1), channel_id=1, source_target_pairs={{0,16},{16,0},{32,48},{48,32},{64,80},{80,64},{96,112},{112,96},{1... | collective-permute-start | bytes 1572872 | tf_op jit(solution)/shard_map/ppermute | solution.py:269
  3.2 13.8 %collective-permute-start.4 = (f32[8,4,32,128]{3,2,1,0:T(8,128)}, f32[8,4,32,128]{3,2,1,0:T(8,128)S(1)}, u32[]{:S(2)}, u32[]{:S(2)}) collective-permute-start(f32[8,4,32,128]{3,2,1,0:T(8,128)} %phi.1), channel_id=1, source_target_pairs={{0,1},{1,0},{2,3},{3,2},{4,5},{5,4},{6,7},{7,6},{8,9},{9,8},{10,11... | collective-permute-start | bytes 1572872 | tf_op jit(solution)/shard_map/ppermute | solution.py:265
  3.2 0.7 %copy-start.2 = (s32[32]{0:T(128)S(1)}, s32[32]{0:T(128)}, u32[]{:S(2)}) copy-start(s32[32]{0:T(128)} %order.1) | copy-start | bytes 388
  5.0 1.0 %copy-start = (f32[8,4,32,128]{3,2,1,0:T(8,128)S(1)}, f32[8,4,32,128]{3,2,1,0:T(8,128)}, u32[]{:S(2)}) copy-start(f32[8,4,32,128]{3,2,1,0:T(8,128)} %phi.1) | copy-start | bytes 1572868
  6.1 29.5 %copy-start.1 = (f32[8,4,32,128]{3,2,1,0:T(8,128)S(1)}, f32[8,4,32,128]{3,2,1,0:T(8,128)}, u32[]{:S(2)}) copy-start(f32[8,4,32,128]{3,2,1,0:T(8,128)} %phi.1) | copy-start | bytes 1572868
  6.1 3.5 %collective-permute-start.1 = (f32[4,32,128]{2,1,0:T(8,128)S(1)}, f32[4,32,128]{2,1,0:T(8,128)S(1)}, u32[]{:S(2)}, u32[]{:S(2)}) collective-permute-start(f32[4,32,128]{2,1,0:T(8,128)S(1)} %get-tuple-element.20), channel_id=1, source_target_pairs={{0,96},{16,112},{32,0},{48,16},{64,32},{80,48},{96,64},{112,80},{1... | collective-permute-start | bytes 196616 | tf_op jit(solution)/shard_map/ppermute | solution.py:276
  7.9 4.7 %collective-permute-start.2 = (f32[4,32,128]{2,1,0:T(8,128)S(1)}, f32[4,32,128]{2,1,0:T(8,128)S(1)}, u32[]{:S(2)}, u32[]{:S(2)}) collective-permute-start(f32[4,32,128]{2,1,0:T(8,128)S(1)} %get-tuple-element.21), channel_id=1, source_target_pairs={{0,64},{16,80},{32,96},{48,112},{64,0},{80,16},{96,32},{112,48},{1... | collective-permute-start | bytes 196616 | tf_op jit(solution)/shard_map/ppermute | solution.py:275
  8.2 6.1 %collective-permute-start.3 = (f32[4,32,128]{2,1,0:T(8,128)S(1)}, f32[4,32,128]{2,1,0:T(8,128)S(1)}, u32[]{:S(2)}, u32[]{:S(2)}) collective-permute-start(f32[4,32,128]{2,1,0:T(8,128)S(1)} %get-tuple-element.22), channel_id=1, source_target_pairs={{0,32},{16,48},{32,64},{48,80},{64,96},{80,112},{96,0},{112,16},{1... | collective-permute-start | bytes 196616 | tf_op jit(solution)/shard_map/ppermute | solution.py:274
  14.4 4.7 %collective-permute-start.5 = (f32[4,32,128]{2,1,0:T(8,128)S(1)}, f32[4,32,128]{2,1,0:T(8,128)S(1)}, u32[]{:S(2)}, u32[]{:S(2)}) collective-permute-start(f32[4,32,128]{2,1,0:T(8,128)S(1)} %shard_map.30.cells), channel_id=1, source_target_pairs={{0,128},{16,144},{32,160},{48,176},{64,192},{80,208},{96,224},{112... | collective-permute-start | bytes 196616 | tf_op jit(solution)/shard_map/ppermute | solution.py:279
  17.1 18.5 %collective-permute-start.12 = (f32[8,3,32,128]{3,2,1,0:T(8,128)S(1)}, f32[8,3,32,128]{3,2,1,0:T(8,128)S(1)}, u32[]{:S(2)}, u32[]{:S(2)}) collective-permute-start(f32[8,3,32,128]{3,2,1,0:T(8,128)S(1)} %slice_select_fusion), channel_id=1, source_target_pairs={{0,2},{1,15},{2,4},{3,1},{4,6},{5,3},{6,8},{7,5},{8,10},{9,7},{10,... | collective-permute-start | bytes 1179656 | tf_op jit(solution)/shard_map/ppermute | solution.py:283
  19.1 3.9 %collective-permute-start.8 = (f32[4,32,128]{2,1,0:T(8,128)S(1)}, f32[4,32,128]{2,1,0:T(8,128)S(1)}, u32[]{:S(2)}, u32[]{:S(2)}) collective-permute-start(f32[4,32,128]{2,1,0:T(8,128)S(1)} %shard_map.32.own), channel_id=1, source_target_pairs={{0,96},{16,112},{32,0},{48,16},{64,32},{80,48},{96,64},{112,80},{1... | collective-permute-start | bytes 196616 | tf_op jit(solution)/shard_map/ppermute | solution.py:286
  21.7 4.7 %collective-permute-start.7 = (f32[4,32,128]{2,1,0:T(8,128)S(1)}, f32[4,32,128]{2,1,0:T(8,128)S(1)}, u32[]{:S(2)}, u32[]{:S(2)}) collective-permute-start(f32[4,32,128]{2,1,0:T(8,128)S(1)} %shard_map.32.own), channel_id=1, source_target_pairs={{0,64},{16,80},{32,96},{48,112},{64,0},{80,16},{96,32},{112,48},{1... | collective-permute-start | bytes 196616 | tf_op jit(solution)/shard_map/ppermute | solution.py:285
  22.0 5.3 %collective-permute-start.6 = (f32[4,32,128]{2,1,0:T(8,128)S(1)}, f32[4,32,128]{2,1,0:T(8,128)S(1)}, u32[]{:S(2)}, u32[]{:S(2)}) collective-permute-start(f32[4,32,128]{2,1,0:T(8,128)S(1)} %shard_map.32.own), channel_id=1, source_target_pairs={{0,32},{16,48},{32,64},{48,80},{64,96},{80,112},{96,0},{112,16},{1... | collective-permute-start | bytes 196616 | tf_op jit(solution)/shard_map/ppermute | solution.py:284
  27.4 8.2 %collective-permute-start.11 = (f32[4,4,32,128]{3,2,1,0:T(8,128)S(1)}, f32[4,4,32,128]{3,2,1,0:T(8,128)S(1)}, u32[]{:S(2)}, u32[]{:S(2)}) collective-permute-start(f32[4,4,32,128]{3,2,1,0:T(8,128)S(1)} %get-tuple-element.26.b_mine), channel_id=1, source_target_pairs={{0,16},{16,0},{32,48},{48,32},{64,80},{80,64},{96,112},{112,96},{1... | collective-permute-start | bytes 786440 | tf_op jit(solution)/shard_map/ppermute | solution.py:290
  29.4 12.0 %collective-permute-start.9 = (f32[4,3,32,128]{3,2,1,0:T(8,128)S(1)}, f32[4,3,32,128]{3,2,1,0:T(8,128)S(1)}, u32[]{:S(2)}, u32[]{:S(2)}) collective-permute-start(f32[4,3,32,128]{3,2,1,0:T(8,128)S(1)} %get-tuple-element.24), channel_id=1, source_target_pairs={{0,1},{1,130},{2,3},{3,132},{4,5},{5,134},{6,7},{7,136},{8,9},{9,1... | collective-permute-start | bytes 589832 | tf_op jit(solution)/shard_map/ppermute | solution.py:288
  33.1 8.3 %collective-permute-start.10 = (f32[4,3,32,128]{3,2,1,0:T(8,128)S(1)}, f32[4,3,32,128]{3,2,1,0:T(8,128)S(1)}, u32[]{:S(2)}, u32[]{:S(2)}) collective-permute-start(f32[4,3,32,128]{3,2,1,0:T(8,128)S(1)} %get-tuple-element.25), channel_id=1, source_target_pairs={{1,0},{130,1},{3,2},{132,3},{5,4},{134,5},{7,6},{136,7},{9,8},{138... | collective-permute-start | bytes 589832 | tf_op jit(solution)/shard_map/ppermute | solution.py:289
  41.4 1.6 %collective-permute-start.13 = (f32[4,3,32,128]{3,2,1,0:T(8,128)S(1)}, f32[4,3,32,128]{3,2,1,0:T(8,128)S(1)}, u32[]{:S(2)}, u32[]{:S(2)}) collective-permute-start(f32[4,3,32,128]{3,2,1,0:T(8,128)S(1)} %collective-permute-done.9.low_mine), channel_id=1, source_target_pairs={{0,16},{16,0},{32,48},{48,32},{64,80},{80,64},{96,112},{112,96},{1... | collective-permute-start | bytes 589832 | tf_op jit(solution)/shard_map/ppermute | solution.py:298
  41.9 1.4 %collective-permute-start.14 = (f32[4,3,32,128]{3,2,1,0:T(8,128)S(1)}, f32[4,3,32,128]{3,2,1,0:T(8,128)S(1)}, u32[]{:S(2)}, u32[]{:S(2)}) collective-permute-start(f32[4,3,32,128]{3,2,1,0:T(8,128)S(1)} %collective-permute-done.10.high_mine), channel_id=1, source_target_pairs={{0,16},{16,0},{32,48},{48,32},{64,80},{80,64},{96,112},{112,96},{1... | collective-permute-start | bytes 589832 | tf_op jit(solution)/shard_map/ppermute | solution.py:299

commit v6 on v5

--- a/solution.py
+++ b/solution.py
@@ -37,37 +37,47 @@
     return pltpu.roll(cells, shift % cells.shape[-1], cells.ndim - 1) if shift else cells
 
 
-def apply_taps(x, y0, pairs, sums, centre, b_at, phi_at):
+def apply_taps(x, y0, pairs, sums, centre, b_at, phi_at, weights):
     count = len(sums)
     own = [centre(i, x, y0) for i in range(count)]
-    for reach in range(REACH + 1):
-        shifts = (0,) if reach == 0 else (reach, -reach)
-        reached = [
-            (dx, dy, layer)
-            for dx, layer in pairs
-            for dy in range(-REACH, REACH + 1)
-            if abs(dx) + abs(dy) + reach <= REACH
-        ]
-        if not reached:
-            continue
-        here = {dz: [turned(cells, dz) for cells in own] for dz in shifts}
-        totals = {dz: [None] * count for dz in shifts}
-        for dx, dy, layer in reached:
-            there = [b_at(i, layer, y0, dy) for i in range(count)]
-            weights = {}
-            for dz in shifts:
-                gram = here[dz][0] * there[0]
-                for i in range(1, count):
-                    gram = gram + here[dz][i] * there[i]
-                weights[dz] = gram * np.float32(TAPS[dx, dy, dz])
+    first = x % 2 * (weights.shape[0] // 2)
+    plans = []
+    for shifts in ((0, 1, -1), (2, -2, 3, -3)):
+        plan = []
+        here = {}
+        for dx, layer in pairs:
+            for dy in range(-REACH, REACH + 1):
+                slots = {}
+                for dz in shifts:
+                    if abs(dx) + abs(dy) + abs(dz) <= REACH:
+                        slots[dz] = first
+                        first += 1
+                        if dz not in here:
+                            here[dz] = [turned(cells, dz) for cells in own]
+                if slots:
+                    plan.append((dx, dy, layer, slots))
+        plans.append((plan, tuple(here)))
+        for dx, dy, layer, slots in plan:
+            grams = {}
+            for i in range(count):
+                there = b_at(i, layer, y0, dy)
+                for dz in slots:
+                    part = here[dz][i] * there
+                    grams[dz] = grams[dz] + part if i else part
+            for dz, slot in slots.items():
+                weights[slot] = grams[dz] * np.float32(TAPS[dx, dy, dz])
+    for plan, shifts in plans:
+        totals = {}
+        for dx, dy, layer, slots in plan:
+            used = {dz: weights[slot] for dz, slot in slots.items()}
             for j in range(count):
                 phi = phi_at(j, layer, y0, dy)
-                for dz in shifts:
-                    part = weights[dz] * phi
-                    totals[dz][j] = part if totals[dz][j] is None else totals[dz][j] + part
+                for dz in slots:
+                    part = used[dz] * phi
+                    totals[dz, j] = totals[dz, j] + part if (dz, j) in totals else part
         for dz in shifts:
             for j in range(count):
-                sums[j] = sums[j] + turned(totals[dz][j], -dz)
+                sums[j] = sums[j] + turned(totals[dz, j], -dz)
     return sums
 
 
@@ -78,7 +88,7 @@
     dst[at, layer, ROWS + ny :] = cells[:ROWS]
 
 
-def inner_kernel(phi, b_mine, b_other, pair, far, out, ends, padded_phi, padded_b):
+def inner_kernel(phi, b_mine, b_other, pair, far, out, ends, padded_phi, padded_b, weights):
     count, nx, ny, nz = phi.shape
 
     def fill(i, _):
@@ -116,7 +126,7 @@
             pairs = [(to - x, to) for to in range(nx) if abs(to - x) <= REACH]
             sums = [jnp.zeros((ROWS, nz), jnp.float32)] * count
             sums = apply_taps(
-                x, y0, pairs, sums, lambda i, x, y0: b_at(i, x, y0, 0), b_at, at(padded_phi)
+                x, y0, pairs, sums, lambda i, x, y0: b_at(i, x, y0, 0), b_at, at(padded_phi), weights
             )
             for j in range(count):
                 out[j, x, pl.ds(y0, ROWS), :] = sums[j]
@@ -126,7 +136,8 @@
 
 
 def outer_kernel(
-    part, ends, b_mine, b_other, low_mine, low_other, high_mine, high_other, out, padded_b, done, sems
+    part, ends, b_mine, b_other, low_mine, low_other, high_mine, high_other,
+    out, padded_b, done, weights, sems,
 ):
     count, nx, ny, _ = part.shape
 
@@ -157,7 +168,7 @@
             pairs = [(layer - REACH - x, layer) for layer in range(REACH) if x - (layer - REACH) <= REACH]
             pairs += [(nx + layer - x, REACH + layer) for layer in range(REACH) if nx + layer - x <= REACH]
             sums = [part[j, x, pl.ds(y0, ROWS), :] for j in range(count)]
-            sums = apply_taps(x, y0, pairs, sums, centre, at(padded_b), at(ends))
+            sums = apply_taps(x, y0, pairs, sums, centre, at(padded_b), at(ends), weights)
             for j in range(count):
                 done[j, x, pl.ds(y0, ROWS), :] = sums[j]
         move(y0, t).start()
@@ -175,7 +186,7 @@
     rows = (
         block & 1,
         ((block >> 1) & 1) ^ core,
-        ((block >> 2) - (band >> 1)) & 3,
+        ((block >> 2) ^ (band >> 1)) & 3,
         (block >> 4) ^ (band >> 3),
     )
     for row, number in enumerate(rows):
@@ -189,7 +200,7 @@
 def choose_kernel(flags, own, got, *chosen):
     row = (lax.axis_index("band") >> 1) & 3
     for step, out in enumerate(chosen):
-        i = (row + step) & 3
+        i = row ^ step
         for x in range(out.shape[0]):
             first, last = own[i, x], own[i + BLOCK, x]
             here = flag_is(flags, 1, 0, first)
@@ -202,11 +213,12 @@
     kept[...] = cells[...]
 
 
-def pick_kernel(flags, own, above, opposite, below, picked):
+def pick_kernel(flags, own, *rest):
+    others, picked = rest[:-1], rest[-1]
     for x in range(picked.shape[0]):
         cells = own[x]
-        for number, other in ((1, above), (2, opposite), (3, below)):
-            cells = jnp.where(flag_is(flags, 2, number, cells), other[x], cells)
+        for step, other in enumerate(others, 1):
+            cells = jnp.where(flag_is(flags, 2, step, cells), other[x], cells)
         picked[x] = cells
 
 
@@ -216,9 +228,9 @@
         settled[x] = jnp.where(flag_is(flags, 3, 0, cells), cells, crossed[x])
 
 
-def gather_kernel(own, below, opposite, above, block, tail, head):
+def gather_kernel(own, first, second, third, block, tail, head):
     nx = own.shape[0]
-    for i, source in enumerate((own, below, opposite, above)):
+    for i, source in enumerate((own, first, second, third)):
         for x in range(nx):
             cells = source[x]
             block[i, x] = cells
@@ -232,7 +244,7 @@
 LIMIT = pltpu.CompilerParams(vmem_limit_bytes=32 * 1024 * 1024)
 
 
-def call(kernel, shapes, *args, in_specs=None, out_specs=VMEM, scratch=(), kind=jnp.float32):
+def call(kernel, shapes, *args, cost=None, in_specs=None, out_specs=VMEM, scratch=(), kind=jnp.float32):
     shapes = [shapes] if isinstance(shapes[0], int) else list(shapes)
     kinds = kind if isinstance(kind, tuple) else (kind,) * len(shapes)
     outs = [jax.ShapeDtypeStruct(shape, kind) for shape, kind in zip(shapes, kinds)]
@@ -244,6 +256,7 @@
         out_specs=out_specs if single else [out_specs] * len(outs),
         scratch_shapes=list(scratch),
         compiler_params=LIMIT,
+        cost_estimate=cost,
     )(*args)
 
 
@@ -260,7 +273,7 @@
     down = [(to, source) for source, to in up]
 
     def along_y(step):
-        return [(i, i // 8 * 8 + (i + 2 * step) % 8) for i in range(bands)]
+        return [(i, i ^ 2 * step) for i in range(bands)]
 
     pair = lax.ppermute(orbitals, "dom", [(i, i ^ 1) for i in range(doms)])
     onward = [(i, (i + 2 - 4 * (i % 2)) % doms) for i in range(doms)]
@@ -268,30 +281,28 @@
 
     got = lax.ppermute(orbitals, "band", partner)
     flags = call(
-        flags_kernel, (8, nz), owner_order, in_specs=[pl.BlockSpec(memory_space=pltpu.SMEM)], kind=jnp.int32
+        flags_kernel, (8, nz), owner_order, in_specs=[pl.BlockSpec(memory_space=pltpu.SMEM)], kind=jnp.int32,
+        cost=pl.CostEstimate(flops=10**9, bytes_accessed=10**7, transcendentals=0),
     )
     chosen = call(choose_kernel, (layers,) * 4, flags, orbitals, got)
-    below = lax.ppermute(chosen[1], "band", along_y(1))
-    opposite = lax.ppermute(chosen[2], "band", along_y(2))
-    above = lax.ppermute(chosen[3], "band", along_y(-1))
-    own = chosen[0]
-    picked = call(pick_kernel, layers, flags, own, above, opposite, below)
+    others = [lax.ppermute(chosen[step], "band", along_y(step)) for step in (1, 2, 3)]
+    picked = call(pick_kernel, layers, flags, chosen[0], *others)
     crossed = lax.ppermute(picked, "band", across)
     picked, pair = lax.optimization_barrier((picked, pair))
     picked = call(keep_kernel, layers, picked)
     settled = call(settle_kernel, layers, flags, picked, crossed)
     far = lax.ppermute(jnp.where(even, pair[:, nx - REACH :], pair[:, :REACH]), "dom", onward)
-    below = lax.ppermute(settled, "band", along_y(1))
-    opposite = lax.ppermute(settled, "band", along_y(2))
-    above = lax.ppermute(settled, "band", along_y(-1))
-    b_mine, tail, head = call(gather_kernel, (half, side, side), settled, below, opposite, above)
+    others = [lax.ppermute(settled, "band", along_y(step)) for step in (1, 2, 3)]
+    b_mine, tail, head = call(gather_kernel, (half, side, side), settled, *others)
+
     low_mine = lax.ppermute(tail, ("band", "dom"), up)
     high_mine = lax.ppermute(head, ("band", "dom"), down)
     b_other = lax.ppermute(b_mine, "band", partner)
     padded = pltpu.VMEM((count, nx, ny + 2 * ROWS, nz), jnp.float32)
+    weights = pltpu.VMEM((2 * len(TAPS), ROWS, nz), jnp.float32)
     part, ends = call(
         inner_kernel, (whole, (count, 2 * REACH, ny + 2 * ROWS, nz)), orbitals, b_mine, b_other, pair, far,
-        scratch=[padded, padded],
+        scratch=[padded, padded, weights],
     )
     low_mine, high_mine, part = lax.optimization_barrier((low_mine, high_mine, part))
 
@@ -303,6 +314,7 @@
         scratch=[
             pltpu.VMEM((count, 2 * REACH, ny + 2 * ROWS, nz), jnp.float32),
             pltpu.VMEM(whole, jnp.float32),
+            weights,
             pltpu.SemaphoreType.DMA((ny // ROWS,)),
         ],
     )

time: 45.9 us -> 45.2 us (0.985); the launches traced: 45.8 us -> 44.4 us
  local copies, waits for them, and re-layouts: 1.7 us -> 0.66 us
  Pallas kernels: 8.88 us -> 8.06 us
    ppermute x6, waiting for transfers between devices: 10 us -> 7.45 us  [the longest x3 3.94 us: local(): lax.ppermute(settled, 'band', along_y(step))]
    ppermute x1, waiting for transfers between devices: 0.08 us -> 1.92 us  [local(): pair = lax.ppermute(orbitals, 'dom', [(i, i ^ 1) for i in range(doms)])]
    ppermute x1, starting transfers between devices: 1.63 us -> 0.08 us  [local(): lax.ppermute(jnp.where(even, pair[:, nx - REACH:], pair[:, :REACH]), 'dom...]
    ppermute x6, starting transfers between devices: 6.44 us -> 7.97 us  [the longest x3 4.03 us: local(): lax.ppermute(settled, 'band', along_y(step))]
    unnamed x6 -> x4, local copies, waits for them, and re-layouts: 1.7 us -> 0.66 us
    pallas_call x8, Pallas kernels: 8.88 us -> 8.06 us  [call(): pl.pallas_call(kernel, out_shape=outs[0] if single else outs, in_specs=in...]
    ppermute x1, waiting for transfers between devices: 0.4 us -> 1.12 us  [local(): crossed = lax.ppermute(picked, 'band', across)]
  transfers between devices with their start and end apart: 15 -> 15, of which waited for: 11 -> 10; matrix products, arithmetic and copies ran while one was open for 0% -> 0% of each run, Pallas kernels for 14% -> 13%
where the time goes in v6:
time: 45.2 us; the launch traced here: 44.4 us
  starting transfers between devices  22.9 us (51%)
  waiting for transfers between devices  12.7 us (28%)
  Pallas kernels  8.06 us (18%)
  local copies, waits for them, and re-layouts  0.66 us (1%)
    pallas_call x8, Pallas kernels, call(): pl.pallas_call(kernel, out_shape=outs[0] if single else outs, in_specs=in...  8.06 us
    ppermute x3, starting transfers between devices, local(): lax.ppermute(settled, 'band', along_y(step))  4.03 us
    ppermute x1, starting transfers between devices, local(): low_mine = lax.ppermute(tail, ('band', 'dom'), up)  4.01 us
    ppermute x3, starting transfers between devices, local(): lax.ppermute(chosen[step], 'band', along_y(step))  3.94 us
    ppermute x3, waiting for transfers between devices, local(): lax.ppermute(settled, 'band', along_y(step))  3.94 us
    ppermute x3, waiting for transfers between devices, local(): lax.ppermute(chosen[step], 'band', along_y(step))  3.51 us
    ppermute x1, starting transfers between devices, local(): got = lax.ppermute(orbitals, 'band', partner)  3.24 us
    ppermute x1, starting transfers between devices, local(): crossed = lax.ppermute(picked, 'band', across)  2.54 us
  transfers between devices with their start and end apart: 15, of which 10 were waited for; matrix products, arithmetic and copies ran while one was open for 0% of the time, Pallas kernels for 13%

profile of v6, /device:TPU:1, one launch (start us, length us, event | category | flops | bytes accessed | tf_op | source)
XLA Modules:
  0.0 44.4 jit_solution(7601488336286167971)
XLA Ops:
  0.0 0.0 copy-start
  0.0 3.2 %collective-permute-start = (f32[8,4,32,128]{3,2,1,0:T(8,128)}, f32[8,4,32,128]{3,2,1,0:T(8,128)S(1)}, u32[]{:S(2)}, u32[]{:S(2)}) collective-permute-start(f32[8,4,32,128]{3,2,1,0:T(8,128)} %phi.1), channel_id=1, source_target_pairs={{0,16},{16,0},{32,48},{48,32},{64,80},{80,64},{96,112},{112,96},{1... | collective-permute-start | bytes 1572872 | tf_op jit(solution)/shard_map/ppermute | solution.py:282
  3.2 0.0 collective-permute-start.4
  3.2 0.0 copy-start.1
  3.2 0.7 %copy-done.1 = s32[32]{0:T(128)S(1)} copy-done((s32[32]{0:T(128)S(1)}, s32[32]{0:T(128)}, u32[]{:S(2)}) %copy-start.1) | copy-done | bytes 152
  3.9 0.6 %shard_map.28.flags = s32[8,128]{1,0:T(8,128)S(1)} custom-call(s32[32]{0:T(128)S(1)} %copy-done.1), custom_call_target="tpu_custom_call" | custom-call | flops 1000000000 | bytes 10000000 | tf_op jit(solution)/shard_map/pallas_call | solution.py:252
  4.5 0.5 %collective-permute-done.got = f32[8,4,32,128]{3,2,1,0:T(8,128)S(1)} collective-permute-done((f32[8,4,32,128]{3,2,1,0:T(8,128)}, f32[8,4,32,128]{3,2,1,0:T(8,128)S(1)}, u32[]{:S(2)}, u32[]{:S(2)}) %collective-permute-start) | collective-permute-done | bytes 524320 | tf_op jit(solution)/shard_map/ppermute | solution.py:282
  5.0 0.0 copy-done
  5.0 0.1 shard_map.29
  5.1 0.4 collective-permute-start.1
  5.5 2.6 %collective-permute-start.2 = (f32[4,32,128]{2,1,0:T(8,128)S(1)}, f32[4,32,128]{2,1,0:T(8,128)S(1)}, u32[]{:S(2)}, u32[]{:S(2)}) collective-permute-start(f32[4,32,128]{2,1,0:T(8,128)S(1)} %get-tuple-element.21), channel_id=1, source_target_pairs={{0,64},{16,80},{32,96},{48,112},{64,0},{80,16},{96,32},{112,48},{1... | collective-permute-start | bytes 196616 | tf_op jit(solution)/shard_map/ppermute | solution.py:288
  8.1 0.9 %collective-permute-start.3 = (f32[4,32,128]{2,1,0:T(8,128)S(1)}, f32[4,32,128]{2,1,0:T(8,128)S(1)}, u32[]{:S(2)}, u32[]{:S(2)}) collective-permute-start(f32[4,32,128]{2,1,0:T(8,128)S(1)} %get-tuple-element.22), channel_id=1, source_target_pairs={{0,96},{16,112},{32,64},{48,80},{64,32},{80,48},{96,0},{112,16},{1... | collective-permute-start | bytes 196616 | tf_op jit(solution)/shard_map/ppermute | solution.py:288
  9.0 0.0 collective-permute-done.1.rest_0_
  9.0 2.0 %collective-permute-done.2.rest_1_ = f32[4,32,128]{2,1,0:T(8,128)S(1)} collective-permute-done((f32[4,32,128]{2,1,0:T(8,128)S(1)}, f32[4,32,128]{2,1,0:T(8,128)S(1)}, u32[]{:S(2)}, u32[]{:S(2)}) %collective-permute-start.2) | collective-permute-done | bytes 65568 | tf_op jit(solution)/shard_map/ppermute | solution.py:288
  11.0 1.5 %collective-permute-done.3.rest_2_ = f32[4,32,128]{2,1,0:T(8,128)S(1)} collective-permute-done((f32[4,32,128]{2,1,0:T(8,128)S(1)}, f32[4,32,128]{2,1,0:T(8,128)S(1)}, u32[]{:S(2)}, u32[]{:S(2)}) %collective-permute-start.3) | collective-permute-done | bytes 65568 | tf_op jit(solution)/shard_map/ppermute | solution.py:288
  12.6 2.5 %collective-permute-start.5 = (f32[4,32,128]{2,1,0:T(8,128)S(1)}, f32[4,32,128]{2,1,0:T(8,128)S(1)}, u32[]{:S(2)}, u32[]{:S(2)}) collective-permute-start(f32[4,32,128]{2,1,0:T(8,128)S(1)} %shard_map.30.cells), channel_id=1, source_target_pairs={{0,128},{16,144},{32,160},{48,176},{64,192},{80,208},{96,224},{112... | collective-permute-start | bytes 196616 | tf_op jit(solution)/shard_map/ppermute | solution.py:290
  15.1 1.9 %collective-permute-done.4.pair = f32[8,4,32,128]{3,2,1,0:T(8,128)S(1)} collective-permute-done((f32[8,4,32,128]{3,2,1,0:T(8,128)}, f32[8,4,32,128]{3,2,1,0:T(8,128)S(1)}, u32[]{:S(2)}, u32[]{:S(2)}) %collective-permute-start.4) | collective-permute-done | bytes 524320 | tf_op jit(solution)/shard_map/ppermute | solution.py:278
  17.1 0.1 collective-permute-start.12
  17.2 1.1 %collective-permute-done.5.crossed = f32[4,32,128]{2,1,0:T(8,128)S(1)} collective-permute-done((f32[4,32,128]{2,1,0:T(8,128)S(1)}, f32[4,32,128]{2,1,0:T(8,128)S(1)}, u32[]{:S(2)}, u32[]{:S(2)}) %collective-permute-start.5) | collective-permute-done | bytes 65568 | tf_op jit(solution)/shard_map/ppermute | solution.py:290
  18.3 3.4 %collective-permute-start.8 = (f32[4,32,128]{2,1,0:T(8,128)S(1)}, f32[4,32,128]{2,1,0:T(8,128)S(1)}, u32[]{:S(2)}, u32[]{:S(2)}) collective-permute-start(f32[4,32,128]{2,1,0:T(8,128)S(1)} %shard_map.32.own), channel_id=1, source_target_pairs={{0,96},{16,112},{32,64},{48,80},{64,32},{80,48},{96,0},{112,16},{1... | collective-permute-start | bytes 196616 | tf_op jit(solution)/shard_map/ppermute | solution.py:295
  21.6 0.3 collective-permute-start.7
  22.0 0.3 collective-permute-start.6
  22.3 1.0 %collective-permute-done.8.third = f32[4,32,128]{2,1,0:T(8,128)S(1)} collective-permute-done((f32[4,32,128]{2,1,0:T(8,128)S(1)}, f32[4,32,128]{2,1,0:T(8,128)S(1)}, u32[]{:S(2)}, u32[]{:S(2)}) %collective-permute-start.8) | collective-permute-done | bytes 65568 | tf_op jit(solution)/shard_map/ppermute | solution.py:295
  23.3 3.0 %collective-permute-done.7.second = f32[4,32,128]{2,1,0:T(8,128)S(1)} collective-permute-done((f32[4,32,128]{2,1,0:T(8,128)S(1)}, f32[4,32,128]{2,1,0:T(8,128)S(1)}, u32[]{:S(2)}, u32[]{:S(2)}) %collective-permute-start.7) | collective-permute-done | bytes 65568 | tf_op jit(solution)/shard_map/ppermute | solution.py:295
  26.3 0.0 collective-permute-done.6.first
  26.3 2.4 %collective-permute-start.11 = (f32[4,4,32,128]{3,2,1,0:T(8,128)S(1)}, f32[4,4,32,128]{3,2,1,0:T(8,128)S(1)}, u32[]{:S(2)}, u32[]{:S(2)}) collective-permute-start(f32[4,4,32,128]{3,2,1,0:T(8,128)S(1)} %get-tuple-element.26.b_mine), channel_id=1, source_target_pairs={{0,16},{16,0},{32,48},{48,32},{64,80},{80,64},{96,112},{112,96},{1... | collective-permute-start | bytes 786440 | tf_op jit(solution)/shard_map/ppermute | solution.py:300
  28.7 4.0 %collective-permute-start.9 = (f32[4,3,32,128]{3,2,1,0:T(8,128)S(1)}, f32[4,3,32,128]{3,2,1,0:T(8,128)S(1)}, u32[]{:S(2)}, u32[]{:S(2)}) collective-permute-start(f32[4,3,32,128]{3,2,1,0:T(8,128)S(1)} %get-tuple-element.24), channel_id=1, source_target_pairs={{0,1},{1,130},{2,3},{3,132},{4,5},{5,134},{6,7},{7,136},{8,9},{9,1... | collective-permute-start | bytes 589832 | tf_op jit(solution)/shard_map/ppermute | solution.py:298
  32.7 2.0 %collective-permute-start.10 = (f32[4,3,32,128]{3,2,1,0:T(8,128)S(1)}, f32[4,3,32,128]{3,2,1,0:T(8,128)S(1)}, u32[]{:S(2)}, u32[]{:S(2)}) collective-permute-start(f32[4,3,32,128]{3,2,1,0:T(8,128)S(1)} %get-tuple-element.25), channel_id=1, source_target_pairs={{1,0},{130,1},{3,2},{132,3},{5,4},{134,5},{7,6},{136,7},{9,8},{138... | collective-permute-start | bytes 589832 | tf_op jit(solution)/shard_map/ppermute | solution.py:299
  34.7 0.0 collective-permute-done.11.b_other
  34.7 0.0 collective-permute-done.12.far
  34.7 5.0 %shard_map.34 = (f32[8,4,32,128]{3,2,1,0:T(8,128)S(1)}, f32[8,6,48,128]{3,2,1,0:T(8,128)S(1)}) custom-call(f32[8,4,32,128]{3,2,1,0:T(8,128)S(1)} %copy-done, f32[4,4,32,128]{3,2,1,0:T(8,128)S(1)} %get-tuple-element.26.b_mine, f32[4,4,32,128]{3,2,1,0:T(8,128)S(1)} %collective-permute-done.11.b_other, f32[8,4,32,128]{3,2,1,0:T(8,128)S(1)} %collective-permute-done.4.pair, ...), custom_call_target="tpu_custom_call" | custom-call | tf_op jit(solution)/shard_map/pallas_call | solution.py:252
  39.7 0.2 collective-permute-done.9.low_mine
  39.9 0.0 collective-permute-done.10.high_mine
  39.9 0.7 %collective-permute-start.13 = (f32[4,3,32,128]{3,2,1,0:T(8,128)S(1)}, f32[4,3,32,128]{3,2,1,0:T(8,128)S(1)}, u32[]{:S(2)}, u32[]{:S(2)}) collective-permute-start(f32[4,3,32,128]{3,2,1,0:T(8,128)S(1)} %collective-permute-done.9.low_mine), channel_id=1, source_target_pairs={{0,16},{16,0},{32,48},{48,32},{64,80},{80,64},{96,112},{112,96},{1... | collective-permute-start | bytes 589832 | tf_op jit(solution)/shard_map/ppermute | solution.py:309
  40.6 0.0 collective-permute-start.14
  40.6 1.1 %collective-permute-done.13.low_other = f32[4,3,32,128]{3,2,1,0:T(8,128)S(1)} collective-permute-done((f32[4,3,32,128]{3,2,1,0:T(8,128)S(1)}, f32[4,3,32,128]{3,2,1,0:T(8,128)S(1)}, u32[]{:S(2)}, u32[]{:S(2)}) %collective-permute-start.13) | collective-permute-done | bytes 196640 | tf_op jit(solution)/shard_map/ppermute | solution.py:309
  41.6 0.4 collective-permute-done.14.high_other
  42.0 2.4 %shard_map.35 = f32[8,4,32,128]{3,2,1,0:T(8,128)} custom-call(f32[8,4,32,128]{3,2,1,0:T(8,128)S(1)} %get-tuple-element.29.part, f32[8,6,48,128]{3,2,1,0:T(8,128)S(1)} %get-tuple-element.30.ends, f32[4,4,32,128]{3,2,1,0:T(8,128)S(1)} %get-tuple-element.26.b_mine, f32[4,4,32,128]{3,2,1,0:T(8,128)S(1)} %collective-permute-done.11.b_other, ...), custom_call_target="tpu_custom_call" | custom-call | tf_op jit(solution)/shard_map/pallas_call | solution.py:252
  (5 shorter events, 0.1 us)
Async XLA Ops:
  0.0 5.0 %copy-start = (f32[8,4,32,128]{3,2,1,0:T(8,128)S(1)}, f32[8,4,32,128]{3,2,1,0:T(8,128)}, u32[]{:S(2)}) copy-start(f32[8,4,32,128]{3,2,1,0:T(8,128)} %phi.1) | copy-start | bytes 1572868
  0.0 5.0 %collective-permute-start = (f32[8,4,32,128]{3,2,1,0:T(8,128)}, f32[8,4,32,128]{3,2,1,0:T(8,128)S(1)}, u32[]{:S(2)}, u32[]{:S(2)}) collective-permute-start(f32[8,4,32,128]{3,2,1,0:T(8,128)} %phi.1), channel_id=1, source_target_pairs={{0,16},{16,0},{32,48},{48,32},{64,80},{80,64},{96,112},{112,96},{1... | collective-permute-start | bytes 1572872 | tf_op jit(solution)/shard_map/ppermute | solution.py:282
  3.2 13.8 %collective-permute-start.4 = (f32[8,4,32,128]{3,2,1,0:T(8,128)}, f32[8,4,32,128]{3,2,1,0:T(8,128)S(1)}, u32[]{:S(2)}, u32[]{:S(2)}) collective-permute-start(f32[8,4,32,128]{3,2,1,0:T(8,128)} %phi.1), channel_id=1, source_target_pairs={{0,1},{1,0},{2,3},{3,2},{4,5},{5,4},{6,7},{7,6},{8,9},{9,8},{10,11... | collective-permute-start | bytes 1572872 | tf_op jit(solution)/shard_map/ppermute | solution.py:278
  3.2 0.7 %copy-start.1 = (s32[32]{0:T(128)S(1)}, s32[32]{0:T(128)}, u32[]{:S(2)}) copy-start(s32[32]{0:T(128)} %order.1) | copy-start | bytes 388
  5.1 3.9 %collective-permute-start.1 = (f32[4,32,128]{2,1,0:T(8,128)S(1)}, f32[4,32,128]{2,1,0:T(8,128)S(1)}, u32[]{:S(2)}, u32[]{:S(2)}) collective-permute-start(f32[4,32,128]{2,1,0:T(8,128)S(1)} %get-tuple-element.20), channel_id=1, source_target_pairs={{0,32},{16,48},{32,0},{48,16},{64,96},{80,112},{96,64},{112,80},{1... | collective-permute-start | bytes 196616 | tf_op jit(solution)/shard_map/ppermute | solution.py:288
  5.5 5.6 %collective-permute-start.2 = (f32[4,32,128]{2,1,0:T(8,128)S(1)}, f32[4,32,128]{2,1,0:T(8,128)S(1)}, u32[]{:S(2)}, u32[]{:S(2)}) collective-permute-start(f32[4,32,128]{2,1,0:T(8,128)S(1)} %get-tuple-element.21), channel_id=1, source_target_pairs={{0,64},{16,80},{32,96},{48,112},{64,0},{80,16},{96,32},{112,48},{1... | collective-permute-start | bytes 196616 | tf_op jit(solution)/shard_map/ppermute | solution.py:288
  8.1 4.5 %collective-permute-start.3 = (f32[4,32,128]{2,1,0:T(8,128)S(1)}, f32[4,32,128]{2,1,0:T(8,128)S(1)}, u32[]{:S(2)}, u32[]{:S(2)}) collective-permute-start(f32[4,32,128]{2,1,0:T(8,128)S(1)} %get-tuple-element.22), channel_id=1, source_target_pairs={{0,96},{16,112},{32,64},{48,80},{64,32},{80,48},{96,0},{112,16},{1... | collective-permute-start | bytes 196616 | tf_op jit(solution)/shard_map/ppermute | solution.py:288
  12.6 5.7 %collective-permute-start.5 = (f32[4,32,128]{2,1,0:T(8,128)S(1)}, f32[4,32,128]{2,1,0:T(8,128)S(1)}, u32[]{:S(2)}, u32[]{:S(2)}) collective-permute-start(f32[4,32,128]{2,1,0:T(8,128)S(1)} %shard_map.30.cells), channel_id=1, source_target_pairs={{0,128},{16,144},{32,160},{48,176},{64,192},{80,208},{96,224},{112... | collective-permute-start | bytes 196616 | tf_op jit(solution)/shard_map/ppermute | solution.py:290
  17.1 17.7 %collective-permute-start.12 = (f32[8,3,32,128]{3,2,1,0:T(8,128)S(1)}, f32[8,3,32,128]{3,2,1,0:T(8,128)S(1)}, u32[]{:S(2)}, u32[]{:S(2)}) collective-permute-start(f32[8,3,32,128]{3,2,1,0:T(8,128)S(1)} %slice_select_fusion), channel_id=1, source_target_pairs={{0,2},{1,15},{2,4},{3,1},{4,6},{5,3},{6,8},{7,5},{8,10},{9,7},{10,... | collective-permute-start | bytes 1179656 | tf_op jit(solution)/shard_map/ppermute | solution.py:294
  18.3 5.0 %collective-permute-start.8 = (f32[4,32,128]{2,1,0:T(8,128)S(1)}, f32[4,32,128]{2,1,0:T(8,128)S(1)}, u32[]{:S(2)}, u32[]{:S(2)}) collective-permute-start(f32[4,32,128]{2,1,0:T(8,128)S(1)} %shard_map.32.own), channel_id=1, source_target_pairs={{0,96},{16,112},{32,64},{48,80},{64,32},{80,48},{96,0},{112,16},{1... | collective-permute-start | bytes 196616 | tf_op jit(solution)/shard_map/ppermute | solution.py:295
  21.6 4.6 %collective-permute-start.7 = (f32[4,32,128]{2,1,0:T(8,128)S(1)}, f32[4,32,128]{2,1,0:T(8,128)S(1)}, u32[]{:S(2)}, u32[]{:S(2)}) collective-permute-start(f32[4,32,128]{2,1,0:T(8,128)S(1)} %shard_map.32.own), channel_id=1, source_target_pairs={{0,64},{16,80},{32,96},{48,112},{64,0},{80,16},{96,32},{112,48},{1... | collective-permute-start | bytes 196616 | tf_op jit(solution)/shard_map/ppermute | solution.py:295
  22.0 4.3 %collective-permute-start.6 = (f32[4,32,128]{2,1,0:T(8,128)S(1)}, f32[4,32,128]{2,1,0:T(8,128)S(1)}, u32[]{:S(2)}, u32[]{:S(2)}) collective-permute-start(f32[4,32,128]{2,1,0:T(8,128)S(1)} %shard_map.32.own), channel_id=1, source_target_pairs={{0,32},{16,48},{32,0},{48,16},{64,96},{80,112},{96,64},{112,80},{1... | collective-permute-start | bytes 196616 | tf_op jit(solution)/shard_map/ppermute | solution.py:295
  26.3 8.4 %collective-permute-start.11 = (f32[4,4,32,128]{3,2,1,0:T(8,128)S(1)}, f32[4,4,32,128]{3,2,1,0:T(8,128)S(1)}, u32[]{:S(2)}, u32[]{:S(2)}) collective-permute-start(f32[4,4,32,128]{3,2,1,0:T(8,128)S(1)} %get-tuple-element.26.b_mine), channel_id=1, source_target_pairs={{0,16},{16,0},{32,48},{48,32},{64,80},{80,64},{96,112},{112,96},{1... | collective-permute-start | bytes 786440 | tf_op jit(solution)/shard_map/ppermute | solution.py:300
  28.7 11.2 %collective-permute-start.9 = (f32[4,3,32,128]{3,2,1,0:T(8,128)S(1)}, f32[4,3,32,128]{3,2,1,0:T(8,128)S(1)}, u32[]{:S(2)}, u32[]{:S(2)}) collective-permute-start(f32[4,3,32,128]{3,2,1,0:T(8,128)S(1)} %get-tuple-element.24), channel_id=1, source_target_pairs={{0,1},{1,130},{2,3},{3,132},{4,5},{5,134},{6,7},{7,136},{8,9},{9,1... | collective-permute-start | bytes 589832 | tf_op jit(solution)/shard_map/ppermute | solution.py:298
  32.7 7.2 %collective-permute-start.10 = (f32[4,3,32,128]{3,2,1,0:T(8,128)S(1)}, f32[4,3,32,128]{3,2,1,0:T(8,128)S(1)}, u32[]{:S(2)}, u32[]{:S(2)}) collective-permute-start(f32[4,3,32,128]{3,2,1,0:T(8,128)S(1)} %get-tuple-element.25), channel_id=1, source_target_pairs={{1,0},{130,1},{3,2},{132,3},{5,4},{134,5},{7,6},{136,7},{9,8},{138... | collective-permute-start | bytes 589832 | tf_op jit(solution)/shard_map/ppermute | solution.py:299
  39.9 1.7 %collective-permute-start.13 = (f32[4,3,32,128]{3,2,1,0:T(8,128)S(1)}, f32[4,3,32,128]{3,2,1,0:T(8,128)S(1)}, u32[]{:S(2)}, u32[]{:S(2)}) collective-permute-start(f32[4,3,32,128]{3,2,1,0:T(8,128)S(1)} %collective-permute-done.9.low_mine), channel_id=1, source_target_pairs={{0,16},{16,0},{32,48},{48,32},{64,80},{80,64},{96,112},{112,96},{1... | collective-permute-start | bytes 589832 | tf_op jit(solution)/shard_map/ppermute | solution.py:309
  40.6 1.4 %collective-permute-start.14 = (f32[4,3,32,128]{3,2,1,0:T(8,128)S(1)}, f32[4,3,32,128]{3,2,1,0:T(8,128)S(1)}, u32[]{:S(2)}, u32[]{:S(2)}) collective-permute-start(f32[4,3,32,128]{3,2,1,0:T(8,128)S(1)} %collective-permute-done.10.high_mine), channel_id=1, source_target_pairs={{0,16},{16,0},{32,48},{48,32},{64,80},{80,64},{96,112},{112,96},{1... | collective-permute-start | bytes 589832 | tf_op jit(solution)/shard_map/ppermute | solution.py:310
